TPU v7x, 32 devices: a whole 2x2x4 slice. The times are simulated.
32 devices in a mesh: section: 4 (over x, core), dp: 2 (over y), tensor: 4 (over z).
Axes of the slice: x: 2, y: 2, z: 4, core: 2. Of those that a mesh axis runs over, the one named last changes fastest.
Arguments:
- saved: bfloat16 [4, 1024, 5120], P('section', ('dp', 'tensor')), may hold values from -0.1875 to 0.1875
- weight: bfloat16 [4, 5120, 5120], P('section', None, 'tensor'), may hold values from -0.078125 to 0.078125
- out_grad: bfloat16 [1024, 5120], P(('dp', 'tensor')), may hold values from -6 to 6
Outputs:
- input_grads: bfloat16 [4, 1024, 5120], P('section', ('dp', 'tensor'))
- weight_grads: float32 [4, 5120, 5120], P('section', 'dp', 'tensor')
All inputs are finite; a program needn't handle non-finite values.
Results may differ from a plain program's by a relative error of at most 0.02.
Values may be sent and summed in bfloat16 or wider, within the bound.
No kernel may reach another device: no remote copies, remote signals or barrier semaphores. Data moves between devices by JAX's collectives and lax.ppermute only.
A program may use at most 192 MiB of HBM per device.

v0:
```python
import jax
import jax.numpy as jnp
from jax import lax
from jax.sharding import PartitionSpec as P


def from_behind(block, axis, distance):
    devices = range(lax.axis_size(axis))
    route = [(i - distance, i) for i in devices if i - distance in devices]
    return lax.ppermute(block, axis, route)


def on_device(saved, weight, out_grad):
    activations = saved[0]
    weight_cols = weight[0]
    sections = lax.axis_size("section")
    section_index = lax.axis_index("section")
    gradient = out_grad
    own_input = jnp.zeros(out_grad.shape, jnp.bfloat16)
    kept_columns = jnp.zeros(
        (out_grad.shape[0] * lax.axis_size("tensor"), weight_cols.shape[1]), jnp.bfloat16
    )
    for rounds in range(sections):
        active = sections - 1 - rounds
        on_duty = section_index == active
        columns = lax.all_to_all(gradient, "tensor", split_axis=1, concat_axis=0, tiled=True)

        def compute(operand):
            return lax.dot_general(
                operand, weight_cols, (((1,), (1,)), ((), ())), preferred_element_type=jnp.float32
            )

        def nothing(operand):
            return jnp.zeros((operand.shape[0], weight_cols.shape[0]), jnp.float32)

        returned = lax.psum_scatter(
            lax.cond(on_duty, compute, nothing, columns).astype(jnp.bfloat16),
            "tensor",
            scatter_dimension=0,
            tiled=True,
        ).astype(jnp.float32)
        updated = (gradient.astype(jnp.float32) + returned).astype(jnp.bfloat16)
        own_input = jnp.where(on_duty, updated, own_input)
        kept_columns = jnp.where(on_duty, columns, kept_columns)
        if rounds + 1 < sections:
            gradient = from_behind(updated, "section", -1)
    gathered = lax.all_gather(activations, "tensor", axis=0, tiled=True)
    weight_grad = lax.psum_scatter(
        lax.dot_general(
            gathered, kept_columns, (((0,), (0,)), ((), ())), preferred_element_type=jnp.float32
        ).astype(jnp.bfloat16),
        "dp",
        scatter_dimension=0,
        tiled=True,
    ).astype(jnp.float32)
    return (own_input[None], weight_grad[None])


def solution(mesh):
    placed = (
        P("section", ("dp", "tensor"), None),
        P("section", None, "tensor"),
        P(("dp", "tensor"), None),
    )
    return jax.shard_map(
        on_device,
        mesh=mesh,
        in_specs=placed,
        out_specs=(P("section", ("dp", "tensor"), None), P("section", "dp", "tensor")),
        check_vma=False,
    )
```

profile of v0, /device:TPU:5, one launch (start us, length us, event | category | flops | bytes accessed | tf_op | source)
XLA Modules:
  0.0 907.0 jit_solution(16417356837763410151)
XLA Ops:
  7.2 2.5 copy.44
  9.6 4.6 all-to-all-start
  14.2 30.8 %all-to-all-done = bf16[128,4,1280]{2,0,1:T(8,128)(2,1)S(1)} async-done(((bf16[128,4,1280]{2,0,1:T(8,128)(2,1)}), bf16[128,4,1280]{2,0,1:T(8,128)(2,1)S(1)}, u32[]{:S(2)}, u32[]{:S(2)}) %all-to-all-start) | async-done | bytes 1310752 | tf_op jit(solution)/shard_map/all_to_all | solution.py:26
  45.1 1.1 copy-done.4
  46.1 3.0 conditional.4
  46.1 3.0 broadcast.8
  49.1 7.9 copy.25
  57.1 7.9 copy.34
  65.0 0.0 reduce-scatter.16.cloned.1.call-update
  65.0 1.3 copy-done
  66.3 0.8 copy.23
  67.1 100.4 %reduce-scatter.16.cloned.1.call-done = bf16[128,5120]{1,0:T(8,128)(2,1)} async-done(((bf16[512,5120]{1,0:T(8,128)(2,1)}), bf16[128,5120]{1,0:T(8,128)(2,1)}) %reduce-scatter.16.cloned.1.call-update) | async-done | bytes 1310736
  167.5 1.8 copy.35
  169.3 0.3 add_convert_fusion.3
  169.6 2.5 collective-permute-start
  172.2 16.7 %collective-permute-done = bf16[128,5120]{0,1:T(8,128)(2,1)S(1)} collective-permute-done((bf16[128,5120]{0,1:T(8,128)(2,1)S(1)}, bf16[128,5120]{0,1:T(8,128)(2,1)S(1)}, u32[]{:S(2)}, u32[]{:S(2)}) %collective-permute-start) | collective-permute-done | bytes 1310752 | tf_op jit(solution)/shard_map/ppermute | solution.py:10
  188.9 1.4 copy.26
  190.3 3.9 all-to-all-start.1
  194.2 18.7 %all-to-all-done.1 = bf16[128,4,1280]{2,0,1:T(8,128)(2,1)S(1)} async-done(((bf16[128,4,1280]{2,0,1:T(8,128)(2,1)}), bf16[128,4,1280]{2,0,1:T(8,128)(2,1)S(1)}, u32[]{:S(2)}, u32[]{:S(2)}) %all-to-all-start.1) | async-done | bytes 1310752 | tf_op jit(solution)/shard_map/all_to_all | solution.py:26
  212.9 1.1 copy-done.6
  214.0 3.0 conditional.5
  214.0 3.0 broadcast.9
  217.0 7.9 copy.27
  224.9 7.9 copy.36
  232.8 0.0 reduce-scatter.18.cloned.1.call-update
  232.9 102.3 %reduce-scatter.18.cloned.1.call-done = bf16[128,5120]{1,0:T(8,128)(2,1)} async-done(((bf16[512,5120]{1,0:T(8,128)(2,1)}), bf16[128,5120]{1,0:T(8,128)(2,1)}) %reduce-scatter.18.cloned.1.call-update) | async-done | bytes 1310736
  335.2 1.8 copy.37
  336.9 0.3 add_convert_fusion.2
  337.3 2.5 collective-permute-start.1
  339.8 16.7 %collective-permute-done.1 = bf16[128,5120]{0,1:T(8,128)(2,1)S(1)} collective-permute-done((bf16[128,5120]{0,1:T(8,128)(2,1)S(1)}, bf16[128,5120]{0,1:T(8,128)(2,1)S(1)}, u32[]{:S(2)}, u32[]{:S(2)}) %collective-permute-start.1) | collective-permute-done | bytes 1310752 | tf_op jit(solution)/shard_map/ppermute | solution.py:10
  356.5 1.4 copy.28
  358.0 3.9 all-to-all-start.2
  361.9 18.7 %all-to-all-done.2 = bf16[128,4,1280]{2,0,1:T(8,128)(2,1)S(1)} async-done(((bf16[128,4,1280]{2,0,1:T(8,128)(2,1)}), bf16[128,4,1280]{2,0,1:T(8,128)(2,1)S(1)}, u32[]{:S(2)}, u32[]{:S(2)}) %all-to-all-start.2) | async-done | bytes 1310752 | tf_op jit(solution)/shard_map/all_to_all | solution.py:26
  380.6 1.1 copy-done.7
  381.6 13.4 %conditional.6 = (bf16[512,5120]{1,0:T(8,128)(2,1)}) conditional(s32[]{:T(128)} %convert_element_type.78, () %tuple.36, (bf16[512,1280]{1,0:T(8,128)(2,1)S(1)}, bf16[5120,1280]{1,0:T(8,128)(2,1)}) %tuple.71), branch_computations={%region_6.7_spmd, %region_7.8_spmd} | conditional | flops 6710886400 | bytes 19660808 | solution.py:37
  381.6 13.4 %fusion.16 = bf16[512,5120]{1,0:T(8,128)(2,1)} fusion(bf16[512,1280]{1,0:T(8,128)(2,1)S(1)} %get-tuple-element.32, bf16[5120,1280]{1,0:T(8,128)(2,1)} %get-tuple-element.33), kind=kOutput, calls=%fused_computation.23 | convolution fusion | flops 6710886400 | bytes 19660800 | tf_op jit(solution)/shard_map/cond/branch_1_fun/dot_general | solution.py:29
  395.0 7.9 copy.29
  403.0 7.9 copy.38
  410.9 0.0 reduce-scatter.20.cloned.1.call-update
  410.9 0.0 all-gather.3.cloned.1.call-start
  410.9 0.5 all-gather.3.cloned.1.call-update
  411.5 91.0 %reduce-scatter.20.cloned.1.call-done = bf16[128,5120]{1,0:T(8,128)(2,1)} async-done(((bf16[512,5120]{1,0:T(8,128)(2,1)}), bf16[128,5120]{1,0:T(8,128)(2,1)}) %reduce-scatter.20.cloned.1.call-update) | async-done | bytes 1310736
  502.5 1.8 copy.39
  504.2 0.3 add_convert_fusion.1
  504.6 2.5 collective-permute-start.2
  507.1 16.8 %collective-permute-done.2 = bf16[128,5120]{0,1:T(8,128)(2,1)S(1)} collective-permute-done((bf16[128,5120]{0,1:T(8,128)(2,1)S(1)}, bf16[128,5120]{0,1:T(8,128)(2,1)S(1)}, u32[]{:S(2)}, u32[]{:S(2)}) %collective-permute-start.2) | collective-permute-done | bytes 1310752 | tf_op jit(solution)/shard_map/ppermute | solution.py:10
  523.9 1.4 copy.30
  525.4 3.9 all-to-all-start.3
  529.3 58.5 %all-to-all-done.3 = bf16[128,4,1280]{2,0,1:T(8,128)(2,1)S(1)} async-done(((bf16[128,4,1280]{2,0,1:T(8,128)(2,1)}), bf16[128,4,1280]{2,0,1:T(8,128)(2,1)S(1)}, u32[]{:S(2)}, u32[]{:S(2)}) %all-to-all-start.3) | async-done | bytes 1310752 | tf_op jit(solution)/shard_map/all_to_all | solution.py:26
  587.8 1.1 copy-done.8
  588.9 3.0 conditional.7
  588.9 3.0 broadcast.11
  591.9 7.9 copy.31
  599.8 7.9 copy.40
  607.7 0.3 reduce-scatter.14.cloned.1.call-start
  608.0 22.4 %all-gather.3.cloned.1.call-done = bf16[1,512,5120]{2,1,0:T(8,128)(2,1)} async-done(((bf16[1,128,5120]{2,1,0:T(8,128)(2,1)}), bf16[1,512,5120]{2,1,0:T(8,128)(2,1)}) %all-gather.3.cloned.1.call-update) | async-done | bytes 5242896 | tf_op jit(solution)/shard_map/all_gather | solution.py:47
  630.4 12.3 %fusion = bf16[5120,1280]{0,1:T(8,128)(2,1)} fusion(bf16[1,512,5120]{2,1,0:T(8,128)(2,1)} %all-gather.3.cloned.1.call-done, bf16[512,1280]{1,0:T(8,128)(2,1)} %bitcast.53, bf16[512,1280]{1,0:T(8,128)(2,1)} %bitcast.51, bf16[512,1280]{1,0:T(8,128)(2,1)} %bitcast.49, bf16[512,1280]{1,0:T(8,128)(2,1)S(1)} %bitcast.47, pred[]{:T(512)S(6)} %eq.13, pred[]{:T(512)S(6)} %eq.14, ...), kind=kOutput, calls=%fused_computation.1 | convolution fusion | flops 6720061440 | bytes 23592964 | tf_op jit(solution)/shard_map/dot_general | solution.py:49
  642.8 81.8 %reduce-scatter.22.cloned.1.call-done = bf16[128,5120]{1,0:T(8,128)(2,1)} async-done(((bf16[512,5120]{1,0:T(8,128)(2,1)}), bf16[128,5120]{1,0:T(8,128)(2,1)}) %reduce-scatter.22.cloned.1.call-update) | async-done | bytes 1310736
  724.5 1.8 copy.41
  726.3 2.9 fusion.3
  729.2 2.4 copy.32
  731.6 145.3 %reduce-scatter.14.cloned.1.call-done = bf16[2560,1280]{0,1:T(8,128)(2,1)} async-done(((bf16[5120,1280]{0,1:T(8,128)(2,1)}), bf16[2560,1280]{0,1:T(8,128)(2,1)}) %reduce-scatter.14.cloned.1.call-update) | async-done | bytes 6553616 | tf_op jit(solution)/shard_map/reduce_scatter | solution.py:48
  876.9 9.4 %bitcast_convert_fusion = f32[1,2560,1280]{1,2,0:T(8,128)} fusion(bf16[2560,1280]{0,1:T(8,128)(2,1)} %reduce-scatter.14.cloned.1.call-done), kind=kLoop, calls=%fused_computation.2 | loop fusion | flops 3276800 | bytes 19660800 | tf_op jit(solution)/shard_map/broadcast_in_dim | solution.py:56
  886.3 13.9 %copy.33 = f32[1,2560,1280]{2,1,0:T(8,128)} copy(f32[1,2560,1280]{1,2,0:T(8,128)} %bitcast_convert_fusion) | data formatting | bytes 26214400
  (19 shorter events, 0.1 us)
Async XLA Ops:
  9.6 35.4 %all-to-all-start = ((bf16[128,4,1280]{2,0,1:T(8,128)(2,1)}), bf16[128,4,1280]{2,0,1:T(8,128)(2,1)S(1)}, u32[]{:S(2)}, u32[]{:S(2)}) async-start(bf16[128,4,1280]{2,0,1:T(8,128)(2,1)} %bitcast.41), calls=%async_computation | async-start | bytes 2621440 | tf_op jit(solution)/shard_map/all_to_all | solution.py:26
  14.2 153.3 %reduce-scatter.16.cloned.1.call-start = ((), (), s32[]{:S(2)}) async-start(), calls=%async_computation.11 | async-start | bytes 6553600
  45.1 1.1 copy-start.4
  65.0 1.3 copy-start
  169.6 19.2 %copy-start.1 = (bf16[128,5120]{0,1:T(8,128)(2,1)}, bf16[128,5120]{0,1:T(8,128)(2,1)S(1)}, u32[]{:S(2)}) copy-start(bf16[128,5120]{0,1:T(8,128)(2,1)S(1)} %add_convert_fusion.3) | copy-start | bytes 3932164
  169.6 19.2 %collective-permute-start = (bf16[128,5120]{0,1:T(8,128)(2,1)S(1)}, bf16[128,5120]{0,1:T(8,128)(2,1)S(1)}, u32[]{:S(2)}, u32[]{:S(2)}) collective-permute-start(bf16[128,5120]{0,1:T(8,128)(2,1)S(1)} %add_convert_fusion.3), channel_id=1, source_target_pairs={{8,0},{16,8},{24,16},{9,1},{17,9},{25,17},{10,2},{18,10},{26,18},{... | collective-permute-start | bytes 3932168 | tf_op jit(solution)/shard_map/ppermute | solution.py:10
  190.3 22.6 %all-to-all-start.1 = ((bf16[128,4,1280]{2,0,1:T(8,128)(2,1)}), bf16[128,4,1280]{2,0,1:T(8,128)(2,1)S(1)}, u32[]{:S(2)}, u32[]{:S(2)}) async-start(bf16[128,4,1280]{2,0,1:T(8,128)(2,1)} %copy.26), calls=%async_computation.1 | async-start | bytes 2621440 | tf_op jit(solution)/shard_map/all_to_all | solution.py:26
  194.2 141.0 %reduce-scatter.18.cloned.1.call-start = ((), (), s32[]{:S(2)}) async-start(), calls=%async_computation.12 | async-start | bytes 6553600
  212.9 1.1 copy-start.6
  337.3 19.2 %copy-start.2 = (bf16[128,5120]{0,1:T(8,128)(2,1)}, bf16[128,5120]{0,1:T(8,128)(2,1)S(1)}, u32[]{:S(2)}) copy-start(bf16[128,5120]{0,1:T(8,128)(2,1)S(1)} %add_convert_fusion.2) | copy-start | bytes 3932164
  337.3 19.2 %collective-permute-start.1 = (bf16[128,5120]{0,1:T(8,128)(2,1)S(1)}, bf16[128,5120]{0,1:T(8,128)(2,1)S(1)}, u32[]{:S(2)}, u32[]{:S(2)}) collective-permute-start(bf16[128,5120]{0,1:T(8,128)(2,1)S(1)} %add_convert_fusion.2), channel_id=1, source_target_pairs={{8,0},{16,8},{24,16},{9,1},{17,9},{25,17},{10,2},{18,10},{26,18},{... | collective-permute-start | bytes 3932168 | tf_op jit(solution)/shard_map/ppermute | solution.py:10
  358.0 22.6 %all-to-all-start.2 = ((bf16[128,4,1280]{2,0,1:T(8,128)(2,1)}), bf16[128,4,1280]{2,0,1:T(8,128)(2,1)S(1)}, u32[]{:S(2)}, u32[]{:S(2)}) async-start(bf16[128,4,1280]{2,0,1:T(8,128)(2,1)} %copy.28), calls=%async_computation.2 | async-start | bytes 2621440 | tf_op jit(solution)/shard_map/all_to_all | solution.py:26
  361.9 140.6 %reduce-scatter.20.cloned.1.call-start = ((), (), s32[]{:S(2)}) async-start(), calls=%async_computation.13 | async-start | bytes 6553600
  380.6 1.1 copy-start.7
  410.9 219.5 %all-gather.3.cloned.1.call-start = ((), (), s32[]{:S(2)}) async-start(), calls=%async_computation.10 | async-start | bytes 6553600 | tf_op jit(solution)/shard_map/all_gather | solution.py:47
  504.6 19.3 %copy-start.3 = (bf16[128,5120]{0,1:T(8,128)(2,1)}, bf16[128,5120]{0,1:T(8,128)(2,1)S(1)}, u32[]{:S(2)}) copy-start(bf16[128,5120]{0,1:T(8,128)(2,1)S(1)} %add_convert_fusion.1) | copy-start | bytes 3932164
  504.6 19.3 %collective-permute-start.2 = (bf16[128,5120]{0,1:T(8,128)(2,1)S(1)}, bf16[128,5120]{0,1:T(8,128)(2,1)S(1)}, u32[]{:S(2)}, u32[]{:S(2)}) collective-permute-start(bf16[128,5120]{0,1:T(8,128)(2,1)S(1)} %add_convert_fusion.1), channel_id=1, source_target_pairs={{8,0},{16,8},{24,16},{9,1},{17,9},{25,17},{10,2},{18,10},{26,18},{... | collective-permute-start | bytes 3932168 | tf_op jit(solution)/shard_map/ppermute | solution.py:10
  525.4 62.5 %all-to-all-start.3 = ((bf16[128,4,1280]{2,0,1:T(8,128)(2,1)}), bf16[128,4,1280]{2,0,1:T(8,128)(2,1)S(1)}, u32[]{:S(2)}, u32[]{:S(2)}) async-start(bf16[128,4,1280]{2,0,1:T(8,128)(2,1)} %copy.30), calls=%async_computation.3 | async-start | bytes 2621440 | tf_op jit(solution)/shard_map/all_to_all | solution.py:26
  529.3 195.2 %reduce-scatter.22.cloned.1.call-start = ((), (), s32[]{:S(2)}) async-start(), calls=%async_computation.14 | async-start | bytes 6553600
  587.8 1.1 copy-start.8
  607.7 22.7 %copy-start.5 = (bf16[128,4,1280]{2,0,1:T(8,128)(2,1)S(1)}, bf16[128,4,1280]{2,0,1:T(8,128)(2,1)}, u32[]{:S(2)}) copy-start(bf16[128,4,1280]{2,0,1:T(8,128)(2,1)} %copy-done.4) | copy-start | bytes 3932164
  607.7 269.1 %reduce-scatter.14.cloned.1.call-start = ((), (), s32[]{:S(2)}) async-start(), calls=%async_computation.9 | async-start | bytes 19660800 | tf_op jit(solution)/shard_map/reduce_scatter | solution.py:48
Sparse Core Ops, SparseCore 0:
  65.1 102.3 reduce-scatter.15
  233.0 102.1 reduce-scatter.17
  411.0 91.4 reduce-scatter.19
  503.9 126.4 all-gather.2
  632.5 91.9 reduce-scatter.21
  727.2 149.5 reduce-scatter.13
where the time goes:
time: 912 us; the launch traced here: 907 us
  waiting for transfers between devices  721 us (79%)
  local copies, waits for them, and re-layouts  109 us (12%)
  matrix products  25.7 us (3%)
  starting transfers between devices  24.2 us (3%)
  between operations  14.2 us (2%)
  other arithmetic  13.3 us (1%)
    unnamed x10, waiting for transfers between devices  376 us
    reduce_scatter x1, waiting for transfers between devices, on_device(): lax.psum_scatter(lax.dot_general(gathered, kept_columns, (((0,), (0,)), (...  145 us
    all_to_all x4, waiting for transfers between devices, on_device(): lax.all_to_all(gradient, 'tensor', split_axis=1, concat_axis=0, tiled=True)  127 us
    unnamed x29, local copies, waits for them, and re-layouts  61.3 us
    ppermute x3, waiting for transfers between devices, from_behind(): return lax.ppermute(block, axis, route)  50.2 us
    cond x4, local copies, waits for them, and re-layouts, on_device(): lax.cond(on_duty, compute, nothing, columns).astype(jnp.bfloat16)  31.8 us
    all_gather x1, waiting for transfers between devices, on_device(): gathered = lax.all_gather(activations, 'tensor', axis=0, tiled=True)  22.4 us
  transfers between devices with their start and end apart: 13, of which 13 were waited for; matrix products, arithmetic and copies ran while one was open for 5% of the time, Pallas kernels for 0%

commit v1 on v0

v1 whole, which is shorter than its diff:
```python
import functools

import jax
import jax.numpy as jnp
from jax import lax
from jax.experimental import pallas as pl
from jax.experimental.pallas import tpu as pltpu
from jax.sharding import PartitionSpec as P

AXES = ("section", "dp", "tensor")
CHUNKS = 2
VMEM = 56 * 1024 * 1024
F32 = jnp.float32
BF16 = jnp.bfloat16
ANY = pl.BlockSpec(memory_space=pl.ANY)


def params(*semantics):
    return pltpu.CompilerParams(vmem_limit_bytes=VMEM, dimension_semantics=semantics or None)


def divisor(total, options):
    for option in options:
        if total % option == 0:
            return option
    return total


def product(lhs, rhs):
    return lax.dot_general(lhs, rhs, (((1,), (1,)), ((), ())), preferred_element_type=F32)


def send_kernel(count, active, where_ref, *refs):
    parts, weight_ref, grad_ref, out_ref = refs[:count], refs[count], refs[-2], refs[-1]

    @pl.when((pl.program_id(0) == 0) & (pl.program_id(1) == 0))
    def _():
        total = parts[0][...].astype(F32)
        for part in parts[1:]:
            total = total + part[...].astype(F32)
        grad_ref[...] = total.astype(BF16)

    @pl.when(where_ref[1] == active)
    def _():
        grad = grad_ref[...].reshape(-1, grad_ref.shape[-1])
        out_ref[0] = product(grad, weight_ref[0]).astype(BF16)

    @pl.when(where_ref[1] != active)
    def _():
        out_ref[...] = jnp.zeros_like(out_ref)


def send_products(active, where, parts, weights, after=()):
    shards, width, _ = weights.shape
    rows = parts[0].shape[-3:]
    tokens = rows[0] * rows[1]
    step = divisor(width, (640, 512, 256, 128))
    whole = pl.BlockSpec(rows, lambda g, j, w: (0, 0, 0))
    return pl.pallas_call(
        functools.partial(send_kernel, len(parts), active),
        grid_spec=pltpu.PrefetchScalarGridSpec(
            num_scalar_prefetch=1,
            grid=(shards // 2, width // step),
            in_specs=[whole] * len(parts)
            + [pl.BlockSpec((1, step, width), lambda g, j, w: ((w[0] ^ (2 * g + 1)) * (w[1] == active), j * (w[1] == active), 0))]
            + [ANY] * len(after),
            out_specs=[whole, pl.BlockSpec((1, tokens, step), lambda g, j, w: (g, 0, j))],
        ),
        out_shape=[
            jax.ShapeDtypeStruct(rows, BF16),
            jax.ShapeDtypeStruct((shards // 2, tokens, width), BF16),
        ],
        compiler_params=params("arbitrary", "arbitrary"),
        cost_estimate=pl.CostEstimate(
            flops=tokens * width * width * shards, bytes_accessed=width * width * shards, transcendentals=0
        ),
        name="send_products",
    )(where, *parts, weights, *after)


def keep_kernel(active, where_ref, grad_ref, weight_ref, *refs):
    out_ref = refs[-1]
    step = out_ref.shape[-1]

    @pl.when(where_ref[1] == active)
    def _():
        grad = grad_ref[...].reshape(-1, grad_ref.shape[-1])
        out_ref[0] = product(grad, weight_ref[0])

    @pl.when((where_ref[1] == active) & (pl.program_id(0) == 0))
    def _():
        columns = pl.ds(pl.multiple_of(pl.program_id(1) * step, 128), step)
        out_ref[0] += grad_ref[:, :, columns].reshape(-1, step).astype(F32)

    @pl.when(where_ref[1] != active)
    def _():
        out_ref[...] = jnp.zeros_like(out_ref)


def keep_products(active, where, grad, weights, after=()):
    shards, width, _ = weights.shape
    rows = grad.shape
    tokens = rows[0] * rows[1]
    step = divisor(width, (640, 512, 256, 128))
    return pl.pallas_call(
        functools.partial(keep_kernel, active),
        grid_spec=pltpu.PrefetchScalarGridSpec(
            num_scalar_prefetch=1,
            grid=(shards // 2, width // step),
            in_specs=[
                pl.BlockSpec(rows, lambda g, j, w: (0, 0, 0)),
                pl.BlockSpec((1, step, width), lambda g, j, w: ((w[0] ^ (2 * g)) * (w[1] == active), j * (w[1] == active), 0)),
            ]
            + [ANY] * len(after),
            out_specs=pl.BlockSpec((1, tokens, step), lambda g, j, w: (g, 0, j)),
        ),
        out_shape=jax.ShapeDtypeStruct((shards // 2, tokens, width), F32),
        compiler_params=params("arbitrary", "arbitrary"),
        cost_estimate=pl.CostEstimate(
            flops=tokens * width * width * shards, bytes_accessed=width * width * shards, transcendentals=0
        ),
        name="keep_products",
    )(where, grad, weights, *after)


def add_kernel(kept_ref, received_ref, *refs):
    own_ref, next_ref = refs[-2], refs[-1]
    own_ref[...] = (kept_ref[0] + received_ref[0].astype(F32)).astype(own_ref.dtype).reshape(own_ref.shape)
    next_ref[...] = (kept_ref[1] + received_ref[1].astype(F32)).astype(next_ref.dtype).reshape(next_ref.shape)


def add_received(kept, received, shape, own_dtype, after=()):
    return pl.pallas_call(
        add_kernel,
        in_specs=[pl.BlockSpec(memory_space=pltpu.VMEM)] * 2 + [ANY] * len(after),
        out_specs=[pl.BlockSpec(memory_space=pltpu.VMEM)] * 2,
        out_shape=[jax.ShapeDtypeStruct(shape, own_dtype), jax.ShapeDtypeStruct(shape, BF16)],
        compiler_params=params(),
        name="add_received",
    )(kept, received, *after)


def last_kernel(active, count, where_ref, own_ref, part_ref, weight_ref, *refs):
    grad_ref, send_ref, keep_ref, ordered = refs[count:]
    shards, rows, width = grad_ref.shape
    step = weight_ref.shape[1]
    n, j = pl.program_id(0), pl.program_id(1)

    @pl.when((n == 0) & (j == 0))
    def _():
        grad_ref[...] = (own_ref[...].astype(F32) + part_ref[...].astype(F32)).astype(BF16)
        for k in range(shards):
            ordered[k] = grad_ref[where_ref[0] ^ k]

    @pl.when(where_ref[1] == active)
    def _():
        columns = pl.ds(pl.multiple_of(j * step, 128), step)
        total = product(ordered[...].reshape(shards * rows, width), weight_ref[0])
        through = ordered[:, :, columns].reshape(shards * rows, step).astype(F32)
        total = total + jnp.where(n == where_ref[0], through, 0.0)
        total = total.reshape(shards // 2, 2, rows, step)
        keep_ref[...] = total[:, 0]
        send_ref[...] = total[:, 1].astype(BF16)

    @pl.when(where_ref[1] != active)
    def _():
        keep_ref[...] = jnp.zeros_like(keep_ref)
        send_ref[...] = jnp.zeros_like(send_ref)


def last_products(active, where, own, part, weights, after=()):
    shards, width, _ = weights.shape
    rows = own.shape[1]
    step = divisor(width, (640, 512, 256, 128))
    blocks = width // step
    whole = pl.BlockSpec(own.shape, lambda n, j, w: (0, 0, 0))
    halves = pl.BlockSpec((shards // 2, rows, step), lambda n, j, w: (0, 0, n * blocks + j))
    return pl.pallas_call(
        functools.partial(last_kernel, active, len(after)),
        grid_spec=pltpu.PrefetchScalarGridSpec(
            num_scalar_prefetch=1,
            grid=(shards, blocks),
            in_specs=[
                whole,
                whole,
                pl.BlockSpec((1, step, width), lambda n, j, w: (n * (w[1] == active), j * (w[1] == active), 0)),
            ]
            + [ANY] * len(after),
            out_specs=[whole, halves, halves],
            scratch_shapes=[pltpu.VMEM(own.shape, BF16)],
        ),
        out_shape=[
            jax.ShapeDtypeStruct(own.shape, BF16),
            jax.ShapeDtypeStruct((shards // 2, rows, shards * width), BF16),
            jax.ShapeDtypeStruct((shards // 2, rows, shards * width), F32),
        ],
        compiler_params=params("arbitrary", "arbitrary"),
        cost_estimate=pl.CostEstimate(
            flops=2 * shards * rows * width * width * shards,
            bytes_accessed=2 * width * width * shards,
            transcendentals=0,
        ),
        name="last_products",
    )(where, own, part, weights, *after)


def place_kernel(count, where_ref, *refs):
    pieces, outs = refs[:count], refs[count:]
    rows = outs[0].shape[1]
    for i, out_ref in enumerate(outs):
        for k, piece in enumerate(pieces):
            out_ref[where_ref[0] ^ k] = piece[i * rows:(i + 1) * rows]


def place_shards(where, pieces, chunks):
    tokens, width = pieces[0].shape
    memory = pl.BlockSpec(memory_space=pltpu.VMEM)
    return pl.pallas_call(
        functools.partial(place_kernel, len(pieces)),
        in_specs=[pl.BlockSpec(memory_space=pltpu.SMEM)] + [memory] * len(pieces),
        out_specs=[memory] * chunks,
        out_shape=[jax.ShapeDtypeStruct((len(pieces), tokens // chunks, width), BF16)] * chunks,
        compiler_params=params(),
        name="place_shards",
    )(where, *pieces)


def inputs_kernel(shards, chunks, where_ref, *refs):
    pieces, owns, parts, out_ref = refs[:shards], refs[shards:shards + chunks], refs[shards + chunks:-1], refs[-1]
    width = pieces[0].shape[-1]
    rows = owns[0].shape[0]
    for i in range(chunks):
        out_ref[i * rows:(i + 1) * rows] = (owns[i][...] + parts[i][...].astype(F32)).astype(BF16)
    for k in range(shards):
        columns = pl.ds(pl.multiple_of((where_ref[0] ^ k) * width, 128), width)
        out_ref[:, columns] = out_ref[:, columns] + pieces[k][...]


def place_inputs(where, pieces, owns, parts):
    memory = pl.BlockSpec(memory_space=pltpu.VMEM)
    return pl.pallas_call(
        functools.partial(inputs_kernel, len(pieces), len(owns)),
        in_specs=[pl.BlockSpec(memory_space=pltpu.SMEM)] + [memory] * (len(pieces) + 2 * len(owns)),
        out_specs=memory,
        out_shape=jax.ShapeDtypeStruct((pieces[0].shape[0], pieces[0].shape[1] * len(pieces)), BF16),
        compiler_params=params(),
        name="place_inputs",
    )(where, *pieces, *owns, *parts)


def weight_kernel(shards, replicas, where_ref, *refs):
    saved, grads, out_ref, ordered = refs[:shards], refs[shards:shards + replicas], refs[-2], refs[-1]
    _, _, rows, width = grads[0].shape
    tokens = saved[0].shape[0] // replicas

    @pl.when(pl.program_id(0) == 0)
    def _():
        for k in range(shards):
            for j, grad in enumerate(grads):
                at = (k * replicas + j) * tokens
                ordered[at:at + tokens] = grad[:, where_ref[0] ^ k].reshape(tokens, width)

    total = None
    for k in range(shards):
        part = lax.dot_general(
            saved[k][...],
            ordered[k * replicas * tokens:(k + 1) * replicas * tokens],
            (((0,), (0,)), ((), ())),
            preferred_element_type=F32,
        )
        total = part if total is None else total + part
    out_ref[...] = total


def weight_products(where, saved, grads, after=()):
    tokens, features = saved[0].shape
    width = grads[0].shape[-1]
    step = divisor(features, (256, 128))
    whole = pl.BlockSpec(grads[0].shape, lambda n, w: (0, 0, 0, 0))
    shards = len(saved)
    return pl.pallas_call(
        functools.partial(weight_kernel, shards, len(grads)),
        grid_spec=pltpu.PrefetchScalarGridSpec(
            num_scalar_prefetch=1,
            grid=(features // step,),
            in_specs=[pl.BlockSpec((tokens, step), lambda n, w: (0, n))] * shards
            + [whole] * len(grads)
            + [ANY] * len(after),
            out_specs=pl.BlockSpec((step, width), lambda n, w: (n, 0)),
            scratch_shapes=[pltpu.VMEM((shards * tokens, width), BF16)],
        ),
        out_shape=jax.ShapeDtypeStruct((features, width), F32),
        compiler_params=params("arbitrary"),
        cost_estimate=pl.CostEstimate(
            flops=2 * shards * tokens * features * width,
            bytes_accessed=4 * features * width + 2 * shards * tokens * features,
            transcendentals=0,
        ),
        name="weight_products",
    )(where, *saved, *grads, *after)


def on_device(sections, replicas, shards, saved, weight, out_grad):
    tokens, model = out_grad.shape
    width = model // shards
    chunks = CHUNKS
    rows = tokens // chunks
    section, dp, tensor = (lax.axis_index(a) for a in AXES)
    weights = weight[0].reshape(shards, width, width)
    activations = saved[0]

    def place(s, d, t):
        return (s * replicas + d) * shards + t

    def permute(value, route, active):
        pairs = []
        for s in active:
            for d in range(replicas):
                for t in range(shards):
                    to = route(s, d, t)
                    if 0 <= to[0] < sections:
                        pairs.append((place(s, d, t), place(*to)))
        return lax.ppermute(value, AXES, pairs)

    def across(k):
        return lambda s, d, t: (s, d, t ^ k)

    everyone = range(sections)
    where = jnp.stack([tensor, section]).astype(jnp.int32)

    last = sections - 1
    pieces = [lax.dynamic_slice(out_grad, (0, tensor * width), (tokens, width)) * (section == last).astype(BF16)]
    for k in range(1, shards):
        block = lax.dynamic_slice(out_grad, (0, (tensor ^ k) * width), (tokens, width))
        pieces.append(permute(block, across(k), [last]))
    first = place_shards(where, pieces, chunks)

    height = model // replicas
    own_rows = [lax.dynamic_slice(activations, (0, dp * height), (tokens, height))]
    for j in range(1, replicas):
        block = lax.dynamic_slice(activations, (0, lax.rem(dp + replicas - j, replicas) * height), (tokens, height))
        own_rows.append(
            permute(block, lambda s, d, t: (s, (d - j) % replicas, t), everyone)
        )
    own_rows = jnp.concatenate(own_rows, axis=0)
    far = permute(own_rows, across(2), everyone)
    near = permute(own_rows, across(1), everyone), permute(far, across(1), everyone)
    gathered = [own_rows, near[0], far, near[1]]
    waits = {1: (own_rows,), 2: (far,), 3: near}

    kept = []
    incoming = [(first[i],) for i in range(chunks)]
    for r in range(sections):
        active = sections - 1 - r
        grads, outgoing = [], []
        for i in range(chunks):
            after = waits.get(r, ()) if i == 0 else ()
            if active > 0:
                grad, send = send_products(active, where, incoming[i], weights, after)
                received = permute(send, across(1), [active])
                keep = keep_products(active, where, grad, weights)
                own, part = add_received(keep, received, grad.shape, BF16)
                down = permute(own, lambda s, d, t: (s - 1, d, t), [active])
                outgoing.append((down, permute(part, lambda s, d, t: (s - 1, d, t ^ 2), [active])))
            else:
                grad, send, keep = last_products(active, where, *incoming[i], weights, after)
                received = permute(send, across(1), [active])
                own, part = add_received(keep, received, (rows, model), F32)
                outgoing.append((own, permute(part, across(2), [active])))
            grads.append(grad)
        incoming = outgoing
        kept.append(grads)

    mine = jnp.stack([functools.reduce(jnp.add, [grads[i] for grads in kept]) for i in range(chunks)])
    others = [
        permute(mine, lambda s, d, t: (s, (d - j) % replicas, t), everyone) for j in range(1, replicas)
    ]

    back = []
    for k in range(shards):
        block = lax.dynamic_slice(mine, (0, tensor ^ k, 0, 0), (chunks, 1, rows, width)).reshape(tokens, width)
        back.append(permute(block, lambda s, d, t: (s + 1, d, t ^ k), range(sections - 1)))
    weight_grad = weight_products(where, gathered, [mine] + others)
    own_input = place_inputs(where, back, [pair[0] for pair in incoming], [pair[1] for pair in incoming])
    return (own_input[None], weight_grad[None])


def solution(mesh):
    placed = (
        P("section", ("dp", "tensor"), None),
        P("section", None, "tensor"),
        P(("dp", "tensor"), None),
    )
    sizes = [mesh.shape[a] for a in AXES]
    return jax.shard_map(
        functools.partial(on_device, *sizes),
        mesh=mesh,
        in_specs=placed,
        out_specs=(P("section", ("dp", "tensor"), None), P("section", "dp", "tensor")),
        check_vma=False,
    )
```

time: 912 us -> 368 us (0.40)
  waiting for transfers between devices: 721 us -> 173 us
  Pallas kernels: 0 us -> 126 us
  local copies, waits for them, and re-layouts: 109 us -> 15.9 us
  matrix products: 25.7 us -> 0 us
  starting transfers between devices: 24.2 us -> 43.3 us
  between operations: 14.2 us -> 1.23 us
    unnamed x10 -> x0, waiting for transfers between devices: 376 us -> none
    reduce_scatter x1 -> x0, waiting for transfers between devices: 145 us -> none  [on_device(): lax.psum_scatter(lax.dot_general(gathered, kept_columns, (((0,), (0,)), (...]
    all_to_all x4 -> x0, waiting for transfers between devices: 127 us -> none  [on_device(): lax.all_to_all(gradient, 'tensor', split_axis=1, concat_axis=0, tiled=True)]
    pallas_call x0 -> x25, Pallas kernels: none -> 126 us  [the longest x6 32.7 us: send_products(): pl.pallas_call(functools.partial(send_kernel, len(parts), active), grid_s...]
    ppermute x3 -> x34, waiting for transfers between devices: 50.2 us -> 173 us  [permute(): return lax.ppermute(value, AXES, pairs)]
    unnamed x29 -> x72, local copies, waits for them, and re-layouts: 61.3 us -> 15.8 us
    ppermute x3 -> x34, starting transfers between devices: 7.57 us -> 43.3 us  [permute(): return lax.ppermute(value, AXES, pairs)]
    cond x4 -> x0, local copies, waits for them, and re-layouts: 31.8 us -> none  [on_device(): lax.cond(on_duty, compute, nothing, columns).astype(jnp.bfloat16)]
  transfers between devices with their start and end apart: 13 -> 34, of which waited for: 13 -> 9; matrix products, arithmetic and copies ran while one was open for 5% -> 1% of each run, Pallas kernels for 0% -> 32%
where the time goes in v1:
time: 368 us; the launch traced here: 367 us
  waiting for transfers between devices  173 us (47%)
  Pallas kernels  126 us (34%)
  starting transfers between devices  43.3 us (12%)
  local copies, waits for them, and re-layouts  15.9 us (4%)
  other arithmetic  6.55 us (2%)
    ppermute x34, waiting for transfers between devices, permute(): return lax.ppermute(value, AXES, pairs)  173 us
    ppermute x34, starting transfers between devices, permute(): return lax.ppermute(value, AXES, pairs)  43.3 us
    pallas_call x6, Pallas kernels, send_products(): pl.pallas_call(functools.partial(send_kernel, len(parts), active), grid_s...  32.7 us
    pallas_call x6, Pallas kernels, keep_products(): pl.pallas_call(functools.partial(keep_kernel, active), grid_spec=pltpu.Pr...  31.5 us
    pallas_call x8, Pallas kernels, add_received(): pl.pallas_call(add_kernel, in_specs=[pl.BlockSpec(memory_space=pltpu.VMEM...  26.9 us
    unnamed x72, local copies, waits for them, and re-layouts  15.8 us
    pallas_call x1, Pallas kernels, weight_products(): pl.pallas_call(functools.partial(weight_kernel, shards, len(grads)), grid...  15.5 us
    pallas_call x2, Pallas kernels, last_products(): pl.pallas_call(functools.partial(last_kernel, active, len(after)), grid_s...  13.2 us
  transfers between devices with their start and end apart: 34, of which 9 were waited for; matrix products, arithmetic and copies ran while one was open for 1% of the time, Pallas kernels for 32%

profile of v1, /device:TPU:5, one launch (start us, length us, event | category | flops | bytes accessed | tf_op | source)
XLA Modules:
  0.0 366.7 jit_solution(14044015281166069879)
XLA Ops:
  0.7 2.1 constant_dynamic-slice_fusion
  6.4 2.4 place_shards.1
  8.8 4.1 %send_products.6 = (bf16[4,64,1280]{2,1,0:T(8,128)(2,1)}, bf16[2,256,1280]{2,1,0:T(8,128)(2,1)}) custom-call(s32[2]{0:T(128)} %pad_add_fusion.where_ref, bf16[4,64,1280]{2,1,0:T(8,128)(2,1)} %get-tuple-element.38.refs_0_, bf16[4,1280,1280]{2,1,0:T(8,128)(2,1)} %bitcast.17), custom_call_target="tpu_custom_call" | custom-call | flops 1677721600 | bytes 6553600 | tf_op jit(solution)/shard_map/send_products/pallas_call | solution.py:59
  13.0 1.7 collective-permute-start.3
  14.7 4.4 %send_products.9 = (bf16[4,64,1280]{2,1,0:T(8,128)(2,1)}, bf16[2,256,1280]{2,1,0:T(8,128)(2,1)}) custom-call(s32[2]{0:T(128)} %pad_add_fusion.where_ref, bf16[4,64,1280]{2,1,0:T(8,128)(2,1)} %get-tuple-element.52.refs_0_, bf16[4,1280,1280]{2,1,0:T(8,128)(2,1)} %bitcast.18), custom_call_target="tpu_custom_call" | custom-call | flops 1677721600 | bytes 6553600 | tf_op jit(solution)/shard_map/send_products/pallas_call | solution.py:59
  20.0 4.2 %keep_products.6.kept_ref = f32[2,256,1280]{2,1,0:T(8,128)} custom-call(s32[2]{0:T(128)} %pad_add_fusion.where_ref, bf16[4,64,1280]{2,1,0:T(8,128)(2,1)} %get-tuple-element.39.grad_ref, bf16[4,1280,1280]{2,1,0:T(8,128)(2,1)} %bitcast.19), custom_call_target="tpu_custom_call" | custom-call | flops 1677721600 | bytes 6553600 | tf_op jit(solution)/shard_map/keep_products/pallas_call | solution.py:105
  24.2 3.3 add_received.8
  28.9 4.2 %keep_products.9.kept_ref = f32[2,256,1280]{2,1,0:T(8,128)} custom-call(s32[2]{0:T(128)} %pad_add_fusion.where_ref, bf16[4,64,1280]{2,1,0:T(8,128)(2,1)} %get-tuple-element.53.grad_ref, bf16[4,1280,1280]{2,1,0:T(8,128)(2,1)} %bitcast.20), custom_call_target="tpu_custom_call" | custom-call | flops 1677721600 | bytes 6553600 | tf_op jit(solution)/shard_map/keep_products/pallas_call | solution.py:105
  33.2 1.1 copy-done.13
  34.3 3.3 add_received.11
  38.9 1.1 pad_maximum_fusion.1.refs_3_.refs_0_
  41.8 4.6 %send_products.7 = (bf16[4,64,1280]{2,1,0:T(8,128)(2,1)}, bf16[2,256,1280]{2,1,0:T(8,128)(2,1)}) custom-call(s32[2]{0:T(128)} %pad_add_fusion.where_ref, bf16[4,64,1280]{2,1,0:T(8,128)(2,1)} %copy-done.18, bf16[4,64,1280]{2,1,0:T(8,128)(2,1)} %copy-done.20, bf16[4,1280,1280]{2,1,0:T(8,128)(2,1)} %bitcast.21, bf16[256,2560]{1,0:T(8,128)(2,1)} %pad_maximum_fusion.1.refs_3_.refs_0_), custom_call_target="tpu_custom_call" | custom-call | flops 1677721600 | bytes 6553600 | tf_op jit(solution)/shard_map/send_products/pallas_call | solution.py:59
  46.3 0.9 collective-permute-start.7
  48.9 4.6 %send_products.10 = (bf16[4,64,1280]{2,1,0:T(8,128)(2,1)}, bf16[2,256,1280]{2,1,0:T(8,128)(2,1)}) custom-call(s32[2]{0:T(128)} %pad_add_fusion.where_ref, bf16[4,64,1280]{2,1,0:T(8,128)(2,1)} %copy-done.19, bf16[4,64,1280]{2,1,0:T(8,128)(2,1)} %copy-done.23, bf16[4,1280,1280]{2,1,0:T(8,128)(2,1)} %bitcast.22), custom_call_target="tpu_custom_call" | custom-call | flops 1677721600 | bytes 6553600 | tf_op jit(solution)/shard_map/send_products/pallas_call | solution.py:59
  54.2 2.6 collective-permute-start.10
  56.8 4.2 %keep_products.7.kept_ref = f32[2,256,1280]{2,1,0:T(8,128)} custom-call(s32[2]{0:T(128)} %pad_add_fusion.where_ref, bf16[4,64,1280]{2,1,0:T(8,128)(2,1)} %get-tuple-element.43.grad_ref, bf16[4,1280,1280]{2,1,0:T(8,128)(2,1)} %bitcast.23), custom_call_target="tpu_custom_call" | custom-call | flops 1677721600 | bytes 6553600 | tf_op jit(solution)/shard_map/keep_products/pallas_call | solution.py:105
  61.1 1.1 copy-done.16
  62.1 3.3 add_received.9
  65.4 1.3 collective-permute-start.8
  66.7 1.3 collective-permute-start.9
  68.0 4.2 %keep_products.10.kept_ref = f32[2,256,1280]{2,1,0:T(8,128)} custom-call(s32[2]{0:T(128)} %pad_add_fusion.where_ref, bf16[4,64,1280]{2,1,0:T(8,128)(2,1)} %get-tuple-element.57.grad_ref, bf16[4,1280,1280]{2,1,0:T(8,128)(2,1)} %bitcast.24), custom_call_target="tpu_custom_call" | custom-call | flops 1677721600 | bytes 6553600 | tf_op jit(solution)/shard_map/keep_products/pallas_call | solution.py:105
  72.3 1.1 copy-done.15
  73.3 3.4 add_received.12
  76.7 1.3 collective-permute-start.20
  78.0 1.3 collective-permute-start.21
  79.3 33.8 %collective-permute-done.10.refs_3_.refs_2_ = bf16[256,2560]{1,0:T(8,128)(2,1)S(1)} collective-permute-done((bf16[256,2560]{1,0:T(8,128)(2,1)S(1)}, bf16[256,2560]{1,0:T(8,128)(2,1)S(1)}, u32[]{:S(2)}, u32[]{:S(2)}) %collective-permute-start.10) | collective-permute-done | bytes 1310752 | tf_op jit(solution)/shard_map/ppermute | solution.py:323
  113.1 15.5 %collective-permute-done.8.refs_0_ = bf16[4,64,1280]{2,1,0:T(8,128)(2,1)S(1)} collective-permute-done((bf16[4,64,1280]{2,1,0:T(8,128)(2,1)}, bf16[4,64,1280]{2,1,0:T(8,128)(2,1)S(1)}, u32[]{:S(2)}, u32[]{:S(2)}) %collective-permute-start.8) | collective-permute-done | bytes 655392 | tf_op jit(solution)/shard_map/ppermute | solution.py:323
  128.6 49.4 %collective-permute-done.9.refs_1_ = bf16[4,64,1280]{2,1,0:T(8,128)(2,1)S(1)} collective-permute-done((bf16[4,64,1280]{2,1,0:T(8,128)(2,1)}, bf16[4,64,1280]{2,1,0:T(8,128)(2,1)S(1)}, u32[]{:S(2)}, u32[]{:S(2)}) %collective-permute-start.9) | collective-permute-done | bytes 655392 | tf_op jit(solution)/shard_map/ppermute | solution.py:323
  178.9 7.5 %send_products.8 = (bf16[4,64,1280]{2,1,0:T(8,128)(2,1)}, bf16[2,256,1280]{2,1,0:T(8,128)(2,1)}) custom-call(s32[2]{0:T(128)} %pad_add_fusion.where_ref, bf16[4,64,1280]{2,1,0:T(8,128)(2,1)} %copy-done.21, bf16[4,64,1280]{2,1,0:T(8,128)(2,1)} %copy-done.25, bf16[4,1280,1280]{2,1,0:T(8,128)(2,1)} %bitcast.25, bf16[256,2560]{1,0:T(8,128)(2,1)} %copy-done.7), custom_call_target="tpu_custom_call" | custom-call | flops 1677721600 | bytes 6553600 | tf_op jit(solution)/shard_map/send_products/pallas_call | solution.py:59
  186.4 2.0 collective-permute-start.11
  190.2 7.5 %send_products.11 = (bf16[4,64,1280]{2,1,0:T(8,128)(2,1)}, bf16[2,256,1280]{2,1,0:T(8,128)(2,1)}) custom-call(s32[2]{0:T(128)} %pad_add_fusion.where_ref, bf16[4,64,1280]{2,1,0:T(8,128)(2,1)} %copy-done.24, bf16[4,64,1280]{2,1,0:T(8,128)(2,1)} %copy-done.26, bf16[4,1280,1280]{2,1,0:T(8,128)(2,1)} %bitcast.26), custom_call_target="tpu_custom_call" | custom-call | flops 1677721600 | bytes 6553600 | tf_op jit(solution)/shard_map/send_products/pallas_call | solution.py:59
  197.7 3.4 collective-permute-start.22
  201.1 1.4 collective-permute-start.15
  202.6 7.2 %keep_products.8.kept_ref = f32[2,256,1280]{2,1,0:T(8,128)} custom-call(s32[2]{0:T(128)} %pad_add_fusion.where_ref, bf16[4,64,1280]{2,1,0:T(8,128)(2,1)} %get-tuple-element.47.grad_ref, bf16[4,1280,1280]{2,1,0:T(8,128)(2,1)} %bitcast.27), custom_call_target="tpu_custom_call" | custom-call | flops 1677721600 | bytes 6553600 | tf_op jit(solution)/shard_map/keep_products/pallas_call | solution.py:105
  209.8 3.3 add_received.10
  213.2 2.1 collective-permute-start.12
  215.3 2.1 collective-permute-start.13
  217.4 7.2 %keep_products.11.kept_ref = f32[2,256,1280]{2,1,0:T(8,128)} custom-call(s32[2]{0:T(128)} %pad_add_fusion.where_ref, bf16[4,64,1280]{2,1,0:T(8,128)(2,1)} %get-tuple-element.61.grad_ref, bf16[4,1280,1280]{2,1,0:T(8,128)(2,1)} %bitcast.28), custom_call_target="tpu_custom_call" | custom-call | flops 1677721600 | bytes 6553600 | tf_op jit(solution)/shard_map/keep_products/pallas_call | solution.py:105
  224.7 1.5 collective-permute-done.22.received_ref
  226.2 1.1 copy-done.14
  227.2 3.3 add_received.13
  230.5 1.3 collective-permute-start.23
  231.8 8.4 %collective-permute-done.14.refs_0_.refs_1_ = bf16[256,2560]{1,0:T(8,128)(2,1)S(1)} collective-permute-done((bf16[256,2560]{1,0:T(8,128)(2,1)S(1)}, bf16[256,2560]{1,0:T(8,128)(2,1)S(1)}, u32[]{:S(2)}, u32[]{:S(2)}) %collective-permute-start.14) | collective-permute-done | bytes 1310752 | tf_op jit(solution)/shard_map/ppermute | solution.py:323
  240.2 1.6 collective-permute-start.24
  241.8 17.3 %collective-permute-done.15.refs_1_.refs_3_ = bf16[256,2560]{1,0:T(8,128)(2,1)S(1)} collective-permute-done((bf16[256,2560]{1,0:T(8,128)(2,1)S(1)}, bf16[256,2560]{1,0:T(8,128)(2,1)S(1)}, u32[]{:S(2)}, u32[]{:S(2)}) %collective-permute-start.15) | collective-permute-done | bytes 1310752 | tf_op jit(solution)/shard_map/ppermute | solution.py:323
  259.1 1.0 copy-done.10
  260.2 6.5 %last_products.2 = (bf16[4,64,1280]{2,1,0:T(8,128)(2,1)}, bf16[2,64,5120]{2,1,0:T(8,128)(2,1)}, f32[2,64,5120]{2,1,0:T(8,128)}) custom-call(s32[2]{0:T(128)} %pad_add_fusion.where_ref, bf16[4,64,1280]{2,1,0:T(8,128)(2,1)} %collective-permute-done.12.own_ref, bf16[4,64,1280]{2,1,0:T(8,128)(2,1)} %collective-permute-done.13.part_ref, ...), custom_call_target="tpu_custom_call" | custom-call | flops 3355443200 | bytes 13107200 | tf_op jit(solution)/shard_map/last_products/pallas_call | solution.py:178
  266.6 1.7 collective-permute-start.29
  268.3 1.2 add_bitcast_fusion.1
  271.3 6.7 %last_products.3 = (bf16[4,64,1280]{2,1,0:T(8,128)(2,1)}, bf16[2,64,5120]{2,1,0:T(8,128)(2,1)}, f32[2,64,5120]{2,1,0:T(8,128)}) custom-call(s32[2]{0:T(128)} %pad_add_fusion.where_ref, bf16[4,64,1280]{2,1,0:T(8,128)(2,1)} %copy-done.17, bf16[4,64,1280]{2,1,0:T(8,128)(2,1)} %copy-done.22, bf16[4,1280,1280]{2,1,0:T(8,128)(2,1)} %bitcast.30), custom_call_target="tpu_custom_call" | custom-call | flops 3355443200 | bytes 13107200 | tf_op jit(solution)/shard_map/last_products/pallas_call | solution.py:178
  278.0 1.2 add_bitcast_fusion
  279.3 1.7 collective-permute-start.30
  281.4 0.9 copy-done.12
  282.2 1.9 collective-permute-start.25
  284.1 3.6 add_received.14
  288.5 3.5 add_received.15
  292.6 1.9 collective-permute-start.28
  294.6 1.9 collective-permute-start.26
  296.5 7.0 %collective-permute-done.33.refs_5_ = bf16[2,4,64,1280]{3,2,1,0:T(8,128)(2,1)} collective-permute-done((bf16[2,4,64,1280]{3,2,1,0:T(8,128)(2,1)S(1)}, bf16[2,4,64,1280]{3,2,1,0:T(8,128)(2,1)}, u32[]{:S(2)}, u32[]{:S(2)}) %collective-permute-start.33) | collective-permute-done | bytes 1310752 | tf_op jit(solution)/shard_map/ppermute | solution.py:323
  303.5 1.9 collective-permute-start.27
  305.5 15.5 %weight_products.1 = f32[2560,1280]{1,0:T(8,128)} custom-call(s32[2]{0:T(128)} %pad_add_fusion.where_ref, bf16[256,2560]{1,0:T(8,128)(2,1)} %pad_maximum_fusion.1.refs_3_.refs_0_, bf16[256,2560]{1,0:T(8,128)(2,1)} %copy-done.9, bf16[256,2560]{1,0:T(8,128)(2,1)} %copy-done.7, bf16[256,2560]{1,0:T(8,128)(2,1)} %copy-done.10, ...), custom_call_target="tpu_custom_call" | custom-call | flops 6710886400 | bytes 18350080 | tf_op jit(solution)/shard_map/weight_products/pallas_call | solution.py:281
  321.0 23.0 %collective-permute-done.28.refs_3_ = bf16[128,1280]{1,0:T(8,128)(2,1)S(1)} collective-permute-done((bf16[128,1280]{1,0:T(8,128)(2,1)S(1)}, bf16[128,1280]{1,0:T(8,128)(2,1)S(1)}, u32[]{:S(2)}, u32[]{:S(2)}) %collective-permute-start.28) | collective-permute-done | bytes 327712 | tf_op jit(solution)/shard_map/ppermute | solution.py:323
  343.9 17.4 %collective-permute-done.27.refs_2_ = bf16[128,1280]{1,0:T(8,128)(2,1)S(1)} collective-permute-done((bf16[128,1280]{1,0:T(8,128)(2,1)S(1)}, bf16[128,1280]{1,0:T(8,128)(2,1)S(1)}, u32[]{:S(2)}, u32[]{:S(2)}) %collective-permute-start.27) | collective-permute-done | bytes 327712 | tf_op jit(solution)/shard_map/ppermute | solution.py:323
  362.6 4.1 %place_inputs.1 = bf16[128,5120]{1,0:T(8,128)(2,1)} custom-call(s32[2]{0:T(128)} %pad_add_fusion.where_ref, bf16[128,1280]{1,0:T(8,128)(2,1)} %copy-done.32, bf16[128,1280]{1,0:T(8,128)(2,1)} %copy-done.34, bf16[128,1280]{1,0:T(8,128)(2,1)} %copy-done.35, bf16[128,1280]{1,0:T(8,128)(2,1)} %copy-done.33, f32[64,5120]{1,0:T(8,128)} %get-tuple-element.68.refs_4_, ...), custom_call_target="tpu_custom_call" | custom-call | tf_op jit(solution)/shard_map/place_inputs/pallas_call | solution.py:241
  (109 shorter events, 18.6 us)
Async XLA Ops:
  2.8 2.7 collective-permute-start.2
  3.4 2.0 collective-permute-start
  4.1 1.4 collective-permute-start.1
  5.5 0.9 copy-start.30
  5.5 0.9 copy-start.31
  13.0 11.3 %collective-permute-start.3 = (bf16[2,256,1280]{2,1,0:T(8,128)(2,1)}, bf16[2,256,1280]{2,1,0:T(8,128)(2,1)}, u32[]{:S(2)}, u32[]{:S(2)}) collective-permute-start(bf16[2,256,1280]{2,1,0:T(8,128)(2,1)} %get-tuple-element.40), channel_id=1, source_target_pairs={{24,25},{25,24},{26,27},{27,26},{28,29},{29,28},{30,31},{31,30}} | collective-permute-start | bytes 3932168 | tf_op jit(solution)/shard_map/ppermute | solution.py:323
  14.7 5.1 %copy-start.11 = (bf16[1,128,5120]{2,1,0:T(8,128)(2,1)S(1)}, bf16[1,128,5120]{2,1,0:T(8,128)(2,1)}, u32[]{:S(2)}) copy-start(bf16[1,128,5120]{2,1,0:T(8,128)(2,1)} %param.3) | copy-start | bytes 3932164
  19.0 14.1 %collective-permute-start.16 = (bf16[2,256,1280]{2,1,0:T(8,128)(2,1)}, bf16[2,256,1280]{2,1,0:T(8,128)(2,1)S(1)}, u32[]{:S(2)}, u32[]{:S(2)}) collective-permute-start(bf16[2,256,1280]{2,1,0:T(8,128)(2,1)} %get-tuple-element.54), channel_id=1, source_target_pairs={{24,25},{25,24},{26,27},{27,26},{28,29},{29,28},{30,31},{31,30}} | collective-permute-start | bytes 3932168 | tf_op jit(solution)/shard_map/ppermute | solution.py:323
  19.9 19.0 %collective-permute-start.6 = (bf16[128,2560]{1,0:T(8,128)(2,1)S(1)}, bf16[128,2560]{1,0:T(8,128)(2,1)S(1)}, u32[]{:S(2)}, u32[]{:S(2)}) collective-permute-start(bf16[128,2560]{1,0:T(8,128)(2,1)S(1)} %get-tuple-element.79), channel_id=1, source_target_pairs={{0,4},{1,5},{2,6},{3,7},{4,0},{5,1},{6,2},{7,3},{8,12},{9,13},{10,... | collective-permute-start | bytes 1966088 | tf_op jit(solution)/shard_map/ppermute | solution.py:323
  27.5 12.6 %collective-permute-start.4 = (bf16[4,64,1280]{2,1,0:T(8,128)(2,1)}, bf16[4,64,1280]{2,1,0:T(8,128)(2,1)S(1)}, u32[]{:S(2)}, u32[]{:S(2)}) collective-permute-start(bf16[4,64,1280]{2,1,0:T(8,128)(2,1)} %get-tuple-element.41), channel_id=1, source_target_pairs={{24,16},{25,17},{26,18},{27,19},{28,20},{29,21},{30,22},{31,23}} | collective-permute-start | bytes 1966088 | tf_op jit(solution)/shard_map/ppermute | solution.py:323
  28.2 11.9 %collective-permute-start.5 = (bf16[4,64,1280]{2,1,0:T(8,128)(2,1)}, bf16[4,64,1280]{2,1,0:T(8,128)(2,1)S(1)}, u32[]{:S(2)}, u32[]{:S(2)}) collective-permute-start(bf16[4,64,1280]{2,1,0:T(8,128)(2,1)} %get-tuple-element.42), channel_id=1, source_target_pairs={{24,18},{25,19},{26,16},{27,17},{28,22},{29,23},{30,20},{31,21}} | collective-permute-start | bytes 1966088 | tf_op jit(solution)/shard_map/ppermute | solution.py:323
  33.2 1.1 copy-start.13
  37.5 9.7 %collective-permute-start.17 = (bf16[4,64,1280]{2,1,0:T(8,128)(2,1)}, bf16[4,64,1280]{2,1,0:T(8,128)(2,1)S(1)}, u32[]{:S(2)}, u32[]{:S(2)}) collective-permute-start(bf16[4,64,1280]{2,1,0:T(8,128)(2,1)} %get-tuple-element.55), channel_id=1, source_target_pairs={{24,16},{25,17},{26,18},{27,19},{28,20},{29,21},{30,22},{31,23}} | collective-permute-start | bytes 1966088 | tf_op jit(solution)/shard_map/ppermute | solution.py:323
  38.2 9.0 %collective-permute-start.18 = (bf16[4,64,1280]{2,1,0:T(8,128)(2,1)}, bf16[4,64,1280]{2,1,0:T(8,128)(2,1)S(1)}, u32[]{:S(2)}, u32[]{:S(2)}) collective-permute-start(bf16[4,64,1280]{2,1,0:T(8,128)(2,1)} %get-tuple-element.56), channel_id=1, source_target_pairs={{24,18},{25,19},{26,16},{27,17},{28,22},{29,23},{30,20},{31,21}} | collective-permute-start | bytes 1966088 | tf_op jit(solution)/shard_map/ppermute | solution.py:323
  46.3 7.9 %copy-start = (bf16[256,2560]{1,0:T(8,128)(2,1)S(1)}, bf16[256,2560]{1,0:T(8,128)(2,1)}, u32[]{:S(2)}) copy-start(bf16[256,2560]{1,0:T(8,128)(2,1)} %pad_maximum_fusion.1.refs_3_.refs_0_) | copy-start | bytes 3932164
  46.3 14.7 %collective-permute-start.7 = (bf16[2,256,1280]{2,1,0:T(8,128)(2,1)}, bf16[2,256,1280]{2,1,0:T(8,128)(2,1)S(1)}, u32[]{:S(2)}, u32[]{:S(2)}) collective-permute-start(bf16[2,256,1280]{2,1,0:T(8,128)(2,1)} %get-tuple-element.44), channel_id=1, source_target_pairs={{16,17},{17,16},{18,19},{19,18},{20,21},{21,20},{22,23},{23,22}} | collective-permute-start | bytes 3932168 | tf_op jit(solution)/shard_map/ppermute | solution.py:323
  47.2 0.8 copy-start.19
  53.5 18.8 %collective-permute-start.19 = (bf16[2,256,1280]{2,1,0:T(8,128)(2,1)}, bf16[2,256,1280]{2,1,0:T(8,128)(2,1)S(1)}, u32[]{:S(2)}, u32[]{:S(2)}) collective-permute-start(bf16[2,256,1280]{2,1,0:T(8,128)(2,1)} %get-tuple-element.58), channel_id=1, source_target_pairs={{16,17},{17,16},{18,19},{19,18},{20,21},{21,20},{22,23},{23,22}} | collective-permute-start | bytes 3932168 | tf_op jit(solution)/shard_map/ppermute | solution.py:323
  54.2 58.9 %collective-permute-start.10 = (bf16[256,2560]{1,0:T(8,128)(2,1)S(1)}, bf16[256,2560]{1,0:T(8,128)(2,1)S(1)}, u32[]{:S(2)}, u32[]{:S(2)}) collective-permute-start(bf16[256,2560]{1,0:T(8,128)(2,1)S(1)} %copy-done), channel_id=1, source_target_pairs={{0,2},{1,3},{2,0},{3,1},{4,6},{5,7},{6,4},{7,5},{8,10},{9,11},{10,... | collective-permute-start | bytes 3932168 | tf_op jit(solution)/shard_map/ppermute | solution.py:323
  61.1 1.1 copy-start.16
  65.4 63.2 %collective-permute-start.8 = (bf16[4,64,1280]{2,1,0:T(8,128)(2,1)}, bf16[4,64,1280]{2,1,0:T(8,128)(2,1)S(1)}, u32[]{:S(2)}, u32[]{:S(2)}) collective-permute-start(bf16[4,64,1280]{2,1,0:T(8,128)(2,1)} %get-tuple-element.45), channel_id=1, source_target_pairs={{16,8},{17,9},{18,10},{19,11},{20,12},{21,13},{22,14},{23,15}} | collective-permute-start | bytes 1966088 | tf_op jit(solution)/shard_map/ppermute | solution.py:323
  66.7 111.3 %collective-permute-start.9 = (bf16[4,64,1280]{2,1,0:T(8,128)(2,1)}, bf16[4,64,1280]{2,1,0:T(8,128)(2,1)S(1)}, u32[]{:S(2)}, u32[]{:S(2)}) collective-permute-start(bf16[4,64,1280]{2,1,0:T(8,128)(2,1)} %get-tuple-element.46), channel_id=1, source_target_pairs={{16,10},{17,11},{18,8},{19,9},{20,14},{21,15},{22,12},{23,13}} | collective-permute-start | bytes 1966088 | tf_op jit(solution)/shard_map/ppermute | solution.py:323
  72.3 1.1 copy-start.15
  76.7 111.8 %collective-permute-start.20 = (bf16[4,64,1280]{2,1,0:T(8,128)(2,1)}, bf16[4,64,1280]{2,1,0:T(8,128)(2,1)S(1)}, u32[]{:S(2)}, u32[]{:S(2)}) collective-permute-start(bf16[4,64,1280]{2,1,0:T(8,128)(2,1)} %get-tuple-element.59), channel_id=1, source_target_pairs={{16,8},{17,9},{18,10},{19,11},{20,12},{21,13},{22,14},{23,15}} | collective-permute-start | bytes 1966088 | tf_op jit(solution)/shard_map/ppermute | solution.py:323
  78.0 110.5 %collective-permute-start.21 = (bf16[4,64,1280]{2,1,0:T(8,128)(2,1)}, bf16[4,64,1280]{2,1,0:T(8,128)(2,1)S(1)}, u32[]{:S(2)}, u32[]{:S(2)}) collective-permute-start(bf16[4,64,1280]{2,1,0:T(8,128)(2,1)} %get-tuple-element.60), channel_id=1, source_target_pairs={{16,10},{17,11},{18,8},{19,9},{20,14},{21,15},{22,12},{23,13}} | collective-permute-start | bytes 1966088 | tf_op jit(solution)/shard_map/ppermute | solution.py:323
  113.1 65.0 %copy-start.7 = (bf16[256,2560]{1,0:T(8,128)(2,1)}, bf16[256,2560]{1,0:T(8,128)(2,1)S(1)}, u32[]{:S(2)}) copy-start(bf16[256,2560]{1,0:T(8,128)(2,1)S(1)} %collective-permute-done.10.refs_3_.refs_2_) | copy-start | bytes 3932164
  128.6 49.4 %copy-start.21 = (bf16[4,64,1280]{2,1,0:T(8,128)(2,1)}, bf16[4,64,1280]{2,1,0:T(8,128)(2,1)S(1)}, u32[]{:S(2)}) copy-start(bf16[4,64,1280]{2,1,0:T(8,128)(2,1)S(1)} %collective-permute-done.8.refs_0_) | copy-start | bytes 1966084
  178.1 0.8 copy-start.25
  186.4 14.7 %copy-start.8 = (bf16[256,2560]{1,0:T(8,128)(2,1)S(1)}, bf16[256,2560]{1,0:T(8,128)(2,1)}, u32[]{:S(2)}) copy-start(bf16[256,2560]{1,0:T(8,128)(2,1)} %copy-done.7) | copy-start | bytes 3932164
  186.4 23.4 %collective-permute-start.11 = (bf16[2,256,1280]{2,1,0:T(8,128)(2,1)}, bf16[2,256,1280]{2,1,0:T(8,128)(2,1)}, u32[]{:S(2)}, u32[]{:S(2)}) collective-permute-start(bf16[2,256,1280]{2,1,0:T(8,128)(2,1)} %get-tuple-element.48), channel_id=1, source_target_pairs={{8,9},{9,8},{10,11},{11,10},{12,13},{13,12},{14,15},{15,14}} | collective-permute-start | bytes 3932168 | tf_op jit(solution)/shard_map/ppermute | solution.py:323
  189.3 0.9 copy-start.26
  197.7 28.5 %collective-permute-start.22 = (bf16[2,256,1280]{2,1,0:T(8,128)(2,1)}, bf16[2,256,1280]{2,1,0:T(8,128)(2,1)S(1)}, u32[]{:S(2)}, u32[]{:S(2)}) collective-permute-start(bf16[2,256,1280]{2,1,0:T(8,128)(2,1)} %get-tuple-element.62), channel_id=1, source_target_pairs={{8,9},{9,8},{10,11},{11,10},{12,13},{13,12},{14,15},{15,14}} | collective-permute-start | bytes 3932168 | tf_op jit(solution)/shard_map/ppermute | solution.py:323
  201.1 39.2 %collective-permute-start.14 = (bf16[256,2560]{1,0:T(8,128)(2,1)S(1)}, bf16[256,2560]{1,0:T(8,128)(2,1)S(1)}, u32[]{:S(2)}, u32[]{:S(2)}) collective-permute-start(bf16[256,2560]{1,0:T(8,128)(2,1)S(1)} %copy-done), channel_id=1, source_target_pairs={{0,1},{1,0},{2,3},{3,2},{4,5},{5,4},{6,7},{7,6},{8,9},{9,8},{10,11... | collective-permute-start | bytes 3932168 | tf_op jit(solution)/shard_map/ppermute | solution.py:323
  201.1 58.0 %collective-permute-start.15 = (bf16[256,2560]{1,0:T(8,128)(2,1)S(1)}, bf16[256,2560]{1,0:T(8,128)(2,1)S(1)}, u32[]{:S(2)}, u32[]{:S(2)}) collective-permute-start(bf16[256,2560]{1,0:T(8,128)(2,1)S(1)} %copy-done.8), channel_id=1, source_target_pairs={{0,1},{1,0},{2,3},{3,2},{4,5},{5,4},{6,7},{7,6},{8,9},{9,8},{10,11... | collective-permute-start | bytes 3932168 | tf_op jit(solution)/shard_map/ppermute | solution.py:323
  213.2 45.9 %collective-permute-start.12 = (bf16[4,64,1280]{2,1,0:T(8,128)(2,1)}, bf16[4,64,1280]{2,1,0:T(8,128)(2,1)}, u32[]{:S(2)}, u32[]{:S(2)}) collective-permute-start(bf16[4,64,1280]{2,1,0:T(8,128)(2,1)} %get-tuple-element.49), channel_id=1, source_target_pairs={{8,0},{9,1},{10,2},{11,3},{12,4},{13,5},{14,6},{15,7}} | collective-permute-start | bytes 1966088 | tf_op jit(solution)/shard_map/ppermute | solution.py:323
  215.3 43.8 %collective-permute-start.13 = (bf16[4,64,1280]{2,1,0:T(8,128)(2,1)}, bf16[4,64,1280]{2,1,0:T(8,128)(2,1)}, u32[]{:S(2)}, u32[]{:S(2)}) collective-permute-start(bf16[4,64,1280]{2,1,0:T(8,128)(2,1)} %get-tuple-element.50), channel_id=1, source_target_pairs={{8,2},{9,3},{10,0},{11,1},{12,6},{13,7},{14,4},{15,5}} | collective-permute-start | bytes 1966088 | tf_op jit(solution)/shard_map/ppermute | solution.py:323
  226.2 1.1 copy-start.14
  230.5 39.1 %collective-permute-start.23 = (bf16[4,64,1280]{2,1,0:T(8,128)(2,1)}, bf16[4,64,1280]{2,1,0:T(8,128)(2,1)S(1)}, u32[]{:S(2)}, u32[]{:S(2)}) collective-permute-start(bf16[4,64,1280]{2,1,0:T(8,128)(2,1)} %get-tuple-element.63), channel_id=1, source_target_pairs={{8,0},{9,1},{10,2},{11,3},{12,4},{13,5},{14,6},{15,7}} | collective-permute-start | bytes 1966088 | tf_op jit(solution)/shard_map/ppermute | solution.py:323
  240.2 18.9 %copy-start.9 = (bf16[256,2560]{1,0:T(8,128)(2,1)}, bf16[256,2560]{1,0:T(8,128)(2,1)S(1)}, u32[]{:S(2)}) copy-start(bf16[256,2560]{1,0:T(8,128)(2,1)S(1)} %collective-permute-done.14.refs_0_.refs_1_) | copy-start | bytes 3932164
  240.2 28.1 %copy-start.2 = (bf16[4,64,1280]{2,1,0:T(8,128)(2,1)S(1)}, bf16[4,64,1280]{2,1,0:T(8,128)(2,1)}, u32[]{:S(2)}) copy-start(bf16[4,64,1280]{2,1,0:T(8,128)(2,1)} %get-tuple-element.39.grad_ref) | copy-start | bytes 1966084
  240.2 28.1 %copy-start.4 = (bf16[4,64,1280]{2,1,0:T(8,128)(2,1)S(1)}, bf16[4,64,1280]{2,1,0:T(8,128)(2,1)}, u32[]{:S(2)}) copy-start(bf16[4,64,1280]{2,1,0:T(8,128)(2,1)} %get-tuple-element.43.grad_ref) | copy-start | bytes 1966084
  240.2 28.1 %copy-start.6 = (bf16[4,64,1280]{2,1,0:T(8,128)(2,1)S(1)}, bf16[4,64,1280]{2,1,0:T(8,128)(2,1)}, u32[]{:S(2)}) copy-start(bf16[4,64,1280]{2,1,0:T(8,128)(2,1)} %get-tuple-element.47.grad_ref) | copy-start | bytes 1966084
  240.2 29.4 %collective-permute-start.24 = (bf16[4,64,1280]{2,1,0:T(8,128)(2,1)}, bf16[4,64,1280]{2,1,0:T(8,128)(2,1)S(1)}, u32[]{:S(2)}, u32[]{:S(2)}) collective-permute-start(bf16[4,64,1280]{2,1,0:T(8,128)(2,1)} %get-tuple-element.64), channel_id=1, source_target_pairs={{8,2},{9,3},{10,0},{11,1},{12,6},{13,7},{14,4},{15,5}} | collective-permute-start | bytes 1966088 | tf_op jit(solution)/shard_map/ppermute | solution.py:323
  259.1 1.0 copy-start.10
  266.6 17.5 %collective-permute-start.29 = (bf16[2,64,5120]{2,1,0:T(8,128)(2,1)}, bf16[2,64,5120]{2,1,0:T(8,128)(2,1)}, u32[]{:S(2)}, u32[]{:S(2)}) collective-permute-start(bf16[2,64,5120]{2,1,0:T(8,128)(2,1)} %get-tuple-element.67), channel_id=1, source_target_pairs={{0,1},{1,0},{2,3},{3,2},{4,5},{5,4},{6,7},{7,6}} | collective-permute-start | bytes 3932168 | tf_op jit(solution)/shard_map/ppermute | solution.py:323
  269.5 8.5 %copy-start.1 = (bf16[4,64,1280]{2,1,0:T(8,128)(2,1)S(1)}, bf16[4,64,1280]{2,1,0:T(8,128)(2,1)}, u32[]{:S(2)}) copy-start(bf16[4,64,1280]{2,1,0:T(8,128)(2,1)} %get-tuple-element.53.grad_ref) | copy-start | bytes 1966084
  269.6 8.5 %copy-start.3 = (bf16[4,64,1280]{2,1,0:T(8,128)(2,1)S(1)}, bf16[4,64,1280]{2,1,0:T(8,128)(2,1)}, u32[]{:S(2)}) copy-start(bf16[4,64,1280]{2,1,0:T(8,128)(2,1)} %get-tuple-element.57.grad_ref) | copy-start | bytes 1966084
  269.6 8.5 %copy-start.5 = (bf16[4,64,1280]{2,1,0:T(8,128)(2,1)S(1)}, bf16[4,64,1280]{2,1,0:T(8,128)(2,1)}, u32[]{:S(2)}) copy-start(bf16[4,64,1280]{2,1,0:T(8,128)(2,1)} %get-tuple-element.61.grad_ref) | copy-start | bytes 1966084
  269.6 0.9 copy-start.17
  270.5 0.9 copy-start.22
  279.3 9.2 %collective-permute-start.30 = (bf16[2,64,5120]{2,1,0:T(8,128)(2,1)}, bf16[2,64,5120]{2,1,0:T(8,128)(2,1)}, u32[]{:S(2)}, u32[]{:S(2)}) collective-permute-start(bf16[2,64,5120]{2,1,0:T(8,128)(2,1)} %get-tuple-element.70), channel_id=1, source_target_pairs={{0,1},{1,0},{2,3},{3,2},{4,5},{5,4},{6,7},{7,6}} | collective-permute-start | bytes 3932168 | tf_op jit(solution)/shard_map/ppermute | solution.py:323
  281.1 1.1 copy-start.12
  281.1 22.4 %collective-permute-start.33 = (bf16[2,4,64,1280]{3,2,1,0:T(8,128)(2,1)S(1)}, bf16[2,4,64,1280]{3,2,1,0:T(8,128)(2,1)}, u32[]{:S(2)}, u32[]{:S(2)}) collective-permute-start(bf16[2,4,64,1280]{3,2,1,0:T(8,128)(2,1)S(1)} %pad_maximum_fusion.refs_4_), channel_id=1, source_target_pairs={{0,4},{1,5},{2,6},{3,7},{4,0},{5,1},{6,2},{7,3},{8,12},{9,13},{10,... | collective-permute-start | bytes 3932168 | tf_op jit(solution)/shard_map/ppermute | solution.py:323
  282.2 12.4 %collective-permute-start.25 = (bf16[128,1280]{1,0:T(8,128)(2,1)S(1)}, bf16[128,1280]{1,0:T(8,128)(2,1)S(1)}, u32[]{:S(2)}, u32[]{:S(2)}) collective-permute-start(bf16[128,1280]{1,0:T(8,128)(2,1)S(1)} %bitcast.35), channel_id=1, source_target_pairs={{0,8},{1,9},{2,10},{3,11},{4,12},{5,13},{6,14},{7,15},{8,16},{9,17... | collective-permute-start | bytes 983048 | tf_op jit(solution)/shard_map/ppermute | solution.py:323
  287.8 73.6 %collective-permute-start.31 = (bf16[64,5120]{1,0:T(8,128)(2,1)}, bf16[64,5120]{1,0:T(8,128)(2,1)S(1)}, u32[]{:S(2)}, u32[]{:S(2)}) collective-permute-start(bf16[64,5120]{1,0:T(8,128)(2,1)} %get-tuple-element.72), channel_id=1, source_target_pairs={{0,2},{1,3},{2,0},{3,1},{4,6},{5,7},{6,4},{7,5}} | collective-permute-start | bytes 1966088 | tf_op jit(solution)/shard_map/ppermute | solution.py:323
  292.0 69.5 %collective-permute-start.32 = (bf16[64,5120]{1,0:T(8,128)(2,1)}, bf16[64,5120]{1,0:T(8,128)(2,1)S(1)}, u32[]{:S(2)}, u32[]{:S(2)}) collective-permute-start(bf16[64,5120]{1,0:T(8,128)(2,1)} %get-tuple-element.73), channel_id=1, source_target_pairs={{0,2},{1,3},{2,0},{3,1},{4,6},{5,7},{6,4},{7,5}} | collective-permute-start | bytes 1966088 | tf_op jit(solution)/shard_map/ppermute | solution.py:323
  292.6 51.3 %collective-permute-start.28 = (bf16[128,1280]{1,0:T(8,128)(2,1)S(1)}, bf16[128,1280]{1,0:T(8,128)(2,1)S(1)}, u32[]{:S(2)}, u32[]{:S(2)}) collective-permute-start(bf16[128,1280]{1,0:T(8,128)(2,1)S(1)} %bitcast.34), channel_id=1, source_target_pairs={{0,11},{1,10},{2,9},{3,8},{4,15},{5,14},{6,13},{7,12},{8,19},{9,18... | collective-permute-start | bytes 983048 | tf_op jit(solution)/shard_map/ppermute | solution.py:323
  294.6 26.4 %copy-start.32 = (bf16[128,1280]{1,0:T(8,128)(2,1)}, bf16[128,1280]{1,0:T(8,128)(2,1)S(1)}, u32[]{:S(2)}) copy-start(bf16[128,1280]{1,0:T(8,128)(2,1)S(1)} %collective-permute-done.25.refs_0_) | copy-start | bytes 983044
  294.6 49.3 %collective-permute-start.26 = (bf16[128,1280]{1,0:T(8,128)(2,1)S(1)}, bf16[128,1280]{1,0:T(8,128)(2,1)S(1)}, u32[]{:S(2)}, u32[]{:S(2)}) collective-permute-start(bf16[128,1280]{1,0:T(8,128)(2,1)S(1)} %bitcast.33), channel_id=1, source_target_pairs={{0,9},{1,8},{2,11},{3,10},{4,13},{5,12},{6,15},{7,14},{8,17},{9,16... | collective-permute-start | bytes 983048 | tf_op jit(solution)/shard_map/ppermute | solution.py:323
  303.5 57.9 %collective-permute-start.27 = (bf16[128,1280]{1,0:T(8,128)(2,1)S(1)}, bf16[128,1280]{1,0:T(8,128)(2,1)S(1)}, u32[]{:S(2)}, u32[]{:S(2)}) collective-permute-start(bf16[128,1280]{1,0:T(8,128)(2,1)S(1)} %bitcast.32), channel_id=1, source_target_pairs={{0,10},{1,11},{2,8},{3,9},{4,14},{5,15},{6,12},{7,13},{8,18},{9,19... | collective-permute-start | bytes 983048 | tf_op jit(solution)/shard_map/ppermute | solution.py:323
  343.9 17.5 %copy-start.33 = (bf16[128,1280]{1,0:T(8,128)(2,1)}, bf16[128,1280]{1,0:T(8,128)(2,1)S(1)}, u32[]{:S(2)}) copy-start(bf16[128,1280]{1,0:T(8,128)(2,1)S(1)} %collective-permute-done.28.refs_3_) | copy-start | bytes 983044
  343.9 17.5 %copy-start.34 = (bf16[128,1280]{1,0:T(8,128)(2,1)}, bf16[128,1280]{1,0:T(8,128)(2,1)S(1)}, u32[]{:S(2)}) copy-start(bf16[128,1280]{1,0:T(8,128)(2,1)S(1)} %collective-permute-done.26.refs_1_) | copy-start | bytes 983044
  361.4 1.0 copy-start.27
  361.4 1.2 copy-start.28
  (6 other events, 4.8 us)

commit v2 on v0

v2 whole, which is shorter than its diff:
```python
import functools

import jax
import jax.numpy as jnp
from jax import lax
from jax.experimental import pallas as pl
from jax.experimental.pallas import tpu as pltpu
from jax.sharding import PartitionSpec as P

AXES = ("section", "dp", "tensor")
CHUNKS = 2
STEP = 1280
PIECES = 1
VMEM = 56 * 1024 * 1024
ADD = 52 * 1024 * 1024
SMALL = 48 * 1024 * 1024
F32 = jnp.float32
BF16 = jnp.bfloat16
LONG = pl.CostEstimate(flops=200000000000, bytes_accessed=1000, transcendentals=0)
BRIEF = pl.CostEstimate(flops=1000, bytes_accessed=1000, transcendentals=0)
ANY = pl.BlockSpec(memory_space=pl.ANY)


def params(limit=VMEM):
    return pltpu.CompilerParams(vmem_limit_bytes=limit)


def divisor(total, options):
    for option in options:
        if total % option == 0:
            return option
    return total


def product(lhs, rhs):
    return lax.dot_general(lhs, rhs, (((1,), (1,)), ((), ())), preferred_element_type=F32)


def products_kernel(active, order, count, after, formed, step, where_ref, *refs):
    parts, weight_ref, outs = refs[:count], refs[count], refs[count + 1 + after:-6]
    part_mem, grad_mem, weight_mem, out_mem, load_sem, store_sem = refs[-6:]
    rows, width = grad_mem.shape[0] * grad_mem.shape[1], grad_mem.shape[2]
    steps = width // step

    @pl.when(where_ref[1] == active)
    def _():
        part_loads = [
            pltpu.make_async_copy(part, part_mem.at[p], load_sem.at[p]) for p, part in enumerate(parts)
        ]
        height = step // PIECES
        weight_loads = [
            pltpu.make_async_copy(
                weight_ref.at[where_ref[0] ^ k, pl.ds(c * height, height)],
                weight_mem.at[b, pl.ds(c * height, height)],
                load_sem.at[count + b * steps * PIECES + c],
            )
            for b, k in enumerate(order)
            for c in range(steps * PIECES)
        ]
        for load in part_loads + weight_loads:
            load.start()
        for load in part_loads:
            load.wait()
        if formed:
            total = part_mem[0].astype(F32)
            for p in range(1, count):
                total = total + part_mem[p].astype(F32)
            grad_mem[...] = total.astype(BF16)
            source = grad_mem
        else:
            source = part_mem.at[0]
        stores = []
        if formed:
            stores.append(pltpu.make_async_copy(grad_mem, outs[0], store_sem.at[0]))
            stores[0].start()
        for b, k in enumerate(order):
            for c in range(steps):
                for load in weight_loads[(b * steps + c) * PIECES:(b * steps + c + 1) * PIECES]:
                    load.wait()
                total = product(source[...].reshape(rows, width), weight_mem[b, c * step:(c + 1) * step])
                if k == 0:
                    total = total + source[:, :, c * step:(c + 1) * step].reshape(rows, step).astype(F32)
                out_mem[b, :, c * step:(c + 1) * step] = total.astype(BF16)
            stores.append(pltpu.make_async_copy(out_mem.at[b], outs[len(stores)], store_sem.at[len(stores)]))
            stores[-1].start()
        for store in stores:
            store.wait()


def products(active, where, parts, weights, order, formed, name, cost, after=()):
    shards, width, _ = weights.shape
    shape = parts[0].shape
    tokens = shape[0] * shape[1]
    step = divisor(width, (STEP, 256, 128))
    loads = len(parts) + len(order) * (width // step) * PIECES
    block = jax.ShapeDtypeStruct((tokens, width), BF16)
    return pl.pallas_call(
        functools.partial(products_kernel, active, order, len(parts), len(after), formed, step),
        in_specs=[pl.BlockSpec(memory_space=pltpu.SMEM)] + [ANY] * (len(parts) + 1 + len(after)),
        out_specs=[ANY] * (len(order) + formed),
        out_shape=[jax.ShapeDtypeStruct(shape, BF16)] * formed + [block] * len(order),
        scratch_shapes=[
            pltpu.VMEM((len(parts), *shape), BF16),
            pltpu.VMEM(shape, BF16),
            pltpu.VMEM((len(order), width, width), BF16),
            pltpu.VMEM((len(order), tokens, width), BF16),
            pltpu.SemaphoreType.DMA((loads,)),
            pltpu.SemaphoreType.DMA((len(order) + formed,)),
        ],
        compiler_params=params(),
        cost_estimate=cost,
        name=name,
    )(where, *parts, weights, *after)


def lead_products(active, where, parts, weights, after=()):
    return products(active, where, parts, weights, (3,), 1, "lead_products", BRIEF, after)


def rest_products(active, where, grad, weights, after=()):
    return products(active, where, (grad,), weights, (2, 1, 0), 0, "rest_products", LONG, after)


def add_kernel(active, where_ref, kept_ref, received_ref, *refs):
    out_ref, kept, received, total, sem = refs[-5:]

    @pl.when(where_ref[1] == active)
    def _():
        loads = [
            pltpu.make_async_copy(kept_ref, kept, sem.at[0]),
            pltpu.make_async_copy(received_ref, received, sem.at[1]),
        ]
        for load in loads:
            load.start()
        for load in loads:
            load.wait()
        total[...] = (kept[...].astype(F32) + received[...].astype(F32)).astype(BF16)
        store = pltpu.make_async_copy(total, out_ref, sem.at[2])
        store.start()
        store.wait()


def add_received(active, where, kept, received, after=()):
    return pl.pallas_call(
        functools.partial(add_kernel, active),
        in_specs=[pl.BlockSpec(memory_space=pltpu.SMEM)] + [ANY] * (2 + len(after)),
        out_specs=ANY,
        out_shape=jax.ShapeDtypeStruct(received.shape, BF16),
        scratch_shapes=[pltpu.VMEM(received.shape, BF16)] * 3 + [pltpu.SemaphoreType.DMA((3,))],
        compiler_params=params(ADD),
        cost_estimate=BRIEF,
        name="add_received",
    )(where, kept, received, *after)


def last_kernel(active, count, after, step, where_ref, *refs):
    parts, weight_ref, outs = refs[:count], refs[count], refs[count + 1 + after:-7]
    part_mem, grad_mem, weight_mem, out_mem, own_mem, load_sem, store_sem = refs[-7:]
    shards, rows, width = grad_mem.shape
    steps = width // step

    @pl.when(where_ref[1] == active)
    def _():
        part_loads = [
            pltpu.make_async_copy(part, part_mem.at[p], load_sem.at[p]) for p, part in enumerate(parts)
        ]
        height = step // PIECES
        weight_loads = [
            pltpu.make_async_copy(
                weight_ref.at[n, pl.ds(c * height, height)],
                weight_mem.at[n, pl.ds(c * height, height)],
                load_sem.at[count + n * steps * PIECES + c],
            )
            for n in range(shards)
            for c in range(steps * PIECES)
        ]
        for load in part_loads + weight_loads:
            load.start()
        for load in part_loads:
            load.wait()
        total = part_mem[0].astype(F32)
        for p in range(1, count):
            total = total + part_mem[p].astype(F32)
        part_mem[0] = total.astype(BF16)
        stores = [pltpu.make_async_copy(part_mem.at[0], outs[0], store_sem.at[0])]
        stores[0].start()
        for k in range(shards):
            grad_mem[k] = part_mem[0, where_ref[0] ^ k]
        for n in range(shards):
            for c in range(steps):
                for load in weight_loads[(n * steps + c) * PIECES:(n * steps + c + 1) * PIECES]:
                    load.wait()
                at = slice(n * width + c * step, n * width + (c + 1) * step)
                total = product(grad_mem[...].reshape(shards * rows, width), weight_mem[n, c * step:(c + 1) * step])
                through = grad_mem[:, :, c * step:(c + 1) * step].reshape(shards * rows, step).astype(F32)
                total = total + jnp.where(where_ref[0] == n, through, 0.0)
                own_mem[:, at] = total[:rows]
                for k in range(1, shards):
                    out_mem[k - 1, :, at] = total[k * rows:(k + 1) * rows].astype(BF16)
        for k in range(1, shards):
            stores.append(pltpu.make_async_copy(out_mem.at[k - 1], outs[k], store_sem.at[k]))
        stores.append(pltpu.make_async_copy(own_mem, outs[shards], store_sem.at[shards]))
        for store in stores[1:]:
            store.start()
        for store in stores:
            store.wait()


def last_products(active, where, parts, weights, after=()):
    shards, width, _ = weights.shape
    shape = parts[0].shape
    rows = shape[1]
    step = divisor(width, (STEP, 256, 128))
    half = jax.ShapeDtypeStruct((rows, shards * width), BF16)
    return pl.pallas_call(
        functools.partial(last_kernel, active, len(parts), len(after), step),
        in_specs=[pl.BlockSpec(memory_space=pltpu.SMEM)] + [ANY] * (len(parts) + 1 + len(after)),
        out_specs=[ANY] * (shards + 1),
        out_shape=[jax.ShapeDtypeStruct(shape, BF16)]
        + [half] * (shards - 1)
        + [jax.ShapeDtypeStruct((rows, shards * width), F32)],
        scratch_shapes=[
            pltpu.VMEM((len(parts), *shape), BF16),
            pltpu.VMEM(shape, BF16),
            pltpu.VMEM(weights.shape, BF16),
            pltpu.VMEM((shards - 1, rows, shards * width), BF16),
            pltpu.VMEM((rows, shards * width), F32),
            pltpu.SemaphoreType.DMA((len(parts) + shards * (width // step) * PIECES,)),
            pltpu.SemaphoreType.DMA((shards + 1,)),
        ],
        compiler_params=params(),
        cost_estimate=BRIEF,
        name="last_products",
    )(where, *parts, weights, *after)


def place_kernel(count, where_ref, *refs):
    pieces, outs = refs[:count], refs[count:]
    rows = outs[0].shape[1]
    for i, out_ref in enumerate(outs):
        for k, piece in enumerate(pieces):
            out_ref[where_ref[0] ^ k] = piece[i * rows:(i + 1) * rows]


def place_shards(where, pieces, chunks):
    tokens, width = pieces[0].shape
    memory = pl.BlockSpec(memory_space=pltpu.VMEM)
    return pl.pallas_call(
        functools.partial(place_kernel, len(pieces)),
        in_specs=[pl.BlockSpec(memory_space=pltpu.SMEM)] + [memory] * len(pieces),
        out_specs=[memory] * chunks,
        out_shape=[jax.ShapeDtypeStruct((len(pieces), tokens // chunks, width), BF16)] * chunks,
        compiler_params=params(SMALL),
        name="place_shards",
    )(where, *pieces)


def first_kernel(where_ref, *refs):
    out_ref = refs[-1]
    for i in range((len(refs) - 2) // 3):
        own, near, far = refs[3 * i:3 * i + 3]
        rows = own.shape[0]
        total = (own[...] + near[...].astype(F32) + far[...].astype(F32)).astype(BF16)
        out_ref[i * rows:(i + 1) * rows] = jnp.where(where_ref[1] == 0, total, jnp.zeros_like(total))


def first_inputs(where, sums, tokens, model, after):
    memory = pl.BlockSpec(memory_space=pltpu.VMEM)
    terms = [term for chunk in sums for term in chunk]
    return pl.pallas_call(
        first_kernel,
        in_specs=[pl.BlockSpec(memory_space=pltpu.SMEM)] + [memory] * len(terms) + [ANY],
        out_specs=memory,
        out_shape=jax.ShapeDtypeStruct((tokens, model), BF16),
        compiler_params=params(SMALL),
        cost_estimate=BRIEF,
        name="first_inputs",
    )(where, *terms, after)


def inputs_kernel(where_ref, sums_ref, *refs):
    pieces, out_ref = refs[:-1], refs[-1]
    width = pieces[0].shape[-1]
    for k, piece in enumerate(pieces):
        columns = pl.ds(pl.multiple_of((where_ref[0] ^ k) * width, 128), width)
        out_ref[:, columns] = sums_ref[:, columns] + piece[...]


def place_inputs(where, sums, pieces):
    memory = pl.BlockSpec(memory_space=pltpu.VMEM)
    return pl.pallas_call(
        inputs_kernel,
        in_specs=[pl.BlockSpec(memory_space=pltpu.SMEM)] + [memory] * (1 + len(pieces)),
        out_specs=memory,
        out_shape=jax.ShapeDtypeStruct(sums.shape, BF16),
        compiler_params=params(SMALL),
        name="place_inputs",
    )(where, sums, *pieces)


def cut_kernel(owners, chunks, where_ref, *refs):
    held, sem = refs[-2:]
    shards = held.shape[0]
    outs = refs[-2 - shards:-2]
    rows = refs[0].shape[1]
    for o, section in enumerate(owners):
        grads = refs[o * chunks:(o + 1) * chunks]

        @pl.when(where_ref[1] == section)
        def _():
            loads = [
                pltpu.make_async_copy(grad.at[where_ref[0] ^ k], held.at[k, pl.ds(i * rows, rows)], sem.at[k, i])
                for k in range(shards)
                for i, grad in enumerate(grads)
            ]
            for load in loads:
                load.start()
            for load in loads:
                load.wait()
            stores = [pltpu.make_async_copy(held.at[k], out, sem.at[k, 0]) for k, out in enumerate(outs)]
            for store in stores:
                store.start()
            for store in stores:
                store.wait()


def cut_shards(where, owners, after):
    grads = [grad for _, chunk in owners for grad in chunk]
    chunks = len(owners[0][1])
    shards, rows, width = grads[0].shape
    tokens = rows * chunks
    return pl.pallas_call(
        functools.partial(cut_kernel, [section for section, _ in owners], chunks),
        in_specs=[pl.BlockSpec(memory_space=pltpu.SMEM)] + [ANY] * (len(grads) + len(after)),
        out_specs=[ANY] * shards,
        out_shape=[jax.ShapeDtypeStruct((tokens, width), BF16)] * shards,
        scratch_shapes=[
            pltpu.VMEM((shards, tokens, width), BF16),
            pltpu.SemaphoreType.DMA((shards, chunks)),
        ],
        compiler_params=params(SMALL),
        cost_estimate=BRIEF,
        name="cut_shards",
    )(where, *grads, *after)


def pick_kernel(owners, chunks, where_ref, *refs):
    out_ref, held, sem = refs[-3:]
    for o, section in enumerate(owners):
        grads = refs[o * chunks:(o + 1) * chunks]

        @pl.when(where_ref[1] == section)
        def _():
            loads = [pltpu.make_async_copy(grad, held.at[i], sem.at[i]) for i, grad in enumerate(grads)]
            for load in loads:
                load.start()
            for load in loads:
                load.wait()
            store = pltpu.make_async_copy(held, out_ref, sem.at[0])
            store.start()
            store.wait()


def pick(where, owners, after):
    grads = [grad for _, chunk in owners for grad in chunk]
    shape = (len(owners[0][1]), *grads[0].shape)
    return pl.pallas_call(
        functools.partial(pick_kernel, [section for section, _ in owners], shape[0]),
        in_specs=[pl.BlockSpec(memory_space=pltpu.SMEM)] + [ANY] * (len(grads) + len(after)),
        out_specs=ANY,
        out_shape=jax.ShapeDtypeStruct(shape, BF16),
        scratch_shapes=[pltpu.VMEM(shape, BF16), pltpu.SemaphoreType.DMA(shape[:1])],
        compiler_params=params(SMALL),
        cost_estimate=BRIEF,
        name="pick",
    )(where, *grads, *after)


def mark_kernel(*refs):
    refs[-1][...] = jnp.zeros_like(refs[-1])


def mark(cost, *after):
    return pl.pallas_call(
        mark_kernel,
        in_specs=[ANY] * len(after),
        out_specs=pl.BlockSpec(memory_space=pltpu.VMEM),
        out_shape=jax.ShapeDtypeStruct((8, 128), F32),
        compiler_params=params(SMALL),
        cost_estimate=cost,
        name="mark",
    )(*after)


def join_kernel(sections, count, where_ref, *refs):
    parts, out_ref, held, sem = refs[:count], refs[-3], refs[-2], refs[-1]
    rows = parts[0].shape[0]

    @pl.when((where_ref[1] >= sections[0]) & (where_ref[1] <= sections[-1]))
    def _():
        loads = [
            pltpu.make_async_copy(part, held.at[pl.ds(j * rows, rows)], sem.at[j]) for j, part in enumerate(parts)
        ]
        for load in loads:
            load.start()
        for load in loads:
            load.wait()
        store = pltpu.make_async_copy(held, out_ref, sem.at[0])
        store.start()
        store.wait()


def join(sections, where, parts, after):
    rows, width = parts[0].shape
    return pl.pallas_call(
        functools.partial(join_kernel, sections, len(parts)),
        in_specs=[pl.BlockSpec(memory_space=pltpu.SMEM)] + [ANY] * (len(parts) + 1),
        out_specs=ANY,
        out_shape=jax.ShapeDtypeStruct((rows * len(parts), width), BF16),
        scratch_shapes=[pltpu.VMEM((rows * len(parts), width), BF16), pltpu.SemaphoreType.DMA((len(parts),))],
        compiler_params=params(SMALL),
        cost_estimate=BRIEF,
        name="join",
    )(where, *parts, after)


def weight_kernel(owners, sections, shards, replicas, where_ref, *refs):
    groups, grads = refs[:len(owners) * shards], refs[len(owners) * shards:-6]
    out_ref, saved, ordered, out_mem, load_sem, store_sem = refs[-6:]
    chunks = (len(grads) - replicas + 1) // (sections + replicas - 1)
    _, rows, width = grads[0].shape
    tokens = chunks * rows
    step = out_mem.shape[1]
    steps = out_ref.shape[0] // step

    loads = []
    for k in range(shards):
        for g, owner in enumerate(owners):
            @pl.when((where_ref[1] >= owner[0]) & (where_ref[1] <= owner[-1]))
            def _():
                pltpu.make_async_copy(groups[g * shards + k], saved.at[k], load_sem.at[k]).start()

        loads.append(pltpu.make_async_copy(groups[k], saved.at[k], load_sem.at[k]))
    def grad_loads(section):
        for k in range(shards):
            for j in range(replicas):
                for i in range(chunks):
                    if j == 0:
                        grad = grads[section * chunks + i]
                    elif section == 0:
                        grad = grads[(sections + j - 1) * chunks + i]
                    else:
                        grad = grads[(sections + replicas - 1) * chunks + j - 1].at[i]
                    at = (k * replicas + j) * tokens + i * rows
                    yield pltpu.make_async_copy(
                        grad.at[where_ref[0] ^ k],
                        ordered.at[pl.ds(at, rows)],
                        load_sem.at[shards + (k * replicas + j) * chunks + i],
                    )

    for section in range(sections):
        @pl.when(where_ref[1] == section)
        def _():
            for load in grad_loads(section):
                load.start()

    loads.extend(grad_loads(0))
    for load in loads:
        load.wait()

    def store(n):
        slot = lax.rem(n, 2)
        return pltpu.make_async_copy(
            out_mem.at[slot], out_ref.at[pl.ds(pl.multiple_of(n * step, step), step)], store_sem.at[slot]
        )

    @pl.loop(0, steps)
    def _(n):
        @pl.when(n >= 2)
        def _():
            store(n - 2).wait()

        features = pl.ds(pl.multiple_of(n * step, step), step)
        out_mem[lax.rem(n, 2)] = lax.dot_general(
            saved[:, :, features].reshape(ordered.shape[0], step),
            ordered[...],
            (((0,), (0,)), ((), ())),
            preferred_element_type=F32,
        )
        store(n).start()

    for n in range(max(steps - 2, 0), steps):
        store(n).wait()


def weight_products(where, gathered, own_grads, first_peers, other_peers):
    owners = tuple(tuple(sections) for sections, _ in gathered)
    groups = [array for _, arrays in gathered for array in arrays]
    shards = len(gathered[0][1])
    tokens, features = groups[0].shape
    sections, replicas = len(own_grads), len(first_peers) + 1
    chunks, width = len(own_grads[0]), own_grads[0][0].shape[-1]
    grads = [grad for chunk in (*own_grads, *first_peers) for grad in chunk] + other_peers
    step = divisor(features, (256, 128))
    return pl.pallas_call(
        functools.partial(weight_kernel, owners, sections, shards, replicas),
        in_specs=[pl.BlockSpec(memory_space=pltpu.SMEM)] + [ANY] * (len(groups) + len(grads)),
        out_specs=ANY,
        out_shape=jax.ShapeDtypeStruct((features, width), F32),
        scratch_shapes=[
            pltpu.VMEM((shards, tokens, features), BF16),
            pltpu.VMEM((shards * tokens, width), BF16),
            pltpu.VMEM((2, step, width), F32),
            pltpu.SemaphoreType.DMA((shards + shards * replicas * chunks,)),
            pltpu.SemaphoreType.DMA((2,)),
        ],
        compiler_params=params(),
        cost_estimate=LONG,
        name="weight_products",
    )(where, *groups, *grads)


def on_device(sections, replicas, shards, saved, weight, out_grad):
    tokens, model = out_grad.shape
    width = model // shards
    chunks = CHUNKS
    rows = tokens // chunks
    section, dp, tensor = (lax.axis_index(a) for a in AXES)
    weights = weight[0].reshape(shards, width, width)
    activations = saved[0]

    def place(s, d, t):
        return (s * replicas + d) * shards + t

    def permute(value, route, active):
        pairs = []
        for s in active:
            for d in range(replicas):
                for t in range(shards):
                    to = route(s, d, t)
                    if 0 <= to[0] < sections:
                        pairs.append((place(s, d, t), place(*to)))
        return lax.ppermute(value, AXES, pairs)

    def across(k):
        return lambda s, d, t: (s, d, t ^ k)

    everyone = range(sections)
    where = jnp.stack([tensor, section]).astype(jnp.int32)

    last = sections - 1
    pieces = [lax.dynamic_slice(out_grad, (0, tensor * width), (tokens, width))]
    for k in range(1, shards):
        block = lax.dynamic_slice(out_grad, (0, (tensor ^ k) * width), (tokens, width))
        pieces.append(permute(block, across(k), [last]))
    first = place_shards(where, pieces, chunks)

    height = model // replicas
    own_rows = [lax.dynamic_slice(activations, (0, dp * height), (tokens, height))]
    for j in range(1, replicas):
        block = lax.dynamic_slice(activations, (0, lax.rem(dp + replicas - j, replicas) * height), (tokens, height))
        own_rows.append(
            permute(block, lambda s, d, t: (s, (d - j) % replicas, t), everyone)
        )

    def swap(value, active):
        return [permute(value, lambda s, d, t: (s, (d - j) % replicas, t), active) for j in range(1, replicas)]

    half = sections // 2
    low, high = range(half), range(half, sections)
    def gather(value, active):
        near, far = permute(value, across(1), active), permute(value, across(2), active)
        return [value, near, far, permute(far, across(1), active)]

    gathered, kept = [(low, gather(join(low, where, own_rows, first[0]), low))], []
    swapped = []
    due = {(0, 1): gathered[0][1][1:3], (half, 0): gathered[0][1][3:]}
    incoming = [(first[i],) for i in range(chunks)]
    ended = ()
    for r in range(sections - 1):
        active = sections - 1 - r
        grads, outgoing = [], []
        for i in range(chunks):
            before = outgoing[-1] if i else incoming[-1] if r else ()
            pinned = (*before[:2], *due.get((r, i), ()))
            grad, lead = lead_products(active, where, incoming[i], weights, ended)
            received = permute(lead, across(1), [active])
            if active == half - 1 and i == chunks - 1:
                token = permute(mark(BRIEF, grad), lambda s, d, t: (s + 1, d, t), range(half - 1, sections - 1))
                gathered.append((high, gather(join(high, where, own_rows, token), high)))
                pinned = (*pinned, token)
            keep, near, own = rest_products(active, where, grad, weights, pinned)
            sums = [
                permute(own.reshape(grad.shape), lambda s, d, t: (s - 1, d, t), [active]),
                permute(near.reshape(grad.shape), lambda s, d, t: (s - 1, d, t ^ 1), [active]),
            ]
            stop = (mark(LONG, keep, before[2]),) if i else (near,)
            part = add_received(active, where, keep, received, stop)
            sums.append(permute(part.reshape(grad.shape), lambda s, d, t: (s - 1, d, t ^ 2), [active]))
            ended = (part,)
            outgoing.append(sums)
            grads.append(grad)
        incoming = outgoing
        kept.append(grads)

    def send_back(owners, after):
        blocks = cut_shards(where, [(s, kept[sections - 1 - s]) for s in owners], after)
        return [permute(block, lambda s, d, t: (s + 1, d, t ^ k), owners) for k, block in enumerate(blocks)]

    first_products, finals, last_grads = [], [], []
    ended = (*ended, *gathered[-1][1][1:3])
    for i in range(chunks):
        grad, near, keep, lead, own = last_products(0, where, incoming[i], weights, ended)
        first_products.append((keep, permute(lead, across(1), [0])))
        finals.append([own, permute(near, across(1), [0])])
        swapped.append(swap(grad, [0]))
        if not i:
            picked = pick(where, [(s, kept[sections - 1 - s]) for s in range(1, sections)], (grad,))
            others = swap(picked, range(1, sections))
            ended = (mark(LONG, keep, *incoming[-1]),)
        last_grads.append(grad)
    kept.append(last_grads)
    ended = (keep,)
    for i, (keep, received) in enumerate(first_products):
        if i:
            ended = (mark(LONG, *ended, received, *swapped[0], *others),)
        part = add_received(0, where, keep, received, ended)
        finals[i].append(permute(part, across(2), [0]))
        ended = (part,)

    back = send_back(range(sections - 1), (part,))
    weight_grad = weight_products(where, gathered, kept[::-1], list(zip(*swapped)), others)
    own_input = place_inputs(where, first_inputs(where, finals, tokens, model, weight_grad), back)
    return (own_input[None], weight_grad[None])


def solution(mesh):
    placed = (
        P("section", ("dp", "tensor"), None),
        P("section", None, "tensor"),
        P(("dp", "tensor"), None),
    )
    sizes = [mesh.shape[a] for a in AXES]
    return jax.shard_map(
        functools.partial(on_device, *sizes),
        mesh=mesh,
        in_specs=placed,
        out_specs=(P("section", ("dp", "tensor"), None), P("section", "dp", "tensor")),
        check_vma=False,
    )
```

time: 912 us -> 328 us (0.36)
  waiting for transfers between devices: 721 us -> 111 us
  local copies, waits for them, and re-layouts: 109 us -> 22.7 us
  starting transfers between devices: 24.2 us -> 106 us
  Pallas kernels: 0 us -> 80.2 us
  matrix products: 25.7 us -> 0 us
  other arithmetic: 13.3 us -> 0.08 us
  between operations: 14.2 us -> 1.8 us
    unnamed x10 -> x0, waiting for transfers between devices: 376 us -> none
    reduce_scatter x1 -> x0, waiting for transfers between devices: 145 us -> none  [on_device(): lax.psum_scatter(lax.dot_general(gathered, kept_columns, (((0,), (0,)), (...]
    all_to_all x4 -> x0, waiting for transfers between devices: 127 us -> none  [on_device(): lax.all_to_all(gradient, 'tensor', split_axis=1, concat_axis=0, tiled=True)]
    ppermute x3 -> x48, starting transfers between devices: 7.57 us -> 106 us  [permute(): return lax.ppermute(value, AXES, pairs)]
    pallas_call x0 -> x36, Pallas kernels: none -> 80.2 us  [the longest x12 41.5 us: products(): pl.pallas_call(functools.partial(products_kernel, active, order, len(part...]
    ppermute x3 -> x48, waiting for transfers between devices: 50.2 us -> 111 us  [permute(): return lax.ppermute(value, AXES, pairs)]
    unnamed x29 -> x102, local copies, waits for them, and re-layouts: 61.3 us -> 19.5 us
    cond x4 -> x0, local copies, waits for them, and re-layouts: 31.8 us -> none  [on_device(): lax.cond(on_duty, compute, nothing, columns).astype(jnp.bfloat16)]
  transfers between devices with their start and end apart: 13 -> 48, of which waited for: 13 -> 8; matrix products, arithmetic and copies ran while one was open for 5% -> 0% of each run, Pallas kernels for 0% -> 24%
where the time goes in v2:
time: 328 us; the launch traced here: 322 us
  waiting for transfers between devices  111 us (34%)
  starting transfers between devices  106 us (32%)
  Pallas kernels  80.2 us (24%)
  local copies, waits for them, and re-layouts  22.7 us (7%)
    ppermute x48, waiting for transfers between devices, permute(): return lax.ppermute(value, AXES, pairs)  111 us
    ppermute x48, starting transfers between devices, permute(): return lax.ppermute(value, AXES, pairs)  106 us
    pallas_call x12, Pallas kernels, products(): pl.pallas_call(functools.partial(products_kernel, active, order, len(part...  41.5 us
    unnamed x102, local copies, waits for them, and re-layouts  19.5 us
    pallas_call x1, Pallas kernels, weight_products(): pl.pallas_call(functools.partial(weight_kernel, owners, sections, shards,...  14.8 us
    pallas_call x8, Pallas kernels, add_received(): pl.pallas_call(functools.partial(add_kernel, active), in_specs=[pl.BlockS...  8.55 us
  transfers between devices with their start and end apart: 48, of which 8 were waited for; matrix products, arithmetic and copies ran while one was open for 0% of the time, Pallas kernels for 24%

profile of v2, /device:TPU:5, one launch (start us, length us, event | category | flops | bytes accessed | tf_op | source)
XLA Modules:
  0.0 322.4 jit_solution(13801379417347415630)
XLA Ops:
  0.7 2.3 dynamic-slice_bitcast_fusion
  9.3 1.5 collective-permute-start.5
  10.8 8.0 %collective-permute-done.7.refs_1_ = bf16[128,2560]{1,0:T(8,128)(2,1)S(1)} collective-permute-done((bf16[128,2560]{1,0:T(8,128)(2,1)}, bf16[128,2560]{1,0:T(8,128)(2,1)S(1)}, u32[]{:S(2)}, u32[]{:S(2)}) %collective-permute-start.7) | collective-permute-done | bytes 655392 | tf_op jit(solution)/shard_map/ppermute | solution.py:543
  19.4 2.0 join.2.refs_0_
  21.4 4.2 %collective-permute-start.9 = (bf16[256,2560]{1,0:T(8,128)(2,1)}, bf16[256,2560]{1,0:T(8,128)(2,1)}, u32[]{:S(2)}, u32[]{:S(2)}) collective-permute-start(bf16[256,2560]{1,0:T(8,128)(2,1)} %join.2.refs_0_), channel_id=1, source_target_pairs={{0,2},{1,3},{2,0},{3,1},{4,6},{5,7},{6,4},{7,5},{8,10},{9,11},{10,... | collective-permute-start | bytes 3932168 | tf_op jit(solution)/shard_map/ppermute | solution.py:543
  25.6 3.2 collective-permute-start.8
  33.5 1.5 collective-permute-start.10
  35.0 1.5 collective-permute-start.6
  36.5 45.8 %collective-permute-done.9.refs_5_.refs_2_ = bf16[256,2560]{1,0:T(8,128)(2,1)} collective-permute-done((bf16[256,2560]{1,0:T(8,128)(2,1)}, bf16[256,2560]{1,0:T(8,128)(2,1)}, u32[]{:S(2)}, u32[]{:S(2)}) %collective-permute-start.9) | collective-permute-done | bytes 1310752 | tf_op jit(solution)/shard_map/ppermute | solution.py:543
  83.0 1.5 collective-permute-start.12
  84.5 1.5 collective-permute-start.11
  86.0 1.1 copy-done.18
  88.8 1.5 collective-permute-start.17
  91.1 1.5 collective-permute-start.15
  92.6 1.1 rest_products.8
  93.7 1.3 collective-permute-start.13
  95.0 1.3 collective-permute-start.14
  96.3 3.4 %collective-permute-start.21 = (bf16[256,2560]{1,0:T(8,128)(2,1)}, bf16[256,2560]{1,0:T(8,128)(2,1)}, u32[]{:S(2)}, u32[]{:S(2)}) collective-permute-start(bf16[256,2560]{1,0:T(8,128)(2,1)} %collective-permute-done.9.refs_5_.refs_2_), channel_id=1, source_target_pairs={{0,1},{1,0},{2,3},{3,2},{4,5},{5,4},{6,7},{7,6},{8,9},{9,8},{10,11... | collective-permute-start | bytes 3932168 | tf_op jit(solution)/shard_map/ppermute | solution.py:543
  101.4 1.3 collective-permute-start.16
  103.4 1.5 collective-permute-start.18
  105.0 12.6 %collective-permute-done.13.refs_2_.refs_0_ = bf16[4,64,1280]{2,1,0:T(8,128)(2,1)S(1)} collective-permute-done((bf16[4,64,1280]{2,1,0:T(8,128)(2,1)}, bf16[4,64,1280]{2,1,0:T(8,128)(2,1)S(1)}, u32[]{:S(2)}, u32[]{:S(2)}) %collective-permute-start.13) | collective-permute-done | bytes 655392 | tf_op jit(solution)/shard_map/ppermute | solution.py:543
  119.5 1.3 collective-permute-start.20
  120.8 1.3 collective-permute-start.19
  122.1 6.3 %collective-permute-done.16.refs_1_.refs_2_ = bf16[4,64,1280]{2,1,0:T(8,128)(2,1)} collective-permute-done((bf16[4,64,1280]{2,1,0:T(8,128)(2,1)}, bf16[4,64,1280]{2,1,0:T(8,128)(2,1)}, u32[]{:S(2)}, u32[]{:S(2)}) %collective-permute-start.16) | collective-permute-done | bytes 655392 | tf_op jit(solution)/shard_map/ppermute | solution.py:543
  131.1 1.3 collective-permute-start.26
  132.4 5.1 %lead_products.10 = (bf16[4,64,1280]{2,1,0:T(8,128)(2,1)}, bf16[256,1280]{1,0:T(8,128)(2,1)}) custom-call(s32[2]{0:T(128)} %copy-done.28, bf16[4,64,1280]{2,1,0:T(8,128)(2,1)} %copy-done.44, bf16[4,64,1280]{2,1,0:T(8,128)(2,1)} %copy-done.46, bf16[4,64,1280]{2,1,0:T(8,128)(2,1)} %collective-permute-done.16.refs_1_.refs_2_, bf16[4,1280,1280]{2,1,0:T(8,128)(2,1)} %bitcast.36, ...), custom_call_target="tpu_custom_call" | custom-call | flops 1000 | bytes 1000 | tf_op jit(solution)/shard_map/lead_products/pallas_call | solution.py:97
  137.5 2.1 collective-permute-start.24
  139.6 2.7 collective-permute-done.20.refs_3_.refs_1_
  142.4 6.7 %collective-permute-done.19.refs_2_.refs_0_ = bf16[4,64,1280]{2,1,0:T(8,128)(2,1)} collective-permute-done((bf16[4,64,1280]{2,1,0:T(8,128)(2,1)}, bf16[4,64,1280]{2,1,0:T(8,128)(2,1)}, u32[]{:S(2)}, u32[]{:S(2)}) %collective-permute-start.19) | collective-permute-done | bytes 655392 | tf_op jit(solution)/shard_map/ppermute | solution.py:543
  149.1 7.4 %rest_products.10 = (bf16[256,1280]{1,0:T(8,128)(2,1)}, bf16[256,1280]{1,0:T(8,128)(2,1)}, bf16[256,1280]{1,0:T(8,128)(2,1)}) custom-call(s32[2]{0:T(128)} %copy-done.28, bf16[4,64,1280]{2,1,0:T(8,128)(2,1)} %get-tuple-element.68.refs_0_.refs_10_.refs_2_, bf16[4,1280,1280]{2,1,0:T(8,128)(2,1)} %bitcast.37, ...), custom_call_target="tpu_custom_call" | custom-call | flops 199999995904 | bytes 1000 | tf_op jit(solution)/shard_map/rest_products/pallas_call | solution.py:97
  156.5 1.3 collective-permute-start.22
  157.8 1.3 collective-permute-start.23
  160.2 2.9 add_received.12.refs_4_
  163.2 5.2 %lead_products.11 = (bf16[4,64,1280]{2,1,0:T(8,128)(2,1)}, bf16[256,1280]{1,0:T(8,128)(2,1)}) custom-call(s32[2]{0:T(128)} %copy-done.28, bf16[4,64,1280]{2,1,0:T(8,128)(2,1)} %collective-permute-done.19.refs_2_.refs_0_, bf16[4,64,1280]{2,1,0:T(8,128)(2,1)} %collective-permute-done.20.refs_3_.refs_1_, bf16[4,64,1280]{2,1,0:T(8,128)(2,1)} %collective-permute-done.26.refs_2_, ...), custom_call_target="tpu_custom_call" | custom-call | flops 1000 | bytes 1000 | tf_op jit(solution)/shard_map/lead_products/pallas_call | solution.py:97
  169.4 1.3 collective-permute-start.27
  170.7 2.1 collective-permute-start.25
  172.9 7.8 %collective-permute-start.28 = (bf16[256,1280]{1,0:T(8,128)(2,1)}, bf16[256,1280]{1,0:T(8,128)(2,1)}, u32[]{:S(2)}, u32[]{:S(2)}) collective-permute-start(bf16[256,1280]{1,0:T(8,128)(2,1)} %get-tuple-element.77), channel_id=1, source_target_pairs={{8,9},{9,8},{10,11},{11,10},{12,13},{13,12},{14,15},{15,14}} | collective-permute-start | bytes 1966088 | tf_op jit(solution)/shard_map/ppermute | solution.py:543
  181.2 1.7 collective-permute-start.30
  183.0 1.8 collective-permute-start.29
  185.7 17.4 %rest_products.11 = (bf16[256,1280]{1,0:T(8,128)(2,1)}, bf16[256,1280]{1,0:T(8,128)(2,1)}, bf16[256,1280]{1,0:T(8,128)(2,1)}) custom-call(s32[2]{0:T(128)} %copy-done.28, bf16[4,64,1280]{2,1,0:T(8,128)(2,1)} %get-tuple-element.75.refs_0_.refs_1_.refs_11_.refs_3_, bf16[4,1280,1280]{2,1,0:T(8,128)(2,1)} %bitcast.39, bf16[4,64,1280]{2,1,0:T(8,128)(2,1)} %copy-done.48, ...), custom_call_target="tpu_custom_call" | custom-call | flops 199999995904 | bytes 1000 | tf_op jit(solution)/shard_map/rest_products/pallas_call | solution.py:97
  205.2 2.2 add_received.13.refs_4_
  207.5 1.3 collective-permute-start.35
  208.8 1.3 collective-permute-start.34
  210.2 1.6 collective-permute-start.33
  212.7 1.5 collective-permute-start.39
  215.3 2.0 pick.1
  217.3 1.5 collective-permute-start.32
  218.9 3.9 %collective-permute-start.40 = (bf16[2,4,64,1280]{3,2,1,0:T(8,128)(2,1)}, bf16[2,4,64,1280]{3,2,1,0:T(8,128)(2,1)}, u32[]{:S(2)}, u32[]{:S(2)}) collective-permute-start(bf16[2,4,64,1280]{3,2,1,0:T(8,128)(2,1)} %pick.1), channel_id=1, source_target_pairs={{8,12},{9,13},{10,14},{11,15},{12,8},{13,9},{14,10},{15,11},{16,20... | collective-permute-start | bytes 3932168 | tf_op jit(solution)/shard_map/ppermute | solution.py:543
  222.7 7.7 %collective-permute-done.34.refs_2_.refs_1_ = bf16[4,64,1280]{2,1,0:T(8,128)(2,1)S(1)} collective-permute-done((bf16[4,64,1280]{2,1,0:T(8,128)(2,1)}, bf16[4,64,1280]{2,1,0:T(8,128)(2,1)S(1)}, u32[]{:S(2)}, u32[]{:S(2)}) %collective-permute-start.34) | collective-permute-done | bytes 655392 | tf_op jit(solution)/shard_map/ppermute | solution.py:543
  233.8 1.5 collective-permute-start.31
  235.3 1.5 collective-permute-start.37
  237.4 1.5 collective-permute-start.43
  239.0 1.7 collective-permute-start.42
  240.7 1.5 collective-permute-start.36
  244.4 3.4 %cut_shards.1 = (bf16[128,1280]{1,0:T(8,128)(2,1)}, bf16[128,1280]{1,0:T(8,128)(2,1)}, bf16[128,1280]{1,0:T(8,128)(2,1)}, bf16[128,1280]{1,0:T(8,128)(2,1)}) custom-call(s32[2]{0:T(128)S(1)} %copy-done.39, bf16[4,64,1280]{2,1,0:T(8,128)(2,1)S(1)} %copy-done.6, bf16[4,64,1280]{2,1,0:T(8,128)(2,1)} %get-tuple-element.89.refs_9_.refs_1_, ...), custom_call_target="tpu_custom_call" | custom-call | flops 1000 | bytes 1000 | tf_op jit(solution)/shard_map/cut_shards/pallas_call | solution.py:332
  247.8 1.5 collective-permute-start.41
  249.4 24.0 %collective-permute-start.44 = (bf16[128,1280]{1,0:T(8,128)(2,1)}, bf16[128,1280]{1,0:T(8,128)(2,1)}, u32[]{:S(2)}, u32[]{:S(2)}) collective-permute-start(bf16[128,1280]{1,0:T(8,128)(2,1)} %get-tuple-element.90), channel_id=1, source_target_pairs={{0,8},{1,9},{2,10},{3,11},{4,12},{5,13},{6,14},{7,15},{8,16},{9,17... | collective-permute-start | bytes 983048 | tf_op jit(solution)/shard_map/ppermute | solution.py:543
  273.4 1.9 collective-permute-start.45
  275.3 1.9 collective-permute-start.46
  277.3 3.8 %collective-permute-start.47 = (bf16[128,1280]{1,0:T(8,128)(2,1)}, bf16[128,1280]{1,0:T(8,128)(2,1)}, u32[]{:S(2)}, u32[]{:S(2)}) collective-permute-start(bf16[128,1280]{1,0:T(8,128)(2,1)} %get-tuple-element.93), channel_id=1, source_target_pairs={{0,11},{1,10},{2,9},{3,8},{4,15},{5,14},{6,13},{7,12},{8,19},{9,18... | collective-permute-start | bytes 983048 | tf_op jit(solution)/shard_map/ppermute | solution.py:543
  281.0 14.8 %weight_products.1.refs_6_ = f32[2560,1280]{1,0:T(8,128)} custom-call(s32[2]{0:T(128)} %copy-done.28, bf16[256,2560]{1,0:T(8,128)(2,1)} %join.2.refs_0_, bf16[256,2560]{1,0:T(8,128)(2,1)} %collective-permute-done.8.refs_4_.refs_1_, bf16[256,2560]{1,0:T(8,128)(2,1)} %collective-permute-done.9.refs_5_.refs_2_, ...), custom_call_target="tpu_custom_call" | custom-call | flops 199999995904 | bytes 1000 | tf_op jit(solution)/shard_map/weight_products/pallas_call | solution.py:505
  295.9 2.6 first_inputs.1.sums_ref
  298.5 21.2 %collective-permute-done.46.refs_2_ = bf16[128,1280]{1,0:T(8,128)(2,1)} collective-permute-done((bf16[128,1280]{1,0:T(8,128)(2,1)}, bf16[128,1280]{1,0:T(8,128)(2,1)}, u32[]{:S(2)}, u32[]{:S(2)}) %collective-permute-start.46) | collective-permute-done | bytes 327712 | tf_op jit(solution)/shard_map/ppermute | solution.py:543
  319.7 2.5 place_inputs.1
  (173 shorter events, 35.3 us)
Async XLA Ops:
  3.0 15.8 %collective-permute-start.7 = (bf16[128,2560]{1,0:T(8,128)(2,1)}, bf16[128,2560]{1,0:T(8,128)(2,1)S(1)}, u32[]{:S(2)}, u32[]{:S(2)}) collective-permute-start(bf16[128,2560]{1,0:T(8,128)(2,1)} %get-tuple-element.94), channel_id=1, source_target_pairs={{0,4},{1,5},{2,6},{3,7},{4,0},{5,1},{6,2},{7,3},{8,12},{9,13},{10,... | collective-permute-start | bytes 1966088 | tf_op jit(solution)/shard_map/ppermute | solution.py:543
  3.9 2.1 collective-permute-start.2
  4.6 1.5 collective-permute-start
  5.3 0.8 collective-permute-start.1
  8.4 10.4 %copy-start.9 = (bf16[4,64,1280]{2,1,0:T(8,128)(2,1)S(1)}, bf16[4,64,1280]{2,1,0:T(8,128)(2,1)}, u32[]{:S(2)}) copy-start(bf16[4,64,1280]{2,1,0:T(8,128)(2,1)} %copy-done.8) | copy-start | bytes 1966084
  9.3 21.8 %collective-permute-start.5 = (bf16[256,1280]{1,0:T(8,128)(2,1)}, bf16[256,1280]{1,0:T(8,128)(2,1)}, u32[]{:S(2)}, u32[]{:S(2)}) collective-permute-start(bf16[256,1280]{1,0:T(8,128)(2,1)} %get-tuple-element.53), channel_id=1, source_target_pairs={{24,25},{25,24},{26,27},{27,26},{28,29},{29,28},{30,31},{31,30}} | collective-permute-start | bytes 1966088 | tf_op jit(solution)/shard_map/ppermute | solution.py:543
  21.4 60.9 %collective-permute-start.9 = (bf16[256,2560]{1,0:T(8,128)(2,1)}, bf16[256,2560]{1,0:T(8,128)(2,1)}, u32[]{:S(2)}, u32[]{:S(2)}) collective-permute-start(bf16[256,2560]{1,0:T(8,128)(2,1)} %join.2.refs_0_), channel_id=1, source_target_pairs={{0,2},{1,3},{2,0},{3,1},{4,6},{5,7},{6,4},{7,5},{8,10},{9,11},{10,... | collective-permute-start | bytes 3932168 | tf_op jit(solution)/shard_map/ppermute | solution.py:543
  25.6 56.6 %collective-permute-start.8 = (bf16[256,2560]{1,0:T(8,128)(2,1)}, bf16[256,2560]{1,0:T(8,128)(2,1)}, u32[]{:S(2)}, u32[]{:S(2)}) collective-permute-start(bf16[256,2560]{1,0:T(8,128)(2,1)} %join.2.refs_0_), channel_id=1, source_target_pairs={{0,1},{1,0},{2,3},{3,2},{4,5},{5,4},{6,7},{7,6},{8,9},{9,8},{10,11... | collective-permute-start | bytes 3932168 | tf_op jit(solution)/shard_map/ppermute | solution.py:543
  29.7 5.3 %collective-permute-start.3 = (bf16[4,64,1280]{2,1,0:T(8,128)(2,1)}, bf16[4,64,1280]{2,1,0:T(8,128)(2,1)S(1)}, u32[]{:S(2)}, u32[]{:S(2)}) collective-permute-start(bf16[4,64,1280]{2,1,0:T(8,128)(2,1)} %bitcast.54), channel_id=1, source_target_pairs={{24,16},{25,17},{26,18},{27,19},{28,20},{29,21},{30,22},{31,23}} | collective-permute-start | bytes 1966088 | tf_op jit(solution)/shard_map/ppermute | solution.py:543
  30.4 6.1 %collective-permute-start.4 = (bf16[4,64,1280]{2,1,0:T(8,128)(2,1)}, bf16[4,64,1280]{2,1,0:T(8,128)(2,1)S(1)}, u32[]{:S(2)}, u32[]{:S(2)}) collective-permute-start(bf16[4,64,1280]{2,1,0:T(8,128)(2,1)} %bitcast.46), channel_id=1, source_target_pairs={{24,17},{25,16},{26,19},{27,18},{28,21},{29,20},{30,23},{31,22}} | collective-permute-start | bytes 1966088 | tf_op jit(solution)/shard_map/ppermute | solution.py:543
  33.5 53.6 %collective-permute-start.10 = (bf16[256,1280]{1,0:T(8,128)(2,1)}, bf16[256,1280]{1,0:T(8,128)(2,1)}, u32[]{:S(2)}, u32[]{:S(2)}) collective-permute-start(bf16[256,1280]{1,0:T(8,128)(2,1)} %get-tuple-element.57), channel_id=1, source_target_pairs={{24,25},{25,24},{26,27},{27,26},{28,29},{29,28},{30,31},{31,30}} | collective-permute-start | bytes 1966088 | tf_op jit(solution)/shard_map/ppermute | solution.py:543
  35.0 47.3 %copy-start.45 = (bf16[4,64,1280]{2,1,0:T(8,128)(2,1)}, bf16[4,64,1280]{2,1,0:T(8,128)(2,1)S(1)}, u32[]{:S(2)}) copy-start(bf16[4,64,1280]{2,1,0:T(8,128)(2,1)S(1)} %collective-permute-done.3.refs_2_.refs_0_) | copy-start | bytes 1966084
  35.0 51.0 %collective-permute-start.6 = (bf16[4,64,1280]{2,1,0:T(8,128)(2,1)}, bf16[4,64,1280]{2,1,0:T(8,128)(2,1)}, u32[]{:S(2)}, u32[]{:S(2)}) collective-permute-start(bf16[4,64,1280]{2,1,0:T(8,128)(2,1)} %bitcast.5), channel_id=1, source_target_pairs={{24,18},{25,19},{26,16},{27,17},{28,22},{29,23},{30,20},{31,21}} | collective-permute-start | bytes 1966088 | tf_op jit(solution)/shard_map/ppermute | solution.py:543
  36.5 45.8 %copy-start.47 = (bf16[4,64,1280]{2,1,0:T(8,128)(2,1)}, bf16[4,64,1280]{2,1,0:T(8,128)(2,1)S(1)}, u32[]{:S(2)}) copy-start(bf16[4,64,1280]{2,1,0:T(8,128)(2,1)S(1)} %collective-permute-done.4.refs_3_.refs_1_) | copy-start | bytes 1966084
  83.0 9.6 %collective-permute-start.12 = (bf16[4,64,1280]{2,1,0:T(8,128)(2,1)}, bf16[4,64,1280]{2,1,0:T(8,128)(2,1)}, u32[]{:S(2)}, u32[]{:S(2)}) collective-permute-start(bf16[4,64,1280]{2,1,0:T(8,128)(2,1)} %bitcast.53), channel_id=1, source_target_pairs={{24,17},{25,16},{26,19},{27,18},{28,21},{29,20},{30,23},{31,22}} | collective-permute-start | bytes 1966088 | tf_op jit(solution)/shard_map/ppermute | solution.py:543
  84.5 8.1 %collective-permute-start.11 = (bf16[4,64,1280]{2,1,0:T(8,128)(2,1)}, bf16[4,64,1280]{2,1,0:T(8,128)(2,1)}, u32[]{:S(2)}, u32[]{:S(2)}) collective-permute-start(bf16[4,64,1280]{2,1,0:T(8,128)(2,1)} %bitcast.50), channel_id=1, source_target_pairs={{24,16},{25,17},{26,18},{27,19},{28,20},{29,21},{30,22},{31,23}} | collective-permute-start | bytes 1966088 | tf_op jit(solution)/shard_map/ppermute | solution.py:543
  88.8 13.9 %collective-permute-start.17 = (bf16[4,64,1280]{2,1,0:T(8,128)(2,1)}, bf16[4,64,1280]{2,1,0:T(8,128)(2,1)}, u32[]{:S(2)}, u32[]{:S(2)}) collective-permute-start(bf16[4,64,1280]{2,1,0:T(8,128)(2,1)} %bitcast.13), channel_id=1, source_target_pairs={{24,18},{25,19},{26,16},{27,17},{28,22},{29,23},{30,20},{31,21}} | collective-permute-start | bytes 1966088 | tf_op jit(solution)/shard_map/ppermute | solution.py:543
  91.1 8.6 %collective-permute-start.15 = (bf16[256,1280]{1,0:T(8,128)(2,1)}, bf16[256,1280]{1,0:T(8,128)(2,1)}, u32[]{:S(2)}, u32[]{:S(2)}) collective-permute-start(bf16[256,1280]{1,0:T(8,128)(2,1)} %get-tuple-element.64), channel_id=1, source_target_pairs={{16,17},{17,16},{18,19},{19,18},{20,21},{21,20},{22,23},{23,22}} | collective-permute-start | bytes 1966088 | tf_op jit(solution)/shard_map/ppermute | solution.py:543
  92.6 7.1 %copy-start.32 = (s32[2]{0:T(128)S(1)}, s32[2]{0:T(128)}, u32[]{:S(2)}) copy-start(s32[2]{0:T(128)} %copy-done.28) | copy-start | bytes 28
  93.7 23.9 %collective-permute-start.13 = (bf16[4,64,1280]{2,1,0:T(8,128)(2,1)}, bf16[4,64,1280]{2,1,0:T(8,128)(2,1)S(1)}, u32[]{:S(2)}, u32[]{:S(2)}) collective-permute-start(bf16[4,64,1280]{2,1,0:T(8,128)(2,1)} %bitcast.52), channel_id=1, source_target_pairs={{16,8},{17,9},{18,10},{19,11},{20,12},{21,13},{22,14},{23,15}} | collective-permute-start | bytes 1966088 | tf_op jit(solution)/shard_map/ppermute | solution.py:543
  95.0 22.6 %collective-permute-start.14 = (bf16[4,64,1280]{2,1,0:T(8,128)(2,1)}, bf16[4,64,1280]{2,1,0:T(8,128)(2,1)S(1)}, u32[]{:S(2)}, u32[]{:S(2)}) collective-permute-start(bf16[4,64,1280]{2,1,0:T(8,128)(2,1)} %bitcast.45), channel_id=1, source_target_pairs={{16,9},{17,8},{18,11},{19,10},{20,13},{21,12},{22,15},{23,14}} | collective-permute-start | bytes 1966088 | tf_op jit(solution)/shard_map/ppermute | solution.py:543
  96.3 43.3 %collective-permute-start.21 = (bf16[256,2560]{1,0:T(8,128)(2,1)}, bf16[256,2560]{1,0:T(8,128)(2,1)}, u32[]{:S(2)}, u32[]{:S(2)}) collective-permute-start(bf16[256,2560]{1,0:T(8,128)(2,1)} %collective-permute-done.9.refs_5_.refs_2_), channel_id=1, source_target_pairs={{0,1},{1,0},{2,3},{3,2},{4,5},{5,4},{6,7},{7,6},{8,9},{9,8},{10,11... | collective-permute-start | bytes 3932168 | tf_op jit(solution)/shard_map/ppermute | solution.py:543
  101.4 26.9 %collective-permute-start.16 = (bf16[4,64,1280]{2,1,0:T(8,128)(2,1)}, bf16[4,64,1280]{2,1,0:T(8,128)(2,1)}, u32[]{:S(2)}, u32[]{:S(2)}) collective-permute-start(bf16[4,64,1280]{2,1,0:T(8,128)(2,1)} %bitcast.12), channel_id=1, source_target_pairs={{16,10},{17,11},{18,8},{19,9},{20,14},{21,15},{22,12},{23,13}} | collective-permute-start | bytes 1966088 | tf_op jit(solution)/shard_map/ppermute | solution.py:543
  103.4 26.0 %collective-permute-start.18 = (bf16[256,1280]{1,0:T(8,128)(2,1)}, bf16[256,1280]{1,0:T(8,128)(2,1)}, u32[]{:S(2)}, u32[]{:S(2)}) collective-permute-start(bf16[256,1280]{1,0:T(8,128)(2,1)} %get-tuple-element.67), channel_id=1, source_target_pairs={{16,17},{17,16},{18,19},{19,18},{20,21},{21,20},{22,23},{23,22}} | collective-permute-start | bytes 1966088 | tf_op jit(solution)/shard_map/ppermute | solution.py:543
  119.5 22.9 %collective-permute-start.20 = (bf16[4,64,1280]{2,1,0:T(8,128)(2,1)}, bf16[4,64,1280]{2,1,0:T(8,128)(2,1)}, u32[]{:S(2)}, u32[]{:S(2)}) collective-permute-start(bf16[4,64,1280]{2,1,0:T(8,128)(2,1)} %bitcast.51), channel_id=1, source_target_pairs={{16,9},{17,8},{18,11},{19,10},{20,13},{21,12},{22,15},{23,14}} | collective-permute-start | bytes 1966088 | tf_op jit(solution)/shard_map/ppermute | solution.py:543
  120.8 28.3 %collective-permute-start.19 = (bf16[4,64,1280]{2,1,0:T(8,128)(2,1)}, bf16[4,64,1280]{2,1,0:T(8,128)(2,1)}, u32[]{:S(2)}, u32[]{:S(2)}) collective-permute-start(bf16[4,64,1280]{2,1,0:T(8,128)(2,1)} %bitcast.49), channel_id=1, source_target_pairs={{16,8},{17,9},{18,10},{19,11},{20,12},{21,13},{22,14},{23,15}} | collective-permute-start | bytes 1966088 | tf_op jit(solution)/shard_map/ppermute | solution.py:543
  131.1 32.1 %collective-permute-start.26 = (bf16[4,64,1280]{2,1,0:T(8,128)(2,1)}, bf16[4,64,1280]{2,1,0:T(8,128)(2,1)}, u32[]{:S(2)}, u32[]{:S(2)}) collective-permute-start(bf16[4,64,1280]{2,1,0:T(8,128)(2,1)} %bitcast.19), channel_id=1, source_target_pairs={{16,10},{17,11},{18,8},{19,9},{20,14},{21,15},{22,12},{23,13}} | collective-permute-start | bytes 1966088 | tf_op jit(solution)/shard_map/ppermute | solution.py:543
  137.5 21.6 %collective-permute-start.24 = (bf16[256,1280]{1,0:T(8,128)(2,1)}, bf16[256,1280]{1,0:T(8,128)(2,1)}, u32[]{:S(2)}, u32[]{:S(2)}) collective-permute-start(bf16[256,1280]{1,0:T(8,128)(2,1)} %get-tuple-element.74), channel_id=1, source_target_pairs={{8,9},{9,8},{10,11},{11,10},{12,13},{13,12},{14,15},{15,14}} | collective-permute-start | bytes 1966088 | tf_op jit(solution)/shard_map/ppermute | solution.py:543
  149.1 10.1 %copy-start.34 = (s32[2]{0:T(128)S(1)}, s32[2]{0:T(128)}, u32[]{:S(2)}) copy-start(s32[2]{0:T(128)} %copy-done.28) | copy-start | bytes 28
  156.5 26.5 %collective-permute-start.22 = (bf16[4,64,1280]{2,1,0:T(8,128)(2,1)}, bf16[4,64,1280]{2,1,0:T(8,128)(2,1)S(1)}, u32[]{:S(2)}, u32[]{:S(2)}) collective-permute-start(bf16[4,64,1280]{2,1,0:T(8,128)(2,1)} %bitcast.48), channel_id=1, source_target_pairs={{8,0},{9,1},{10,2},{11,3},{12,4},{13,5},{14,6},{15,7}} | collective-permute-start | bytes 1966088 | tf_op jit(solution)/shard_map/ppermute | solution.py:543
  157.8 27.0 %collective-permute-start.23 = (bf16[4,64,1280]{2,1,0:T(8,128)(2,1)}, bf16[4,64,1280]{2,1,0:T(8,128)(2,1)S(1)}, u32[]{:S(2)}, u32[]{:S(2)}) collective-permute-start(bf16[4,64,1280]{2,1,0:T(8,128)(2,1)} %bitcast.44), channel_id=1, source_target_pairs={{8,1},{9,0},{10,3},{11,2},{12,5},{13,4},{14,7},{15,6}} | collective-permute-start | bytes 1966088 | tf_op jit(solution)/shard_map/ppermute | solution.py:543
  163.1 17.5 %copy-start.35 = (s32[2]{0:T(128)S(1)}, s32[2]{0:T(128)}, u32[]{:S(2)}) copy-start(s32[2]{0:T(128)} %copy-done.28) | copy-start | bytes 28
  169.4 11.2 %collective-permute-start.27 = (f32[8,128]{1,0:T(8,128)S(1)}, f32[8,128]{1,0:T(8,128)S(1)}, u32[]{:S(2)}, u32[]{:S(2)}) collective-permute-start(f32[8,128]{1,0:T(8,128)S(1)} %mark.8), channel_id=1, source_target_pairs={{8,16},{9,17},{10,18},{11,19},{12,20},{13,21},{14,22},{15,23},{16,... | collective-permute-start | bytes 12296 | tf_op jit(solution)/shard_map/ppermute | solution.py:543
  170.7 32.3 %collective-permute-start.25 = (bf16[4,64,1280]{2,1,0:T(8,128)(2,1)}, bf16[4,64,1280]{2,1,0:T(8,128)(2,1)}, u32[]{:S(2)}, u32[]{:S(2)}) collective-permute-start(bf16[4,64,1280]{2,1,0:T(8,128)(2,1)} %bitcast.18), channel_id=1, source_target_pairs={{8,2},{9,3},{10,0},{11,1},{12,6},{13,7},{14,4},{15,5}} | collective-permute-start | bytes 1966088 | tf_op jit(solution)/shard_map/ppermute | solution.py:543
  172.9 31.3 %collective-permute-start.28 = (bf16[256,1280]{1,0:T(8,128)(2,1)}, bf16[256,1280]{1,0:T(8,128)(2,1)}, u32[]{:S(2)}, u32[]{:S(2)}) collective-permute-start(bf16[256,1280]{1,0:T(8,128)(2,1)} %get-tuple-element.77), channel_id=1, source_target_pairs={{8,9},{9,8},{10,11},{11,10},{12,13},{13,12},{14,15},{15,14}} | collective-permute-start | bytes 1966088 | tf_op jit(solution)/shard_map/ppermute | solution.py:543
  181.2 30.6 %collective-permute-start.30 = (bf16[256,2560]{1,0:T(8,128)(2,1)}, bf16[256,2560]{1,0:T(8,128)(2,1)}, u32[]{:S(2)}, u32[]{:S(2)}) collective-permute-start(bf16[256,2560]{1,0:T(8,128)(2,1)} %join.3.refs_4_), channel_id=1, source_target_pairs={{16,18},{17,19},{18,16},{19,17},{20,22},{21,23},{22,20},{23,21},{2... | collective-permute-start | bytes 3932168 | tf_op jit(solution)/shard_map/ppermute | solution.py:543
  183.0 28.9 %collective-permute-start.29 = (bf16[256,2560]{1,0:T(8,128)(2,1)}, bf16[256,2560]{1,0:T(8,128)(2,1)}, u32[]{:S(2)}, u32[]{:S(2)}) collective-permute-start(bf16[256,2560]{1,0:T(8,128)(2,1)} %join.3.refs_4_), channel_id=1, source_target_pairs={{16,17},{17,16},{18,19},{19,18},{20,21},{21,20},{22,23},{23,22},{2... | collective-permute-start | bytes 3932168 | tf_op jit(solution)/shard_map/ppermute | solution.py:543
  204.2 6.0 %copy-start.50 = (bf16[256,1280]{1,0:T(8,128)(2,1)S(1)}, bf16[256,1280]{1,0:T(8,128)(2,1)}, u32[]{:S(2)}) copy-start(bf16[256,1280]{1,0:T(8,128)(2,1)} %get-tuple-element.82) | copy-start | bytes 1966084
  207.5 4.4 %copy-start.10 = (bf16[256,1280]{1,0:T(8,128)(2,1)}, bf16[256,1280]{1,0:T(8,128)(2,1)S(1)}, u32[]{:S(2)}) copy-start(bf16[256,1280]{1,0:T(8,128)(2,1)S(1)} %add_received.13.refs_4_) | copy-start | bytes 1966084
  207.5 11.4 %collective-permute-start.35 = (bf16[4,64,1280]{2,1,0:T(8,128)(2,1)S(1)}, bf16[4,64,1280]{2,1,0:T(8,128)(2,1)S(1)}, u32[]{:S(2)}, u32[]{:S(2)}) collective-permute-start(bf16[4,64,1280]{2,1,0:T(8,128)(2,1)S(1)} %bitcast.27), channel_id=1, source_target_pairs={{8,2},{9,3},{10,0},{11,1},{12,6},{13,7},{14,4},{15,5}} | collective-permute-start | bytes 1966088 | tf_op jit(solution)/shard_map/ppermute | solution.py:543
  208.8 21.7 %collective-permute-start.34 = (bf16[4,64,1280]{2,1,0:T(8,128)(2,1)}, bf16[4,64,1280]{2,1,0:T(8,128)(2,1)S(1)}, u32[]{:S(2)}, u32[]{:S(2)}) collective-permute-start(bf16[4,64,1280]{2,1,0:T(8,128)(2,1)} %bitcast.21), channel_id=1, source_target_pairs={{8,1},{9,0},{10,3},{11,2},{12,5},{13,4},{14,7},{15,6}} | collective-permute-start | bytes 1966088 | tf_op jit(solution)/shard_map/ppermute | solution.py:543
  210.2 4.0 %copy-start.1 = (bf16[4,64,1280]{2,1,0:T(8,128)(2,1)S(1)}, bf16[4,64,1280]{2,1,0:T(8,128)(2,1)}, u32[]{:S(2)}) copy-start(bf16[4,64,1280]{2,1,0:T(8,128)(2,1)} %get-tuple-element.75.refs_0_.refs_1_.refs_11_.refs_3_) | copy-start | bytes 1966084
  210.2 4.0 %copy-start.2 = (bf16[4,64,1280]{2,1,0:T(8,128)(2,1)S(1)}, bf16[4,64,1280]{2,1,0:T(8,128)(2,1)}, u32[]{:S(2)}) copy-start(bf16[4,64,1280]{2,1,0:T(8,128)(2,1)} %get-tuple-element.58.refs_0_.refs_2_.refs_12_.refs_4_) | copy-start | bytes 1966084
  210.2 4.0 %copy-start.3 = (bf16[4,64,1280]{2,1,0:T(8,128)(2,1)S(1)}, bf16[4,64,1280]{2,1,0:T(8,128)(2,1)}, u32[]{:S(2)}) copy-start(bf16[4,64,1280]{2,1,0:T(8,128)(2,1)} %get-tuple-element.65.refs_0_.refs_3_.refs_13_.refs_5_) | copy-start | bytes 1966084
  210.2 20.3 %collective-permute-start.33 = (bf16[4,64,1280]{2,1,0:T(8,128)(2,1)S(1)}, bf16[4,64,1280]{2,1,0:T(8,128)(2,1)S(1)}, u32[]{:S(2)}, u32[]{:S(2)}) collective-permute-start(bf16[4,64,1280]{2,1,0:T(8,128)(2,1)S(1)} %bitcast.47), channel_id=1, source_target_pairs={{8,0},{9,1},{10,2},{11,3},{12,4},{13,5},{14,6},{15,7}} | collective-permute-start | bytes 1966088 | tf_op jit(solution)/shard_map/ppermute | solution.py:543
  212.7 24.8 %collective-permute-start.39 = (bf16[4,64,1280]{2,1,0:T(8,128)(2,1)}, bf16[4,64,1280]{2,1,0:T(8,128)(2,1)}, u32[]{:S(2)}, u32[]{:S(2)}) collective-permute-start(bf16[4,64,1280]{2,1,0:T(8,128)(2,1)} %get-tuple-element.88.refs_6_.refs_8_.refs_0_), channel_id=1, source_target_pairs={{0,4},{1,5},{2,6},{3,7},{4,0},{5,1},{6,2},{7,3}} | collective-permute-start | bytes 1966088 | tf_op jit(solution)/shard_map/ppermute | solution.py:543
  215.3 15.2 %copy-start.24 = (bf16[64,5120]{1,0:T(8,128)(2,1)S(1)}, bf16[64,5120]{1,0:T(8,128)(2,1)}, u32[]{:S(2)}) copy-start(bf16[64,5120]{1,0:T(8,128)(2,1)} %get-tuple-element.80.refs_0_.kept_ref) | copy-start | bytes 1966084
  217.3 18.0 %collective-permute-start.32 = (bf16[64,5120]{1,0:T(8,128)(2,1)}, bf16[64,5120]{1,0:T(8,128)(2,1)}, u32[]{:S(2)}, u32[]{:S(2)}) collective-permute-start(bf16[64,5120]{1,0:T(8,128)(2,1)} %get-tuple-element.81), channel_id=1, source_target_pairs={{0,1},{1,0},{2,3},{3,2},{4,5},{5,4},{6,7},{7,6}} | collective-permute-start | bytes 1966088 | tf_op jit(solution)/shard_map/ppermute | solution.py:543
  218.9 11.7 %copy-start.12 = (bf16[4,64,1280]{2,1,0:T(8,128)(2,1)}, bf16[4,64,1280]{2,1,0:T(8,128)(2,1)S(1)}, u32[]{:S(2)}) copy-start(bf16[4,64,1280]{2,1,0:T(8,128)(2,1)S(1)} %collective-permute-done.35.refs_3_.refs_2_) | copy-start | bytes 1966084
  218.9 21.9 %collective-permute-start.40 = (bf16[2,4,64,1280]{3,2,1,0:T(8,128)(2,1)}, bf16[2,4,64,1280]{3,2,1,0:T(8,128)(2,1)}, u32[]{:S(2)}, u32[]{:S(2)}) collective-permute-start(bf16[2,4,64,1280]{3,2,1,0:T(8,128)(2,1)} %pick.1), channel_id=1, source_target_pairs={{8,12},{9,13},{10,14},{11,15},{12,8},{13,9},{14,10},{15,11},{16,20... | collective-permute-start | bytes 3932168 | tf_op jit(solution)/shard_map/ppermute | solution.py:543
  232.2 4.7 %copy-start.38 = (s32[2]{0:T(128)S(1)}, s32[2]{0:T(128)}, u32[]{:S(2)}) copy-start(s32[2]{0:T(128)} %copy-done.28) | copy-start | bytes 28
  233.1 5.9 %collective-permute-start.38 = (bf16[64,5120]{1,0:T(8,128)(2,1)}, bf16[64,5120]{1,0:T(8,128)(2,1)S(1)}, u32[]{:S(2)}, u32[]{:S(2)}) collective-permute-start(bf16[64,5120]{1,0:T(8,128)(2,1)} %get-tuple-element.87), channel_id=1, source_target_pairs={{0,1},{1,0},{2,3},{3,2},{4,5},{5,4},{6,7},{7,6}} | collective-permute-start | bytes 1966088 | tf_op jit(solution)/shard_map/ppermute | solution.py:543
  233.8 14.0 %collective-permute-start.31 = (bf16[64,5120]{1,0:T(8,128)(2,1)}, bf16[64,5120]{1,0:T(8,128)(2,1)}, u32[]{:S(2)}, u32[]{:S(2)}) collective-permute-start(bf16[64,5120]{1,0:T(8,128)(2,1)} %get-tuple-element.79), channel_id=1, source_target_pairs={{0,1},{1,0},{2,3},{3,2},{4,5},{5,4},{6,7},{7,6}} | collective-permute-start | bytes 1966088 | tf_op jit(solution)/shard_map/ppermute | solution.py:543
  235.3 14.0 %collective-permute-start.37 = (bf16[64,5120]{1,0:T(8,128)(2,1)}, bf16[64,5120]{1,0:T(8,128)(2,1)}, u32[]{:S(2)}, u32[]{:S(2)}) collective-permute-start(bf16[64,5120]{1,0:T(8,128)(2,1)} %get-tuple-element.86), channel_id=1, source_target_pairs={{0,1},{1,0},{2,3},{3,2},{4,5},{5,4},{6,7},{7,6}} | collective-permute-start | bytes 1966088 | tf_op jit(solution)/shard_map/ppermute | solution.py:543
  237.4 35.9 %collective-permute-start.43 = (bf16[4,64,1280]{2,1,0:T(8,128)(2,1)}, bf16[4,64,1280]{2,1,0:T(8,128)(2,1)}, u32[]{:S(2)}, u32[]{:S(2)}) collective-permute-start(bf16[4,64,1280]{2,1,0:T(8,128)(2,1)} %get-tuple-element.89.refs_9_.refs_1_), channel_id=1, source_target_pairs={{0,4},{1,5},{2,6},{3,7},{4,0},{5,1},{6,2},{7,3}} | collective-permute-start | bytes 1966088 | tf_op jit(solution)/shard_map/ppermute | solution.py:543
  239.0 36.3 %collective-permute-start.42 = (bf16[256,2560]{1,0:T(8,128)(2,1)}, bf16[256,2560]{1,0:T(8,128)(2,1)}, u32[]{:S(2)}, u32[]{:S(2)}) collective-permute-start(bf16[256,2560]{1,0:T(8,128)(2,1)} %collective-permute-done.30.refs_6_), channel_id=1, source_target_pairs={{16,17},{17,16},{18,19},{19,18},{20,21},{21,20},{22,23},{23,22},{2... | collective-permute-start | bytes 3932168 | tf_op jit(solution)/shard_map/ppermute | solution.py:543
  240.7 36.5 %collective-permute-start.36 = (bf16[64,5120]{1,0:T(8,128)(2,1)}, bf16[64,5120]{1,0:T(8,128)(2,1)}, u32[]{:S(2)}, u32[]{:S(2)}) collective-permute-start(bf16[64,5120]{1,0:T(8,128)(2,1)} %add_received.14.refs_0_), channel_id=1, source_target_pairs={{0,2},{1,3},{2,0},{3,1},{4,6},{5,7},{6,4},{7,5}} | collective-permute-start | bytes 1966088 | tf_op jit(solution)/shard_map/ppermute | solution.py:543
  247.8 48.1 %collective-permute-start.41 = (bf16[64,5120]{1,0:T(8,128)(2,1)}, bf16[64,5120]{1,0:T(8,128)(2,1)}, u32[]{:S(2)}, u32[]{:S(2)}) collective-permute-start(bf16[64,5120]{1,0:T(8,128)(2,1)} %add_received.15.refs_6_), channel_id=1, source_target_pairs={{0,2},{1,3},{2,0},{3,1},{4,6},{5,7},{6,4},{7,5}} | collective-permute-start | bytes 1966088 | tf_op jit(solution)/shard_map/ppermute | solution.py:543
  249.4 49.1 %collective-permute-start.44 = (bf16[128,1280]{1,0:T(8,128)(2,1)}, bf16[128,1280]{1,0:T(8,128)(2,1)}, u32[]{:S(2)}, u32[]{:S(2)}) collective-permute-start(bf16[128,1280]{1,0:T(8,128)(2,1)} %get-tuple-element.90), channel_id=1, source_target_pairs={{0,8},{1,9},{2,10},{3,11},{4,12},{5,13},{6,14},{7,15},{8,16},{9,17... | collective-permute-start | bytes 983048 | tf_op jit(solution)/shard_map/ppermute | solution.py:543
  273.4 25.1 %collective-permute-start.45 = (bf16[128,1280]{1,0:T(8,128)(2,1)}, bf16[128,1280]{1,0:T(8,128)(2,1)}, u32[]{:S(2)}, u32[]{:S(2)}) collective-permute-start(bf16[128,1280]{1,0:T(8,128)(2,1)} %get-tuple-element.91), channel_id=1, source_target_pairs={{0,9},{1,8},{2,11},{3,10},{4,13},{5,12},{6,15},{7,14},{8,17},{9,16... | collective-permute-start | bytes 983048 | tf_op jit(solution)/shard_map/ppermute | solution.py:543
  275.3 44.4 %collective-permute-start.46 = (bf16[128,1280]{1,0:T(8,128)(2,1)}, bf16[128,1280]{1,0:T(8,128)(2,1)}, u32[]{:S(2)}, u32[]{:S(2)}) collective-permute-start(bf16[128,1280]{1,0:T(8,128)(2,1)} %get-tuple-element.92), channel_id=1, source_target_pairs={{0,10},{1,11},{2,8},{3,9},{4,14},{5,15},{6,12},{7,13},{8,18},{9,19... | collective-permute-start | bytes 983048 | tf_op jit(solution)/shard_map/ppermute | solution.py:543
  277.3 42.5 %collective-permute-start.47 = (bf16[128,1280]{1,0:T(8,128)(2,1)}, bf16[128,1280]{1,0:T(8,128)(2,1)}, u32[]{:S(2)}, u32[]{:S(2)}) collective-permute-start(bf16[128,1280]{1,0:T(8,128)(2,1)} %get-tuple-element.93), channel_id=1, source_target_pairs={{0,11},{1,10},{2,9},{3,8},{4,15},{5,14},{6,13},{7,12},{8,19},{9,18... | collective-permute-start | bytes 983048 | tf_op jit(solution)/shard_map/ppermute | solution.py:543
  281.0 14.9 %copy-start.11 = (f32[64,5120]{1,0:T(8,128)S(1)}, f32[64,5120]{1,0:T(8,128)}, u32[]{:S(2)}) copy-start(f32[64,5120]{1,0:T(8,128)} %get-tuple-element.78.refs_0_) | copy-start | bytes 3932164
  281.0 14.9 %copy-start.40 = (s32[2]{0:T(128)S(1)}, s32[2]{0:T(128)}, u32[]{:S(2)}) copy-start(s32[2]{0:T(128)} %copy-done.28) | copy-start | bytes 28
  (35 other events, 51.4 us)

commit v3 on v2

--- a/solution.py
+++ b/solution.py
@@ -9,8 +9,6 @@
 
 AXES = ("section", "dp", "tensor")
 CHUNKS = 2
-STEP = 1280
-PIECES = 1
 VMEM = 56 * 1024 * 1024
 ADD = 52 * 1024 * 1024
 SMALL = 48 * 1024 * 1024
@@ -36,26 +34,19 @@
     return lax.dot_general(lhs, rhs, (((1,), (1,)), ((), ())), preferred_element_type=F32)
 
 
-def products_kernel(active, order, count, after, formed, step, where_ref, *refs):
+def products_kernel(active, order, count, after, formed, where_ref, *refs):
     parts, weight_ref, outs = refs[:count], refs[count], refs[count + 1 + after:-6]
     part_mem, grad_mem, weight_mem, out_mem, load_sem, store_sem = refs[-6:]
     rows, width = grad_mem.shape[0] * grad_mem.shape[1], grad_mem.shape[2]
-    steps = width // step
 
     @pl.when(where_ref[1] == active)
     def _():
         part_loads = [
             pltpu.make_async_copy(part, part_mem.at[p], load_sem.at[p]) for p, part in enumerate(parts)
         ]
-        height = step // PIECES
         weight_loads = [
-            pltpu.make_async_copy(
-                weight_ref.at[where_ref[0] ^ k, pl.ds(c * height, height)],
-                weight_mem.at[b, pl.ds(c * height, height)],
-                load_sem.at[count + b * steps * PIECES + c],
-            )
+            pltpu.make_async_copy(weight_ref.at[where_ref[0] ^ k], weight_mem.at[b], load_sem.at[count + b])
             for b, k in enumerate(order)
-            for c in range(steps * PIECES)
         ]
         for load in part_loads + weight_loads:
             load.start()
@@ -73,16 +64,30 @@
         if formed:
             stores.append(pltpu.make_async_copy(grad_mem, outs[0], store_sem.at[0]))
             stores[0].start()
-        for b, k in enumerate(order):
-            for c in range(steps):
-                for load in weight_loads[(b * steps + c) * PIECES:(b * steps + c + 1) * PIECES]:
-                    load.wait()
-                total = product(source[...].reshape(rows, width), weight_mem[b, c * step:(c + 1) * step])
-                if k == 0:
-                    total = total + source[:, :, c * step:(c + 1) * step].reshape(rows, step).astype(F32)
-                out_mem[b, :, c * step:(c + 1) * step] = total.astype(BF16)
-            stores.append(pltpu.make_async_copy(out_mem.at[b], outs[len(stores)], store_sem.at[len(stores)]))
-            stores[-1].start()
+        first = len(stores)
+        blocks = [
+            pltpu.make_async_copy(out_mem.at[b], outs[first + b], store_sem.at[first + b]) for b in range(len(order))
+        ]
+
+        @pl.loop(0, len(order))
+        def _(b):
+            pltpu.make_async_copy(weight_mem.at[b], weight_mem.at[b], load_sem.at[count + b]).wait()
+            total = product(source[...].reshape(rows, width), weight_mem[b])
+
+            @pl.when(order[0] - b != 0)
+            def _():
+                out_mem[b] = total.astype(BF16)
+
+            @pl.when(order[0] - b == 0)
+            def _():
+                out_mem[b] = (total + source[...].reshape(rows, width).astype(F32)).astype(BF16)
+
+            for n, block in enumerate(blocks):
+                @pl.when(b == n)
+                def _():
+                    block.start()
+
+        stores.extend(blocks)
         for store in stores:
             store.wait()
 
@@ -91,11 +96,10 @@
     shards, width, _ = weights.shape
     shape = parts[0].shape
     tokens = shape[0] * shape[1]
-    step = divisor(width, (STEP, 256, 128))
-    loads = len(parts) + len(order) * (width // step) * PIECES
+    loads = len(parts) + len(order)
     block = jax.ShapeDtypeStruct((tokens, width), BF16)
     return pl.pallas_call(
-        functools.partial(products_kernel, active, order, len(parts), len(after), formed, step),
+        functools.partial(products_kernel, active, order, len(parts), len(after), formed),
         in_specs=[pl.BlockSpec(memory_space=pltpu.SMEM)] + [ANY] * (len(parts) + 1 + len(after)),
         out_specs=[ANY] * (len(order) + formed),
         out_shape=[jax.ShapeDtypeStruct(shape, BF16)] * formed + [block] * len(order),
@@ -153,26 +157,18 @@
     )(where, kept, received, *after)
 
 
-def last_kernel(active, count, after, step, where_ref, *refs):
+def last_kernel(active, count, after, where_ref, *refs):
     parts, weight_ref, outs = refs[:count], refs[count], refs[count + 1 + after:-7]
     part_mem, grad_mem, weight_mem, out_mem, own_mem, load_sem, store_sem = refs[-7:]
     shards, rows, width = grad_mem.shape
-    steps = width // step
 
     @pl.when(where_ref[1] == active)
     def _():
         part_loads = [
             pltpu.make_async_copy(part, part_mem.at[p], load_sem.at[p]) for p, part in enumerate(parts)
         ]
-        height = step // PIECES
         weight_loads = [
-            pltpu.make_async_copy(
-                weight_ref.at[n, pl.ds(c * height, height)],
-                weight_mem.at[n, pl.ds(c * height, height)],
-                load_sem.at[count + n * steps * PIECES + c],
-            )
-            for n in range(shards)
-            for c in range(steps * PIECES)
+            pltpu.make_async_copy(weight_ref.at[n], weight_mem.at[n], load_sem.at[count + n]) for n in range(shards)
         ]
         for load in part_loads + weight_loads:
             load.start()
@@ -186,17 +182,18 @@
         stores[0].start()
         for k in range(shards):
             grad_mem[k] = part_mem[0, where_ref[0] ^ k]
-        for n in range(shards):
-            for c in range(steps):
-                for load in weight_loads[(n * steps + c) * PIECES:(n * steps + c + 1) * PIECES]:
-                    load.wait()
-                at = slice(n * width + c * step, n * width + (c + 1) * step)
-                total = product(grad_mem[...].reshape(shards * rows, width), weight_mem[n, c * step:(c + 1) * step])
-                through = grad_mem[:, :, c * step:(c + 1) * step].reshape(shards * rows, step).astype(F32)
-                total = total + jnp.where(where_ref[0] == n, through, 0.0)
-                own_mem[:, at] = total[:rows]
-                for k in range(1, shards):
-                    out_mem[k - 1, :, at] = total[k * rows:(k + 1) * rows].astype(BF16)
+
+        @pl.loop(0, shards)
+        def _(n):
+            pltpu.make_async_copy(weight_mem.at[n], weight_mem.at[n], load_sem.at[count + n]).wait()
+            at = pl.ds(pl.multiple_of(n * width, 128), width)
+            total = product(grad_mem[...].reshape(shards * rows, width), weight_mem[n])
+            through = grad_mem[...].reshape(shards * rows, width).astype(F32)
+            total = total + jnp.where(where_ref[0] == n, through, 0.0)
+            own_mem[:, at] = total[:rows]
+            for k in range(1, shards):
+                out_mem[k - 1, :, at] = total[k * rows:(k + 1) * rows].astype(BF16)
+
         for k in range(1, shards):
             stores.append(pltpu.make_async_copy(out_mem.at[k - 1], outs[k], store_sem.at[k]))
         stores.append(pltpu.make_async_copy(own_mem, outs[shards], store_sem.at[shards]))
@@ -210,10 +207,9 @@
     shards, width, _ = weights.shape
     shape = parts[0].shape
     rows = shape[1]
-    step = divisor(width, (STEP, 256, 128))
     half = jax.ShapeDtypeStruct((rows, shards * width), BF16)
     return pl.pallas_call(
-        functools.partial(last_kernel, active, len(parts), len(after), step),
+        functools.partial(last_kernel, active, len(parts), len(after)),
         in_specs=[pl.BlockSpec(memory_space=pltpu.SMEM)] + [ANY] * (len(parts) + 1 + len(after)),
         out_specs=[ANY] * (shards + 1),
         out_shape=[jax.ShapeDtypeStruct(shape, BF16)]
@@ -225,7 +221,7 @@
             pltpu.VMEM(weights.shape, BF16),
             pltpu.VMEM((shards - 1, rows, shards * width), BF16),
             pltpu.VMEM((rows, shards * width), F32),
-            pltpu.SemaphoreType.DMA((len(parts) + shards * (width // step) * PIECES,)),
+            pltpu.SemaphoreType.DMA((len(parts) + shards,)),
             pltpu.SemaphoreType.DMA((shards + 1,)),
         ],
         compiler_params=params(),
@@ -424,10 +420,9 @@
     )(where, *parts, after)
 
 
-def weight_kernel(owners, sections, shards, replicas, where_ref, *refs):
+def weight_kernel(owners, half, sections, shards, replicas, chunks, where_ref, *refs):
     groups, grads = refs[:len(owners) * shards], refs[len(owners) * shards:-6]
     out_ref, saved, ordered, out_mem, load_sem, store_sem = refs[-6:]
-    chunks = (len(grads) - replicas + 1) // (sections + replicas - 1)
     _, rows, width = grads[0].shape
     tokens = chunks * rows
     step = out_mem.shape[1]
@@ -450,7 +445,8 @@
                     elif section == 0:
                         grad = grads[(sections + j - 1) * chunks + i]
                     else:
-                        grad = grads[(sections + replicas - 1) * chunks + j - 1].at[i]
+                        later = (replicas - 1) * (section >= half)
+                        grad = grads[(sections + replicas - 1) * chunks + later + j - 1].at[i]
                     at = (k * replicas + j) * tokens + i * rows
                     yield pltpu.make_async_copy(
                         grad.at[where_ref[0] ^ k],
@@ -493,7 +489,7 @@
         store(n).wait()
 
 
-def weight_products(where, gathered, own_grads, first_peers, other_peers):
+def weight_products(where, gathered, half, own_grads, first_peers, other_peers):
     owners = tuple(tuple(sections) for sections, _ in gathered)
     groups = [array for _, arrays in gathered for array in arrays]
     shards = len(gathered[0][1])
@@ -503,7 +499,7 @@
     grads = [grad for chunk in (*own_grads, *first_peers) for grad in chunk] + other_peers
     step = divisor(features, (256, 128))
     return pl.pallas_call(
-        functools.partial(weight_kernel, owners, sections, shards, replicas),
+        functools.partial(weight_kernel, owners, half, sections, shards, replicas, chunks),
         in_specs=[pl.BlockSpec(memory_space=pltpu.SMEM)] + [ANY] * (len(groups) + len(grads)),
         out_specs=ANY,
         out_shape=jax.ShapeDtypeStruct((features, width), F32),
@@ -515,7 +511,7 @@
             pltpu.SemaphoreType.DMA((2,)),
         ],
         compiler_params=params(),
-        cost_estimate=LONG,
+        cost_estimate=BRIEF,
         name="weight_products",
     )(where, *groups, *grads)
 
@@ -608,28 +604,30 @@
         return [permute(block, lambda s, d, t: (s + 1, d, t ^ k), owners) for k, block in enumerate(blocks)]
 
     first_products, finals, last_grads = [], [], []
-    ended = (*ended, *gathered[-1][1][1:3])
+    picked = pick(where, [(s, kept[sections - 1 - s]) for s in high], ended)
+    others = swap(picked, high)
+    ended = (*ended, *gathered[-1][1][1:3], *others)
     for i in range(chunks):
         grad, near, keep, lead, own = last_products(0, where, incoming[i], weights, ended)
         first_products.append((keep, permute(lead, across(1), [0])))
         finals.append([own, permute(near, across(1), [0])])
         swapped.append(swap(grad, [0]))
         if not i:
-            picked = pick(where, [(s, kept[sections - 1 - s]) for s in range(1, sections)], (grad,))
-            others = swap(picked, range(1, sections))
-            ended = (mark(LONG, keep, *incoming[-1]),)
+            picked = pick(where, [(s, kept[sections - 1 - s]) for s in low[1:]], (grad,))
+            others = swap(picked, low[1:]) + others
+            ended = (mark(LONG, keep, *incoming[-1], finals[0][1]),)
         last_grads.append(grad)
     kept.append(last_grads)
     ended = (keep,)
     for i, (keep, received) in enumerate(first_products):
         if i:
-            ended = (mark(LONG, *ended, received, *swapped[0], *others),)
+            ended = (mark(LONG, *ended, received, *swapped[0], *others[:replicas - 1]),)
         part = add_received(0, where, keep, received, ended)
         finals[i].append(permute(part, across(2), [0]))
         ended = (part,)
 
-    back = send_back(range(sections - 1), (part,))
-    weight_grad = weight_products(where, gathered, kept[::-1], list(zip(*swapped)), others)
+    back = send_back(range(sections - 1), (part, finals[-1][1], *swapped[-1]))
+    weight_grad = weight_products(where, gathered, half, kept[::-1], list(zip(*swapped)), others)
     own_input = place_inputs(where, first_inputs(where, finals, tokens, model, weight_grad), back)
     return (own_input[None], weight_grad[None])
 

time: 328 us -> 312 us (0.951)
  Pallas kernels: 80.2 us -> 68.4 us
  local copies, waits for them, and re-layouts: 22.7 us -> 27.1 us
  starting transfers between devices: 106 us -> 102 us
    pallas_call x12, Pallas kernels: 41.5 us -> 31 us  [products(): pl.pallas_call(functools.partial(products_kernel, active, order, len(part...]
    ppermute x48 -> x49, starting transfers between devices: 106 us -> 102 us  [permute(): return lax.ppermute(value, AXES, pairs)]
    unnamed x102 -> x116, local copies, waits for them, and re-layouts: 19.5 us -> 23.8 us
    ppermute x48 -> x49, waiting for transfers between devices: 111 us -> 108 us  [permute(): return lax.ppermute(value, AXES, pairs)]
  transfers between devices with their start and end apart: 48 -> 49, of which waited for: 8 -> 10; matrix products, arithmetic and copies ran while one was open for 0% -> 0% of each run, Pallas kernels for 24% -> 22%
where the time goes in v3:
time: 312 us; the launch traced here: 307 us
  waiting for transfers between devices  108 us (35%)
  starting transfers between devices  102 us (33%)
  Pallas kernels  68.4 us (22%)
  local copies, waits for them, and re-layouts  27.1 us (9%)
    ppermute x49, waiting for transfers between devices, permute(): return lax.ppermute(value, AXES, pairs)  108 us
    ppermute x49, starting transfers between devices, permute(): return lax.ppermute(value, AXES, pairs)  102 us
    pallas_call x12, Pallas kernels, products(): pl.pallas_call(functools.partial(products_kernel, active, order, len(part...  31 us
    unnamed x116, local copies, waits for them, and re-layouts  23.8 us
    pallas_call x1, Pallas kernels, weight_products(): pl.pallas_call(functools.partial(weight_kernel, owners, half, sections, s...  14.7 us
    pallas_call x8, Pallas kernels, add_received(): pl.pallas_call(functools.partial(add_kernel, active), in_specs=[pl.BlockS...  8.53 us
  transfers between devices with their start and end apart: 49, of which 10 were waited for; matrix products, arithmetic and copies ran while one was open for 0% of the time, Pallas kernels for 22%

profile of v3, /device:TPU:5, one launch (start us, length us, event | category | flops | bytes accessed | tf_op | source)
XLA Modules:
  0.0 306.5 jit_solution(3880736593734642068)
XLA Ops:
  0.7 2.4 dynamic-slice_bitcast_fusion
  9.3 1.5 collective-permute-start.5
  10.8 8.0 %collective-permute-done.7.refs_1_ = bf16[128,2560]{1,0:T(8,128)(2,1)S(1)} collective-permute-done((bf16[128,2560]{1,0:T(8,128)(2,1)}, bf16[128,2560]{1,0:T(8,128)(2,1)S(1)}, u32[]{:S(2)}, u32[]{:S(2)}) %collective-permute-start.7) | collective-permute-done | bytes 655392 | tf_op jit(solution)/shard_map/ppermute | solution.py:539
  19.4 2.0 join.2.refs_0_
  21.5 4.2 %collective-permute-start.9 = (bf16[256,2560]{1,0:T(8,128)(2,1)}, bf16[256,2560]{1,0:T(8,128)(2,1)}, u32[]{:S(2)}, u32[]{:S(2)}) collective-permute-start(bf16[256,2560]{1,0:T(8,128)(2,1)} %join.2.refs_0_), channel_id=1, source_target_pairs={{0,2},{1,3},{2,0},{3,1},{4,6},{5,7},{6,4},{7,5},{8,10},{9,11},{10,... | collective-permute-start | bytes 3932168 | tf_op jit(solution)/shard_map/ppermute | solution.py:539
  25.7 3.2 %collective-permute-start.8 = (bf16[256,2560]{1,0:T(8,128)(2,1)}, bf16[256,2560]{1,0:T(8,128)(2,1)}, u32[]{:S(2)}, u32[]{:S(2)}) collective-permute-start(bf16[256,2560]{1,0:T(8,128)(2,1)} %join.2.refs_0_), channel_id=1, source_target_pairs={{0,1},{1,0},{2,3},{3,2},{4,5},{5,4},{6,7},{7,6},{8,9},{9,8},{10,11... | collective-permute-start | bytes 3932168 | tf_op jit(solution)/shard_map/ppermute | solution.py:539
  33.6 1.5 collective-permute-start.10
  35.1 1.5 collective-permute-start.6
  36.5 45.8 %collective-permute-done.9.refs_5_.refs_2_ = bf16[256,2560]{1,0:T(8,128)(2,1)} collective-permute-done((bf16[256,2560]{1,0:T(8,128)(2,1)}, bf16[256,2560]{1,0:T(8,128)(2,1)}, u32[]{:S(2)}, u32[]{:S(2)}) %collective-permute-start.9) | collective-permute-done | bytes 1310752 | tf_op jit(solution)/shard_map/ppermute | solution.py:539
  83.1 1.5 collective-permute-start.12
  84.6 1.5 collective-permute-start.11
  86.1 1.1 copy-done.23
  88.9 1.6 collective-permute-start.17
  91.2 1.5 collective-permute-start.15
  93.6 1.3 collective-permute-start.13
  94.9 1.3 collective-permute-start.14
  96.2 3.4 %collective-permute-start.21 = (bf16[256,2560]{1,0:T(8,128)(2,1)}, bf16[256,2560]{1,0:T(8,128)(2,1)}, u32[]{:S(2)}, u32[]{:S(2)}) collective-permute-start(bf16[256,2560]{1,0:T(8,128)(2,1)} %collective-permute-done.9.refs_5_.refs_2_), channel_id=1, source_target_pairs={{0,1},{1,0},{2,3},{3,2},{4,5},{5,4},{6,7},{7,6},{8,9},{9,8},{10,11... | collective-permute-start | bytes 3932168 | tf_op jit(solution)/shard_map/ppermute | solution.py:539
  101.2 1.3 collective-permute-start.16
  103.3 1.6 collective-permute-start.18
  104.8 12.4 %collective-permute-done.13.refs_2_.refs_0_ = bf16[4,64,1280]{2,1,0:T(8,128)(2,1)S(1)} collective-permute-done((bf16[4,64,1280]{2,1,0:T(8,128)(2,1)}, bf16[4,64,1280]{2,1,0:T(8,128)(2,1)S(1)}, u32[]{:S(2)}, u32[]{:S(2)}) %collective-permute-start.13) | collective-permute-done | bytes 655392 | tf_op jit(solution)/shard_map/ppermute | solution.py:539
  119.1 1.3 collective-permute-start.20
  120.4 1.3 collective-permute-start.19
  121.7 6.6 %collective-permute-done.16.refs_1_.refs_2_ = bf16[4,64,1280]{2,1,0:T(8,128)(2,1)} collective-permute-done((bf16[4,64,1280]{2,1,0:T(8,128)(2,1)}, bf16[4,64,1280]{2,1,0:T(8,128)(2,1)}, u32[]{:S(2)}, u32[]{:S(2)}) %collective-permute-start.16) | collective-permute-done | bytes 655392 | tf_op jit(solution)/shard_map/ppermute | solution.py:539
  128.3 1.1 copy-done.25
  131.1 1.3 collective-permute-start.26
  132.4 5.3 %lead_products.10 = (bf16[4,64,1280]{2,1,0:T(8,128)(2,1)}, bf16[256,1280]{1,0:T(8,128)(2,1)}) custom-call(s32[2]{0:T(128)} %copy-done.33, bf16[4,64,1280]{2,1,0:T(8,128)(2,1)} %copy-done.53, bf16[4,64,1280]{2,1,0:T(8,128)(2,1)} %copy-done.55, bf16[4,64,1280]{2,1,0:T(8,128)(2,1)} %collective-permute-done.16.refs_1_.refs_2_, bf16[4,1280,1280]{2,1,0:T(8,128)(2,1)} %bitcast.36, ...), custom_call_target="tpu_custom_call" | custom-call | flops 1000 | bytes 1000 | tf_op jit(solution)/shard_map/lead_products/pallas_call | solution.py:101
  137.7 1.9 collective-permute-start.24
  139.7 2.7 collective-permute-done.20.refs_3_.refs_1_
  142.4 6.6 %collective-permute-done.19.refs_2_.refs_0_ = bf16[4,64,1280]{2,1,0:T(8,128)(2,1)} collective-permute-done((bf16[4,64,1280]{2,1,0:T(8,128)(2,1)}, bf16[4,64,1280]{2,1,0:T(8,128)(2,1)}, u32[]{:S(2)}, u32[]{:S(2)}) %collective-permute-start.19) | collective-permute-done | bytes 655392 | tf_op jit(solution)/shard_map/ppermute | solution.py:539
  149.0 7.2 %rest_products.10 = (bf16[256,1280]{1,0:T(8,128)(2,1)}, bf16[256,1280]{1,0:T(8,128)(2,1)}, bf16[256,1280]{1,0:T(8,128)(2,1)}) custom-call(s32[2]{0:T(128)} %copy-done.33, bf16[4,64,1280]{2,1,0:T(8,128)(2,1)} %get-tuple-element.68.refs_0_.refs_10_.refs_2_, bf16[4,1280,1280]{2,1,0:T(8,128)(2,1)} %bitcast.37, ...), custom_call_target="tpu_custom_call" | custom-call | flops 199999995904 | bytes 1000 | tf_op jit(solution)/shard_map/rest_products/pallas_call | solution.py:101
  156.2 1.3 collective-permute-start.22
  157.5 1.3 collective-permute-start.23
  160.0 2.9 add_received.12.refs_4_
  162.9 5.2 %lead_products.11 = (bf16[4,64,1280]{2,1,0:T(8,128)(2,1)}, bf16[256,1280]{1,0:T(8,128)(2,1)}) custom-call(s32[2]{0:T(128)} %copy-done.33, bf16[4,64,1280]{2,1,0:T(8,128)(2,1)} %collective-permute-done.19.refs_2_.refs_0_, bf16[4,64,1280]{2,1,0:T(8,128)(2,1)} %collective-permute-done.20.refs_3_.refs_1_, bf16[4,64,1280]{2,1,0:T(8,128)(2,1)} %collective-permute-done.26.refs_2_, ...), custom_call_target="tpu_custom_call" | custom-call | flops 1000 | bytes 1000 | tf_op jit(solution)/shard_map/lead_products/pallas_call | solution.py:101
  169.2 1.3 collective-permute-start.27
  170.5 2.1 collective-permute-start.25
  172.7 7.7 %collective-permute-start.28 = (bf16[256,1280]{1,0:T(8,128)(2,1)}, bf16[256,1280]{1,0:T(8,128)(2,1)}, u32[]{:S(2)}, u32[]{:S(2)}) collective-permute-start(bf16[256,1280]{1,0:T(8,128)(2,1)} %get-tuple-element.77), channel_id=1, source_target_pairs={{8,9},{9,8},{10,11},{11,10},{12,13},{13,12},{14,15},{15,14}} | collective-permute-start | bytes 1966088 | tf_op jit(solution)/shard_map/ppermute | solution.py:539
  181.0 1.8 collective-permute-start.30
  184.5 7.1 %rest_products.11 = (bf16[256,1280]{1,0:T(8,128)(2,1)}, bf16[256,1280]{1,0:T(8,128)(2,1)}, bf16[256,1280]{1,0:T(8,128)(2,1)}) custom-call(s32[2]{0:T(128)} %copy-done.33, bf16[4,64,1280]{2,1,0:T(8,128)(2,1)} %get-tuple-element.75.refs_0_.refs_1_.refs_11_.refs_3_, bf16[4,1280,1280]{2,1,0:T(8,128)(2,1)} %bitcast.39, bf16[4,64,1280]{2,1,0:T(8,128)(2,1)} %copy-done.51, ...), custom_call_target="tpu_custom_call" | custom-call | flops 199999995904 | bytes 1000 | tf_op jit(solution)/shard_map/rest_products/pallas_call | solution.py:101
  192.7 2.5 collective-permute-done.28.received_ref
  195.2 2.2 add_received.13.refs_4_
  200.6 1.3 collective-permute-start.36
  202.0 1.3 collective-permute-start.35
  203.4 1.5 collective-permute-start.34
  208.5 1.5 collective-permute-start.40
  211.1 2.0 pick.3
  213.1 1.5 collective-permute-start.33
  214.6 5.1 %collective-permute-done.35.refs_2_.refs_1_ = bf16[4,64,1280]{2,1,0:T(8,128)(2,1)S(1)} collective-permute-done((bf16[4,64,1280]{2,1,0:T(8,128)(2,1)}, bf16[4,64,1280]{2,1,0:T(8,128)(2,1)S(1)}, u32[]{:S(2)}, u32[]{:S(2)}) %collective-permute-start.35) | collective-permute-done | bytes 655392 | tf_op jit(solution)/shard_map/ppermute | solution.py:539
  219.7 3.1 %collective-permute-start.41 = (bf16[2,4,64,1280]{3,2,1,0:T(8,128)(2,1)}, bf16[2,4,64,1280]{3,2,1,0:T(8,128)(2,1)}, u32[]{:S(2)}, u32[]{:S(2)}) collective-permute-start(bf16[2,4,64,1280]{3,2,1,0:T(8,128)(2,1)} %pick.3), channel_id=1, source_target_pairs={{8,12},{9,13},{10,14},{11,15},{12,8},{13,9},{14,10},{15,11}} | collective-permute-start | bytes 3932168 | tf_op jit(solution)/shard_map/ppermute | solution.py:539
  226.8 1.8 collective-permute-start.43
  228.5 1.5 collective-permute-start.38
  230.6 1.5 collective-permute-start.37
  232.2 6.5 %collective-permute-done.41.refs_3_.refs_18_ = bf16[2,4,64,1280]{3,2,1,0:T(8,128)(2,1)} collective-permute-done((bf16[2,4,64,1280]{3,2,1,0:T(8,128)(2,1)}, bf16[2,4,64,1280]{3,2,1,0:T(8,128)(2,1)}, u32[]{:S(2)}, u32[]{:S(2)}) %collective-permute-start.41) | collective-permute-done | bytes 1310752 | tf_op jit(solution)/shard_map/ppermute | solution.py:539
  238.6 1.5 collective-permute-start.44
  242.7 1.1 copy-done.10
  243.8 2.7 cut_shards.1
  246.6 14.6 %collective-permute-start.45 = (bf16[128,1280]{1,0:T(8,128)(2,1)S(1)}, bf16[128,1280]{1,0:T(8,128)(2,1)S(1)}, u32[]{:S(2)}, u32[]{:S(2)}) collective-permute-start(bf16[128,1280]{1,0:T(8,128)(2,1)S(1)} %get-tuple-element.90), channel_id=1, source_target_pairs={{0,8},{1,9},{2,10},{3,11},{4,12},{5,13},{6,14},{7,15},{8,16},{9,17... | collective-permute-start | bytes 983048 | tf_op jit(solution)/shard_map/ppermute | solution.py:539
  261.2 3.4 %collective-permute-start.46 = (bf16[128,1280]{1,0:T(8,128)(2,1)S(1)}, bf16[128,1280]{1,0:T(8,128)(2,1)S(1)}, u32[]{:S(2)}, u32[]{:S(2)}) collective-permute-start(bf16[128,1280]{1,0:T(8,128)(2,1)S(1)} %get-tuple-element.91), channel_id=1, source_target_pairs={{0,9},{1,8},{2,11},{3,10},{4,13},{5,12},{6,15},{7,14},{8,17},{9,16... | collective-permute-start | bytes 983048 | tf_op jit(solution)/shard_map/ppermute | solution.py:539
  264.6 8.7 %collective-permute-start.47 = (bf16[128,1280]{1,0:T(8,128)(2,1)S(1)}, bf16[128,1280]{1,0:T(8,128)(2,1)S(1)}, u32[]{:S(2)}, u32[]{:S(2)}) collective-permute-start(bf16[128,1280]{1,0:T(8,128)(2,1)S(1)} %get-tuple-element.92), channel_id=1, source_target_pairs={{0,10},{1,11},{2,8},{3,9},{4,14},{5,15},{6,12},{7,13},{8,18},{9,19... | collective-permute-start | bytes 983048 | tf_op jit(solution)/shard_map/ppermute | solution.py:539
  273.3 3.2 %collective-permute-start.48 = (bf16[128,1280]{1,0:T(8,128)(2,1)S(1)}, bf16[128,1280]{1,0:T(8,128)(2,1)S(1)}, u32[]{:S(2)}, u32[]{:S(2)}) collective-permute-start(bf16[128,1280]{1,0:T(8,128)(2,1)S(1)} %get-tuple-element.93), channel_id=1, source_target_pairs={{0,11},{1,10},{2,9},{3,8},{4,15},{5,14},{6,13},{7,12},{8,19},{9,18... | collective-permute-start | bytes 983048 | tf_op jit(solution)/shard_map/ppermute | solution.py:539
  276.6 14.7 %weight_products.1.refs_6_ = f32[2560,1280]{1,0:T(8,128)} custom-call(s32[2]{0:T(128)} %copy-done.33, bf16[256,2560]{1,0:T(8,128)(2,1)} %join.2.refs_0_, bf16[256,2560]{1,0:T(8,128)(2,1)} %collective-permute-done.8.refs_4_.refs_1_, bf16[256,2560]{1,0:T(8,128)(2,1)} %collective-permute-done.9.refs_5_.refs_2_, ...), custom_call_target="tpu_custom_call" | custom-call | flops 1000 | bytes 1000 | tf_op jit(solution)/shard_map/weight_products/pallas_call | solution.py:501
  291.3 2.2 first_inputs.1.sums_ref
  293.5 11.3 %collective-permute-done.47.refs_2_ = bf16[128,1280]{1,0:T(8,128)(2,1)S(1)} collective-permute-done((bf16[128,1280]{1,0:T(8,128)(2,1)S(1)}, bf16[128,1280]{1,0:T(8,128)(2,1)S(1)}, u32[]{:S(2)}, u32[]{:S(2)}) %collective-permute-start.47) | collective-permute-done | bytes 327712 | tf_op jit(solution)/shard_map/ppermute | solution.py:539
  304.8 1.8 place_inputs.1
  (190 shorter events, 41.7 us)
Async XLA Ops:
  3.0 15.8 %collective-permute-start.7 = (bf16[128,2560]{1,0:T(8,128)(2,1)}, bf16[128,2560]{1,0:T(8,128)(2,1)S(1)}, u32[]{:S(2)}, u32[]{:S(2)}) collective-permute-start(bf16[128,2560]{1,0:T(8,128)(2,1)} %get-tuple-element.94), channel_id=1, source_target_pairs={{0,4},{1,5},{2,6},{3,7},{4,0},{5,1},{6,2},{7,3},{8,12},{9,13},{10,... | collective-permute-start | bytes 1966088 | tf_op jit(solution)/shard_map/ppermute | solution.py:539
  4.0 2.1 collective-permute-start.2
  4.6 1.5 collective-permute-start
  5.3 0.8 collective-permute-start.1
  8.5 10.4 %copy-start.13 = (bf16[4,64,1280]{2,1,0:T(8,128)(2,1)S(1)}, bf16[4,64,1280]{2,1,0:T(8,128)(2,1)}, u32[]{:S(2)}) copy-start(bf16[4,64,1280]{2,1,0:T(8,128)(2,1)} %copy-done.12) | copy-start | bytes 1966084
  9.3 21.8 %collective-permute-start.5 = (bf16[256,1280]{1,0:T(8,128)(2,1)}, bf16[256,1280]{1,0:T(8,128)(2,1)}, u32[]{:S(2)}, u32[]{:S(2)}) collective-permute-start(bf16[256,1280]{1,0:T(8,128)(2,1)} %get-tuple-element.53), channel_id=1, source_target_pairs={{24,25},{25,24},{26,27},{27,26},{28,29},{29,28},{30,31},{31,30}} | collective-permute-start | bytes 1966088 | tf_op jit(solution)/shard_map/ppermute | solution.py:539
  21.5 60.9 %collective-permute-start.9 = (bf16[256,2560]{1,0:T(8,128)(2,1)}, bf16[256,2560]{1,0:T(8,128)(2,1)}, u32[]{:S(2)}, u32[]{:S(2)}) collective-permute-start(bf16[256,2560]{1,0:T(8,128)(2,1)} %join.2.refs_0_), channel_id=1, source_target_pairs={{0,2},{1,3},{2,0},{3,1},{4,6},{5,7},{6,4},{7,5},{8,10},{9,11},{10,... | collective-permute-start | bytes 3932168 | tf_op jit(solution)/shard_map/ppermute | solution.py:539
  25.7 56.6 %collective-permute-start.8 = (bf16[256,2560]{1,0:T(8,128)(2,1)}, bf16[256,2560]{1,0:T(8,128)(2,1)}, u32[]{:S(2)}, u32[]{:S(2)}) collective-permute-start(bf16[256,2560]{1,0:T(8,128)(2,1)} %join.2.refs_0_), channel_id=1, source_target_pairs={{0,1},{1,0},{2,3},{3,2},{4,5},{5,4},{6,7},{7,6},{8,9},{9,8},{10,11... | collective-permute-start | bytes 3932168 | tf_op jit(solution)/shard_map/ppermute | solution.py:539
  29.7 5.3 %collective-permute-start.3 = (bf16[4,64,1280]{2,1,0:T(8,128)(2,1)}, bf16[4,64,1280]{2,1,0:T(8,128)(2,1)S(1)}, u32[]{:S(2)}, u32[]{:S(2)}) collective-permute-start(bf16[4,64,1280]{2,1,0:T(8,128)(2,1)} %bitcast.54), channel_id=1, source_target_pairs={{24,16},{25,17},{26,18},{27,19},{28,20},{29,21},{30,22},{31,23}} | collective-permute-start | bytes 1966088 | tf_op jit(solution)/shard_map/ppermute | solution.py:539
  30.4 6.1 %collective-permute-start.4 = (bf16[4,64,1280]{2,1,0:T(8,128)(2,1)}, bf16[4,64,1280]{2,1,0:T(8,128)(2,1)S(1)}, u32[]{:S(2)}, u32[]{:S(2)}) collective-permute-start(bf16[4,64,1280]{2,1,0:T(8,128)(2,1)} %bitcast.46), channel_id=1, source_target_pairs={{24,17},{25,16},{26,19},{27,18},{28,21},{29,20},{30,23},{31,22}} | collective-permute-start | bytes 1966088 | tf_op jit(solution)/shard_map/ppermute | solution.py:539
  33.6 53.7 %collective-permute-start.10 = (bf16[256,1280]{1,0:T(8,128)(2,1)}, bf16[256,1280]{1,0:T(8,128)(2,1)}, u32[]{:S(2)}, u32[]{:S(2)}) collective-permute-start(bf16[256,1280]{1,0:T(8,128)(2,1)} %get-tuple-element.57), channel_id=1, source_target_pairs={{24,25},{25,24},{26,27},{27,26},{28,29},{29,28},{30,31},{31,30}} | collective-permute-start | bytes 1966088 | tf_op jit(solution)/shard_map/ppermute | solution.py:539
  35.0 47.3 %copy-start.54 = (bf16[4,64,1280]{2,1,0:T(8,128)(2,1)}, bf16[4,64,1280]{2,1,0:T(8,128)(2,1)S(1)}, u32[]{:S(2)}) copy-start(bf16[4,64,1280]{2,1,0:T(8,128)(2,1)S(1)} %collective-permute-done.3.refs_2_.refs_0_) | copy-start | bytes 1966084
  35.1 51.1 %collective-permute-start.6 = (bf16[4,64,1280]{2,1,0:T(8,128)(2,1)}, bf16[4,64,1280]{2,1,0:T(8,128)(2,1)}, u32[]{:S(2)}, u32[]{:S(2)}) collective-permute-start(bf16[4,64,1280]{2,1,0:T(8,128)(2,1)} %bitcast.5), channel_id=1, source_target_pairs={{24,18},{25,19},{26,16},{27,17},{28,22},{29,23},{30,20},{31,21}} | collective-permute-start | bytes 1966088 | tf_op jit(solution)/shard_map/ppermute | solution.py:539
  36.5 45.8 %copy-start.56 = (bf16[4,64,1280]{2,1,0:T(8,128)(2,1)}, bf16[4,64,1280]{2,1,0:T(8,128)(2,1)S(1)}, u32[]{:S(2)}) copy-start(bf16[4,64,1280]{2,1,0:T(8,128)(2,1)S(1)} %collective-permute-done.4.refs_3_.refs_1_) | copy-start | bytes 1966084
  83.1 9.6 %collective-permute-start.12 = (bf16[4,64,1280]{2,1,0:T(8,128)(2,1)}, bf16[4,64,1280]{2,1,0:T(8,128)(2,1)}, u32[]{:S(2)}, u32[]{:S(2)}) collective-permute-start(bf16[4,64,1280]{2,1,0:T(8,128)(2,1)} %bitcast.53), channel_id=1, source_target_pairs={{24,17},{25,16},{26,19},{27,18},{28,21},{29,20},{30,23},{31,22}} | collective-permute-start | bytes 1966088 | tf_op jit(solution)/shard_map/ppermute | solution.py:539
  84.6 8.1 %collective-permute-start.11 = (bf16[4,64,1280]{2,1,0:T(8,128)(2,1)}, bf16[4,64,1280]{2,1,0:T(8,128)(2,1)}, u32[]{:S(2)}, u32[]{:S(2)}) collective-permute-start(bf16[4,64,1280]{2,1,0:T(8,128)(2,1)} %bitcast.50), channel_id=1, source_target_pairs={{24,16},{25,17},{26,18},{27,19},{28,20},{29,21},{30,22},{31,23}} | collective-permute-start | bytes 1966088 | tf_op jit(solution)/shard_map/ppermute | solution.py:539
  88.9 13.6 %collective-permute-start.17 = (bf16[4,64,1280]{2,1,0:T(8,128)(2,1)}, bf16[4,64,1280]{2,1,0:T(8,128)(2,1)}, u32[]{:S(2)}, u32[]{:S(2)}) collective-permute-start(bf16[4,64,1280]{2,1,0:T(8,128)(2,1)} %bitcast.13), channel_id=1, source_target_pairs={{24,18},{25,19},{26,16},{27,17},{28,22},{29,23},{30,20},{31,21}} | collective-permute-start | bytes 1966088 | tf_op jit(solution)/shard_map/ppermute | solution.py:539
  91.2 8.4 %collective-permute-start.15 = (bf16[256,1280]{1,0:T(8,128)(2,1)}, bf16[256,1280]{1,0:T(8,128)(2,1)}, u32[]{:S(2)}, u32[]{:S(2)}) collective-permute-start(bf16[256,1280]{1,0:T(8,128)(2,1)} %get-tuple-element.64), channel_id=1, source_target_pairs={{16,17},{17,16},{18,19},{19,18},{20,21},{21,20},{22,23},{23,22}} | collective-permute-start | bytes 1966088 | tf_op jit(solution)/shard_map/ppermute | solution.py:539
  92.7 6.9 %copy-start.37 = (s32[2]{0:T(128)S(1)}, s32[2]{0:T(128)}, u32[]{:S(2)}) copy-start(s32[2]{0:T(128)} %copy-done.33) | copy-start | bytes 28
  93.6 23.7 %collective-permute-start.13 = (bf16[4,64,1280]{2,1,0:T(8,128)(2,1)}, bf16[4,64,1280]{2,1,0:T(8,128)(2,1)S(1)}, u32[]{:S(2)}, u32[]{:S(2)}) collective-permute-start(bf16[4,64,1280]{2,1,0:T(8,128)(2,1)} %bitcast.52), channel_id=1, source_target_pairs={{16,8},{17,9},{18,10},{19,11},{20,12},{21,13},{22,14},{23,15}} | collective-permute-start | bytes 1966088 | tf_op jit(solution)/shard_map/ppermute | solution.py:539
  94.9 22.4 %collective-permute-start.14 = (bf16[4,64,1280]{2,1,0:T(8,128)(2,1)}, bf16[4,64,1280]{2,1,0:T(8,128)(2,1)S(1)}, u32[]{:S(2)}, u32[]{:S(2)}) collective-permute-start(bf16[4,64,1280]{2,1,0:T(8,128)(2,1)} %bitcast.45), channel_id=1, source_target_pairs={{16,9},{17,8},{18,11},{19,10},{20,13},{21,12},{22,15},{23,14}} | collective-permute-start | bytes 1966088 | tf_op jit(solution)/shard_map/ppermute | solution.py:539
  96.2 43.5 %collective-permute-start.21 = (bf16[256,2560]{1,0:T(8,128)(2,1)}, bf16[256,2560]{1,0:T(8,128)(2,1)}, u32[]{:S(2)}, u32[]{:S(2)}) collective-permute-start(bf16[256,2560]{1,0:T(8,128)(2,1)} %collective-permute-done.9.refs_5_.refs_2_), channel_id=1, source_target_pairs={{0,1},{1,0},{2,3},{3,2},{4,5},{5,4},{6,7},{7,6},{8,9},{9,8},{10,11... | collective-permute-start | bytes 3932168 | tf_op jit(solution)/shard_map/ppermute | solution.py:539
  101.2 27.1 %collective-permute-start.16 = (bf16[4,64,1280]{2,1,0:T(8,128)(2,1)}, bf16[4,64,1280]{2,1,0:T(8,128)(2,1)}, u32[]{:S(2)}, u32[]{:S(2)}) collective-permute-start(bf16[4,64,1280]{2,1,0:T(8,128)(2,1)} %bitcast.12), channel_id=1, source_target_pairs={{16,10},{17,11},{18,8},{19,9},{20,14},{21,15},{22,12},{23,13}} | collective-permute-start | bytes 1966088 | tf_op jit(solution)/shard_map/ppermute | solution.py:539
  103.3 26.1 %collective-permute-start.18 = (bf16[256,1280]{1,0:T(8,128)(2,1)}, bf16[256,1280]{1,0:T(8,128)(2,1)}, u32[]{:S(2)}, u32[]{:S(2)}) collective-permute-start(bf16[256,1280]{1,0:T(8,128)(2,1)} %get-tuple-element.67), channel_id=1, source_target_pairs={{16,17},{17,16},{18,19},{19,18},{20,21},{21,20},{22,23},{23,22}} | collective-permute-start | bytes 1966088 | tf_op jit(solution)/shard_map/ppermute | solution.py:539
  119.1 23.3 %collective-permute-start.20 = (bf16[4,64,1280]{2,1,0:T(8,128)(2,1)}, bf16[4,64,1280]{2,1,0:T(8,128)(2,1)}, u32[]{:S(2)}, u32[]{:S(2)}) collective-permute-start(bf16[4,64,1280]{2,1,0:T(8,128)(2,1)} %bitcast.51), channel_id=1, source_target_pairs={{16,9},{17,8},{18,11},{19,10},{20,13},{21,12},{22,15},{23,14}} | collective-permute-start | bytes 1966088 | tf_op jit(solution)/shard_map/ppermute | solution.py:539
  120.4 28.6 %collective-permute-start.19 = (bf16[4,64,1280]{2,1,0:T(8,128)(2,1)}, bf16[4,64,1280]{2,1,0:T(8,128)(2,1)}, u32[]{:S(2)}, u32[]{:S(2)}) collective-permute-start(bf16[4,64,1280]{2,1,0:T(8,128)(2,1)} %bitcast.49), channel_id=1, source_target_pairs={{16,8},{17,9},{18,10},{19,11},{20,12},{21,13},{22,14},{23,15}} | collective-permute-start | bytes 1966088 | tf_op jit(solution)/shard_map/ppermute | solution.py:539
  131.1 31.8 %collective-permute-start.26 = (bf16[4,64,1280]{2,1,0:T(8,128)(2,1)}, bf16[4,64,1280]{2,1,0:T(8,128)(2,1)}, u32[]{:S(2)}, u32[]{:S(2)}) collective-permute-start(bf16[4,64,1280]{2,1,0:T(8,128)(2,1)} %bitcast.19), channel_id=1, source_target_pairs={{16,10},{17,11},{18,8},{19,9},{20,14},{21,15},{22,12},{23,13}} | collective-permute-start | bytes 1966088 | tf_op jit(solution)/shard_map/ppermute | solution.py:539
  137.7 21.2 %collective-permute-start.24 = (bf16[256,1280]{1,0:T(8,128)(2,1)}, bf16[256,1280]{1,0:T(8,128)(2,1)}, u32[]{:S(2)}, u32[]{:S(2)}) collective-permute-start(bf16[256,1280]{1,0:T(8,128)(2,1)} %get-tuple-element.74), channel_id=1, source_target_pairs={{8,9},{9,8},{10,11},{11,10},{12,13},{13,12},{14,15},{15,14}} | collective-permute-start | bytes 1966088 | tf_op jit(solution)/shard_map/ppermute | solution.py:539
  149.0 9.9 %copy-start.39 = (s32[2]{0:T(128)S(1)}, s32[2]{0:T(128)}, u32[]{:S(2)}) copy-start(s32[2]{0:T(128)} %copy-done.33) | copy-start | bytes 28
  156.2 26.6 %collective-permute-start.22 = (bf16[4,64,1280]{2,1,0:T(8,128)(2,1)}, bf16[4,64,1280]{2,1,0:T(8,128)(2,1)S(1)}, u32[]{:S(2)}, u32[]{:S(2)}) collective-permute-start(bf16[4,64,1280]{2,1,0:T(8,128)(2,1)} %bitcast.48), channel_id=1, source_target_pairs={{8,0},{9,1},{10,2},{11,3},{12,4},{13,5},{14,6},{15,7}} | collective-permute-start | bytes 1966088 | tf_op jit(solution)/shard_map/ppermute | solution.py:539
  157.5 25.2 %collective-permute-start.23 = (bf16[4,64,1280]{2,1,0:T(8,128)(2,1)}, bf16[4,64,1280]{2,1,0:T(8,128)(2,1)S(1)}, u32[]{:S(2)}, u32[]{:S(2)}) collective-permute-start(bf16[4,64,1280]{2,1,0:T(8,128)(2,1)} %bitcast.44), channel_id=1, source_target_pairs={{8,1},{9,0},{10,3},{11,2},{12,5},{13,4},{14,7},{15,6}} | collective-permute-start | bytes 1966088 | tf_op jit(solution)/shard_map/ppermute | solution.py:539
  162.9 17.5 %copy-start.40 = (s32[2]{0:T(128)S(1)}, s32[2]{0:T(128)}, u32[]{:S(2)}) copy-start(s32[2]{0:T(128)} %copy-done.33) | copy-start | bytes 28
  169.2 11.1 %collective-permute-start.27 = (f32[8,128]{1,0:T(8,128)S(1)}, f32[8,128]{1,0:T(8,128)S(1)}, u32[]{:S(2)}, u32[]{:S(2)}) collective-permute-start(f32[8,128]{1,0:T(8,128)S(1)} %mark.8), channel_id=1, source_target_pairs={{8,16},{9,17},{10,18},{11,19},{12,20},{13,21},{14,22},{15,23},{16,... | collective-permute-start | bytes 12296 | tf_op jit(solution)/shard_map/ppermute | solution.py:539
  170.5 21.1 %collective-permute-start.25 = (bf16[4,64,1280]{2,1,0:T(8,128)(2,1)}, bf16[4,64,1280]{2,1,0:T(8,128)(2,1)}, u32[]{:S(2)}, u32[]{:S(2)}) collective-permute-start(bf16[4,64,1280]{2,1,0:T(8,128)(2,1)} %bitcast.18), channel_id=1, source_target_pairs={{8,2},{9,3},{10,0},{11,1},{12,6},{13,7},{14,4},{15,5}} | collective-permute-start | bytes 1966088 | tf_op jit(solution)/shard_map/ppermute | solution.py:539
  172.7 22.5 %collective-permute-start.28 = (bf16[256,1280]{1,0:T(8,128)(2,1)}, bf16[256,1280]{1,0:T(8,128)(2,1)}, u32[]{:S(2)}, u32[]{:S(2)}) collective-permute-start(bf16[256,1280]{1,0:T(8,128)(2,1)} %get-tuple-element.77), channel_id=1, source_target_pairs={{8,9},{9,8},{10,11},{11,10},{12,13},{13,12},{14,15},{15,14}} | collective-permute-start | bytes 1966088 | tf_op jit(solution)/shard_map/ppermute | solution.py:539
  181.0 22.3 %collective-permute-start.30 = (bf16[256,2560]{1,0:T(8,128)(2,1)}, bf16[256,2560]{1,0:T(8,128)(2,1)}, u32[]{:S(2)}, u32[]{:S(2)}) collective-permute-start(bf16[256,2560]{1,0:T(8,128)(2,1)} %join.3.refs_4_), channel_id=1, source_target_pairs={{16,18},{17,19},{18,16},{19,17},{20,22},{21,23},{22,20},{23,21},{2... | collective-permute-start | bytes 3932168 | tf_op jit(solution)/shard_map/ppermute | solution.py:539
  192.7 5.5 %copy-start.5 = (bf16[4,64,1280]{2,1,0:T(8,128)(2,1)S(1)}, bf16[4,64,1280]{2,1,0:T(8,128)(2,1)}, u32[]{:S(2)}) copy-start(bf16[4,64,1280]{2,1,0:T(8,128)(2,1)} %get-tuple-element.65.refs_0_.refs_1_.refs_13_.refs_5_) | copy-start | bytes 1966084
  197.4 7.4 %collective-permute-start.29 = (bf16[256,2560]{1,0:T(8,128)(2,1)}, bf16[256,2560]{1,0:T(8,128)(2,1)S(1)}, u32[]{:S(2)}, u32[]{:S(2)}) collective-permute-start(bf16[256,2560]{1,0:T(8,128)(2,1)} %join.3.refs_4_), channel_id=1, source_target_pairs={{16,17},{17,16},{18,19},{19,18},{20,21},{21,20},{22,23},{23,22},{2... | collective-permute-start | bytes 3932168 | tf_op jit(solution)/shard_map/ppermute | solution.py:539
  199.9 5.0 %collective-permute-start.31 = (bf16[2,4,64,1280]{3,2,1,0:T(8,128)(2,1)S(1)}, bf16[2,4,64,1280]{3,2,1,0:T(8,128)(2,1)S(1)}, u32[]{:S(2)}, u32[]{:S(2)}) collective-permute-start(bf16[2,4,64,1280]{3,2,1,0:T(8,128)(2,1)S(1)} %pick.2), channel_id=1, source_target_pairs={{16,20},{17,21},{18,22},{19,23},{20,16},{21,17},{22,18},{23,19},{2... | collective-permute-start | bytes 3932168 | tf_op jit(solution)/shard_map/ppermute | solution.py:539
  200.6 12.5 %collective-permute-start.36 = (bf16[4,64,1280]{2,1,0:T(8,128)(2,1)S(1)}, bf16[4,64,1280]{2,1,0:T(8,128)(2,1)S(1)}, u32[]{:S(2)}, u32[]{:S(2)}) collective-permute-start(bf16[4,64,1280]{2,1,0:T(8,128)(2,1)S(1)} %bitcast.27), channel_id=1, source_target_pairs={{8,2},{9,3},{10,0},{11,1},{12,6},{13,7},{14,4},{15,5}} | collective-permute-start | bytes 1966088 | tf_op jit(solution)/shard_map/ppermute | solution.py:539
  202.0 17.7 %collective-permute-start.35 = (bf16[4,64,1280]{2,1,0:T(8,128)(2,1)}, bf16[4,64,1280]{2,1,0:T(8,128)(2,1)S(1)}, u32[]{:S(2)}, u32[]{:S(2)}) collective-permute-start(bf16[4,64,1280]{2,1,0:T(8,128)(2,1)} %bitcast.21), channel_id=1, source_target_pairs={{8,1},{9,0},{10,3},{11,2},{12,5},{13,4},{14,7},{15,6}} | collective-permute-start | bytes 1966088 | tf_op jit(solution)/shard_map/ppermute | solution.py:539
  203.3 6.6 %copy-start.1 = (bf16[4,64,1280]{2,1,0:T(8,128)(2,1)S(1)}, bf16[4,64,1280]{2,1,0:T(8,128)(2,1)}, u32[]{:S(2)}) copy-start(bf16[4,64,1280]{2,1,0:T(8,128)(2,1)} %get-tuple-element.75.refs_0_.refs_1_.refs_11_.refs_3_) | copy-start | bytes 1966084
  203.3 6.6 %copy-start.7 = (bf16[4,64,1280]{2,1,0:T(8,128)(2,1)S(1)}, bf16[4,64,1280]{2,1,0:T(8,128)(2,1)}, u32[]{:S(2)}) copy-start(bf16[4,64,1280]{2,1,0:T(8,128)(2,1)} %get-tuple-element.68.refs_0_.refs_10_.refs_2_) | copy-start | bytes 1966084
  203.4 6.6 %copy-start.42 = (s32[2]{0:T(128)S(1)}, s32[2]{0:T(128)}, u32[]{:S(2)}) copy-start(s32[2]{0:T(128)} %copy-done.33) | copy-start | bytes 28
  203.4 19.4 %collective-permute-start.34 = (bf16[4,64,1280]{2,1,0:T(8,128)(2,1)S(1)}, bf16[4,64,1280]{2,1,0:T(8,128)(2,1)S(1)}, u32[]{:S(2)}, u32[]{:S(2)}) collective-permute-start(bf16[4,64,1280]{2,1,0:T(8,128)(2,1)S(1)} %bitcast.47), channel_id=1, source_target_pairs={{8,0},{9,1},{10,2},{11,3},{12,4},{13,5},{14,6},{15,7}} | collective-permute-start | bytes 1966088 | tf_op jit(solution)/shard_map/ppermute | solution.py:539
  207.7 15.1 %collective-permute-start.32 = (bf16[64,5120]{1,0:T(8,128)(2,1)}, bf16[64,5120]{1,0:T(8,128)(2,1)S(1)}, u32[]{:S(2)}, u32[]{:S(2)}) collective-permute-start(bf16[64,5120]{1,0:T(8,128)(2,1)} %get-tuple-element.79), channel_id=1, source_target_pairs={{0,1},{1,0},{2,3},{3,2},{4,5},{5,4},{6,7},{7,6}} | collective-permute-start | bytes 1966088 | tf_op jit(solution)/shard_map/ppermute | solution.py:539
  208.5 22.2 %collective-permute-start.40 = (bf16[4,64,1280]{2,1,0:T(8,128)(2,1)}, bf16[4,64,1280]{2,1,0:T(8,128)(2,1)}, u32[]{:S(2)}, u32[]{:S(2)}) collective-permute-start(bf16[4,64,1280]{2,1,0:T(8,128)(2,1)} %get-tuple-element.88.refs_2_.refs_8_.refs_0_), channel_id=1, source_target_pairs={{0,4},{1,5},{2,6},{3,7},{4,0},{5,1},{6,2},{7,3}} | collective-permute-start | bytes 1966088 | tf_op jit(solution)/shard_map/ppermute | solution.py:539
  211.1 11.8 %copy-start.29 = (bf16[64,5120]{1,0:T(8,128)(2,1)S(1)}, bf16[64,5120]{1,0:T(8,128)(2,1)}, u32[]{:S(2)}) copy-start(bf16[64,5120]{1,0:T(8,128)(2,1)} %get-tuple-element.80.refs_0_.kept_ref) | copy-start | bytes 1966084
  213.1 9.7 %copy-start.19 = (bf16[4,64,1280]{2,1,0:T(8,128)(2,1)}, bf16[4,64,1280]{2,1,0:T(8,128)(2,1)S(1)}, u32[]{:S(2)}) copy-start(bf16[4,64,1280]{2,1,0:T(8,128)(2,1)S(1)} %collective-permute-done.36.refs_3_.refs_2_) | copy-start | bytes 1966084
  213.1 15.4 %collective-permute-start.33 = (bf16[64,5120]{1,0:T(8,128)(2,1)}, bf16[64,5120]{1,0:T(8,128)(2,1)}, u32[]{:S(2)}, u32[]{:S(2)}) collective-permute-start(bf16[64,5120]{1,0:T(8,128)(2,1)} %get-tuple-element.81), channel_id=1, source_target_pairs={{0,1},{1,0},{2,3},{3,2},{4,5},{5,4},{6,7},{7,6}} | collective-permute-start | bytes 1966088 | tf_op jit(solution)/shard_map/ppermute | solution.py:539
  219.7 19.0 %collective-permute-start.41 = (bf16[2,4,64,1280]{3,2,1,0:T(8,128)(2,1)}, bf16[2,4,64,1280]{3,2,1,0:T(8,128)(2,1)}, u32[]{:S(2)}, u32[]{:S(2)}) collective-permute-start(bf16[2,4,64,1280]{3,2,1,0:T(8,128)(2,1)} %pick.3), channel_id=1, source_target_pairs={{8,12},{9,13},{10,14},{11,15},{12,8},{13,9},{14,10},{15,11}} | collective-permute-start | bytes 3932168 | tf_op jit(solution)/shard_map/ppermute | solution.py:539
  226.1 14.1 %collective-permute-start.39 = (bf16[64,5120]{1,0:T(8,128)(2,1)}, bf16[64,5120]{1,0:T(8,128)(2,1)S(1)}, u32[]{:S(2)}, u32[]{:S(2)}) collective-permute-start(bf16[64,5120]{1,0:T(8,128)(2,1)} %get-tuple-element.87), channel_id=1, source_target_pairs={{0,1},{1,0},{2,3},{3,2},{4,5},{5,4},{6,7},{7,6}} | collective-permute-start | bytes 1966088 | tf_op jit(solution)/shard_map/ppermute | solution.py:539
  226.8 37.8 %collective-permute-start.43 = (bf16[256,2560]{1,0:T(8,128)(2,1)}, bf16[256,2560]{1,0:T(8,128)(2,1)}, u32[]{:S(2)}, u32[]{:S(2)}) collective-permute-start(bf16[256,2560]{1,0:T(8,128)(2,1)} %collective-permute-done.30.refs_6_), channel_id=1, source_target_pairs={{16,17},{17,16},{18,19},{19,18},{20,21},{21,20},{22,23},{23,22},{2... | collective-permute-start | bytes 3932168 | tf_op jit(solution)/shard_map/ppermute | solution.py:539
  228.5 14.0 %collective-permute-start.38 = (bf16[64,5120]{1,0:T(8,128)(2,1)}, bf16[64,5120]{1,0:T(8,128)(2,1)}, u32[]{:S(2)}, u32[]{:S(2)}) collective-permute-start(bf16[64,5120]{1,0:T(8,128)(2,1)} %get-tuple-element.86), channel_id=1, source_target_pairs={{0,1},{1,0},{2,3},{3,2},{4,5},{5,4},{6,7},{7,6}} | collective-permute-start | bytes 1966088 | tf_op jit(solution)/shard_map/ppermute | solution.py:539
  230.6 42.6 %collective-permute-start.37 = (bf16[64,5120]{1,0:T(8,128)(2,1)}, bf16[64,5120]{1,0:T(8,128)(2,1)}, u32[]{:S(2)}, u32[]{:S(2)}) collective-permute-start(bf16[64,5120]{1,0:T(8,128)(2,1)} %add_received.14.refs_0_), channel_id=1, source_target_pairs={{0,2},{1,3},{2,0},{3,1},{4,6},{5,7},{6,4},{7,5}} | collective-permute-start | bytes 1966088 | tf_op jit(solution)/shard_map/ppermute | solution.py:539
  238.6 3.9 %collective-permute-start.44 = (bf16[4,64,1280]{2,1,0:T(8,128)(2,1)}, bf16[4,64,1280]{2,1,0:T(8,128)(2,1)}, u32[]{:S(2)}, u32[]{:S(2)}) collective-permute-start(bf16[4,64,1280]{2,1,0:T(8,128)(2,1)} %get-tuple-element.89.refs_9_.refs_1_), channel_id=1, source_target_pairs={{0,4},{1,5},{2,6},{3,7},{4,0},{5,1},{6,2},{7,3}} | collective-permute-start | bytes 1966088 | tf_op jit(solution)/shard_map/ppermute | solution.py:539
  241.9 49.4 %collective-permute-start.42 = (bf16[64,5120]{1,0:T(8,128)(2,1)S(1)}, bf16[64,5120]{1,0:T(8,128)(2,1)S(1)}, u32[]{:S(2)}, u32[]{:S(2)}) collective-permute-start(bf16[64,5120]{1,0:T(8,128)(2,1)S(1)} %add_received.15.refs_6_), channel_id=1, source_target_pairs={{0,2},{1,3},{2,0},{3,1},{4,6},{5,7},{6,4},{7,5}} | collective-permute-start | bytes 1966088 | tf_op jit(solution)/shard_map/ppermute | solution.py:539
  246.6 46.9 %collective-permute-start.45 = (bf16[128,1280]{1,0:T(8,128)(2,1)S(1)}, bf16[128,1280]{1,0:T(8,128)(2,1)S(1)}, u32[]{:S(2)}, u32[]{:S(2)}) collective-permute-start(bf16[128,1280]{1,0:T(8,128)(2,1)S(1)} %get-tuple-element.90), channel_id=1, source_target_pairs={{0,8},{1,9},{2,10},{3,11},{4,12},{5,13},{6,14},{7,15},{8,16},{9,17... | collective-permute-start | bytes 983048 | tf_op jit(solution)/shard_map/ppermute | solution.py:539
  261.2 32.3 %collective-permute-start.46 = (bf16[128,1280]{1,0:T(8,128)(2,1)S(1)}, bf16[128,1280]{1,0:T(8,128)(2,1)S(1)}, u32[]{:S(2)}, u32[]{:S(2)}) collective-permute-start(bf16[128,1280]{1,0:T(8,128)(2,1)S(1)} %get-tuple-element.91), channel_id=1, source_target_pairs={{0,9},{1,8},{2,11},{3,10},{4,13},{5,12},{6,15},{7,14},{8,17},{9,16... | collective-permute-start | bytes 983048 | tf_op jit(solution)/shard_map/ppermute | solution.py:539
  264.6 40.2 %collective-permute-start.47 = (bf16[128,1280]{1,0:T(8,128)(2,1)S(1)}, bf16[128,1280]{1,0:T(8,128)(2,1)S(1)}, u32[]{:S(2)}, u32[]{:S(2)}) collective-permute-start(bf16[128,1280]{1,0:T(8,128)(2,1)S(1)} %get-tuple-element.92), channel_id=1, source_target_pairs={{0,10},{1,11},{2,8},{3,9},{4,14},{5,15},{6,12},{7,13},{8,18},{9,19... | collective-permute-start | bytes 983048 | tf_op jit(solution)/shard_map/ppermute | solution.py:539
  273.3 18.0 %copy-start.16 = (f32[64,5120]{1,0:T(8,128)S(1)}, f32[64,5120]{1,0:T(8,128)}, u32[]{:S(2)}) copy-start(f32[64,5120]{1,0:T(8,128)} %get-tuple-element.78.refs_0_) | copy-start | bytes 3932164
  273.3 18.0 %copy-start.18 = (bf16[64,5120]{1,0:T(8,128)(2,1)S(1)}, bf16[64,5120]{1,0:T(8,128)(2,1)}, u32[]{:S(2)}) copy-start(bf16[64,5120]{1,0:T(8,128)(2,1)} %copy-done.17) | copy-start | bytes 1966084
  273.3 18.0 %copy-start.45 = (s32[2]{0:T(128)S(1)}, s32[2]{0:T(128)}, u32[]{:S(2)}) copy-start(s32[2]{0:T(128)} %copy-done.33) | copy-start | bytes 28
  273.3 31.4 %collective-permute-start.48 = (bf16[128,1280]{1,0:T(8,128)(2,1)S(1)}, bf16[128,1280]{1,0:T(8,128)(2,1)S(1)}, u32[]{:S(2)}, u32[]{:S(2)}) collective-permute-start(bf16[128,1280]{1,0:T(8,128)(2,1)S(1)} %get-tuple-element.93), channel_id=1, source_target_pairs={{0,11},{1,10},{2,9},{3,8},{4,15},{5,14},{6,13},{7,12},{8,19},{9,18... | collective-permute-start | bytes 983048 | tf_op jit(solution)/shard_map/ppermute | solution.py:539
  (43 other events, 70.8 us)

commit v4 on v3

--- a/solution.py
+++ b/solution.py
@@ -10,8 +10,8 @@
 AXES = ("section", "dp", "tensor")
 CHUNKS = 2
 VMEM = 56 * 1024 * 1024
-ADD = 52 * 1024 * 1024
-SMALL = 48 * 1024 * 1024
+ADD = 56 * 1024 * 1024
+SMALL = 56 * 1024 * 1024
 F32 = jnp.float32
 BF16 = jnp.bfloat16
 LONG = pl.CostEstimate(flops=200000000000, bytes_accessed=1000, transcendentals=0)
@@ -578,7 +578,8 @@
         grads, outgoing = [], []
         for i in range(chunks):
             before = outgoing[-1] if i else incoming[-1] if r else ()
-            pinned = (*before[:2], *due.get((r, i), ()))
+            turn = i and active == half - 1
+            pinned = (*(before if turn else before[:2]), *due.get((r, i), ()))
             grad, lead = lead_products(active, where, incoming[i], weights, ended)
             received = permute(lead, across(1), [active])
             if active == half - 1 and i == chunks - 1:
@@ -590,7 +591,7 @@
                 permute(own.reshape(grad.shape), lambda s, d, t: (s - 1, d, t), [active]),
                 permute(near.reshape(grad.shape), lambda s, d, t: (s - 1, d, t ^ 1), [active]),
             ]
-            stop = (mark(LONG, keep, before[2]),) if i else (near,)
+            stop = (mark(LONG, keep, before[2]),) if i and not turn else (near,)
             part = add_received(active, where, keep, received, stop)
             sums.append(permute(part.reshape(grad.shape), lambda s, d, t: (s - 1, d, t ^ 2), [active]))
             ended = (part,)
@@ -615,13 +616,13 @@
         if not i:
             picked = pick(where, [(s, kept[sections - 1 - s]) for s in low[1:]], (grad,))
             others = swap(picked, low[1:]) + others
-            ended = (mark(LONG, keep, *incoming[-1], finals[0][1]),)
+            ended = (mark(LONG, keep, *incoming[-1]),)
         last_grads.append(grad)
     kept.append(last_grads)
     ended = (keep,)
     for i, (keep, received) in enumerate(first_products):
         if i:
-            ended = (mark(LONG, *ended, received, *swapped[0], *others[:replicas - 1]),)
+            ended = (mark(LONG, *ended, received, finals[0][1], *swapped[0], *others[:replicas - 1]),)
         part = add_received(0, where, keep, received, ended)
         finals[i].append(permute(part, across(2), [0]))
         ended = (part,)

time: 312 us -> 306 us (0.981)
  local copies, waits for them, and re-layouts: 27.1 us -> 13.8 us
  Pallas kernels: 68.4 us -> 80 us
  waiting for transfers between devices: 108 us -> 96.9 us
  starting transfers between devices: 102 us -> 109 us
    unnamed x116 -> x58, local copies, waits for them, and re-layouts: 23.8 us -> 10.5 us
    ppermute x49, waiting for transfers between devices: 108 us -> 96.9 us  [permute(): return lax.ppermute(value, AXES, pairs)]
    ppermute x49, starting transfers between devices: 102 us -> 109 us  [permute(): return lax.ppermute(value, AXES, pairs)]
  transfers between devices with their start and end apart: 49 -> 49, of which waited for: 10 -> 10; matrix products, arithmetic and copies ran while one was open for 0% -> 1% of each run, Pallas kernels for 22% -> 26%
where the time goes in v4:
time: 306 us; the launch traced here: 302 us
  starting transfers between devices  109 us (36%)
  waiting for transfers between devices  96.9 us (32%)
  Pallas kernels  80 us (26%)
  local copies, waits for them, and re-layouts  13.8 us (5%)
    ppermute x49, starting transfers between devices, permute(): return lax.ppermute(value, AXES, pairs)  109 us
    ppermute x49, waiting for transfers between devices, permute(): return lax.ppermute(value, AXES, pairs)  96.9 us
    pallas_call x12, Pallas kernels, products(): pl.pallas_call(functools.partial(products_kernel, active, order, len(part...  30.4 us
    pallas_call x1, Pallas kernels, weight_products(): pl.pallas_call(functools.partial(weight_kernel, owners, half, sections, s...  14.7 us
    unnamed x58, local copies, waits for them, and re-layouts  10.5 us
    pallas_call x8, Pallas kernels, add_received(): pl.pallas_call(functools.partial(add_kernel, active), in_specs=[pl.BlockS...  10.4 us
  transfers between devices with their start and end apart: 49, of which 10 were waited for; matrix products, arithmetic and copies ran while one was open for 1% of the time, Pallas kernels for 26%

profile of v4, /device:TPU:5, one launch (start us, length us, event | category | flops | bytes accessed | tf_op | source)
XLA Modules:
  0.0 302.2 jit_solution(2687273064429463198)
XLA Ops:
  0.7 2.3 dynamic-slice_bitcast_fusion
  7.5 2.4 place_shards.1
  10.6 1.5 collective-permute-start.5
  12.2 6.4 %collective-permute-done.7.refs_1_ = bf16[128,2560]{1,0:T(8,128)(2,1)S(1)} collective-permute-done((bf16[128,2560]{1,0:T(8,128)(2,1)S(1)}, bf16[128,2560]{1,0:T(8,128)(2,1)S(1)}, u32[]{:S(2)}, u32[]{:S(2)}) %collective-permute-start.7) | collective-permute-done | bytes 655392 | tf_op jit(solution)/shard_map/ppermute | solution.py:539
  19.4 3.0 join.2.refs_0_
  22.4 4.2 %collective-permute-start.9 = (bf16[256,2560]{1,0:T(8,128)(2,1)}, bf16[256,2560]{1,0:T(8,128)(2,1)}, u32[]{:S(2)}, u32[]{:S(2)}) collective-permute-start(bf16[256,2560]{1,0:T(8,128)(2,1)} %join.2.refs_0_), channel_id=1, source_target_pairs={{0,2},{1,3},{2,0},{3,1},{4,6},{5,7},{6,4},{7,5},{8,10},{9,11},{10,... | collective-permute-start | bytes 3932168 | tf_op jit(solution)/shard_map/ppermute | solution.py:539
  26.7 3.2 %collective-permute-start.8 = (bf16[256,2560]{1,0:T(8,128)(2,1)}, bf16[256,2560]{1,0:T(8,128)(2,1)}, u32[]{:S(2)}, u32[]{:S(2)}) collective-permute-start(bf16[256,2560]{1,0:T(8,128)(2,1)} %join.2.refs_0_), channel_id=1, source_target_pairs={{0,1},{1,0},{2,3},{3,2},{4,5},{5,4},{6,7},{7,6},{8,9},{9,8},{10,11... | collective-permute-start | bytes 3932168 | tf_op jit(solution)/shard_map/ppermute | solution.py:539
  33.5 1.5 collective-permute-start.10
  35.0 1.6 collective-permute-start.6
  36.6 46.7 %collective-permute-done.9.refs_5_.refs_2_ = bf16[256,2560]{1,0:T(8,128)(2,1)} collective-permute-done((bf16[256,2560]{1,0:T(8,128)(2,1)}, bf16[256,2560]{1,0:T(8,128)(2,1)}, u32[]{:S(2)}, u32[]{:S(2)}) %collective-permute-start.9) | collective-permute-done | bytes 1310752 | tf_op jit(solution)/shard_map/ppermute | solution.py:539
  84.1 1.5 collective-permute-start.12
  85.6 1.5 collective-permute-start.11
  88.4 1.6 collective-permute-start.17
  90.7 1.6 collective-permute-start.15
  93.1 1.3 collective-permute-start.13
  94.4 1.3 collective-permute-start.14
  95.7 3.4 %collective-permute-start.21 = (bf16[256,2560]{1,0:T(8,128)(2,1)}, bf16[256,2560]{1,0:T(8,128)(2,1)}, u32[]{:S(2)}, u32[]{:S(2)}) collective-permute-start(bf16[256,2560]{1,0:T(8,128)(2,1)} %collective-permute-done.9.refs_5_.refs_2_), channel_id=1, source_target_pairs={{0,1},{1,0},{2,3},{3,2},{4,5},{5,4},{6,7},{7,6},{8,9},{9,8},{10,11... | collective-permute-start | bytes 3932168 | tf_op jit(solution)/shard_map/ppermute | solution.py:539
  99.8 1.3 collective-permute-start.16
  101.8 1.5 collective-permute-start.18
  103.3 12.4 %collective-permute-done.13.refs_2_.refs_0_ = bf16[4,64,1280]{2,1,0:T(8,128)(2,1)S(1)} collective-permute-done((bf16[4,64,1280]{2,1,0:T(8,128)(2,1)}, bf16[4,64,1280]{2,1,0:T(8,128)(2,1)S(1)}, u32[]{:S(2)}, u32[]{:S(2)}) %collective-permute-start.13) | collective-permute-done | bytes 655392 | tf_op jit(solution)/shard_map/ppermute | solution.py:539
  117.6 1.3 collective-permute-start.20
  118.9 1.3 collective-permute-start.19
  120.2 5.7 %collective-permute-done.16.refs_1_.refs_2_ = bf16[4,64,1280]{2,1,0:T(8,128)(2,1)} collective-permute-done((bf16[4,64,1280]{2,1,0:T(8,128)(2,1)}, bf16[4,64,1280]{2,1,0:T(8,128)(2,1)}, u32[]{:S(2)}, u32[]{:S(2)}) %collective-permute-start.16) | collective-permute-done | bytes 655392 | tf_op jit(solution)/shard_map/ppermute | solution.py:539
  127.2 1.3 collective-permute-start.26
  128.5 5.2 %lead_products.10 = (bf16[4,64,1280]{2,1,0:T(8,128)(2,1)}, bf16[256,1280]{1,0:T(8,128)(2,1)}) custom-call(s32[2]{0:T(128)} %pad_add_fusion.where_ref, bf16[4,64,1280]{2,1,0:T(8,128)(2,1)} %copy-done.9, bf16[4,64,1280]{2,1,0:T(8,128)(2,1)} %copy-done.11, bf16[4,64,1280]{2,1,0:T(8,128)(2,1)} %collective-permute-done.16.refs_1_.refs_2_, ...), custom_call_target="tpu_custom_call" | custom-call | flops 1000 | bytes 1000 | tf_op jit(solution)/shard_map/lead_products/pallas_call | solution.py:101
  133.6 2.7 collective-permute-start.24
  136.3 5.5 %collective-permute-done.20.refs_3_.refs_1_ = bf16[4,64,1280]{2,1,0:T(8,128)(2,1)} collective-permute-done((bf16[4,64,1280]{2,1,0:T(8,128)(2,1)}, bf16[4,64,1280]{2,1,0:T(8,128)(2,1)}, u32[]{:S(2)}, u32[]{:S(2)}) %collective-permute-start.20) | collective-permute-done | bytes 655392 | tf_op jit(solution)/shard_map/ppermute | solution.py:539
  141.8 6.5 %collective-permute-done.19.refs_2_.refs_0_ = bf16[4,64,1280]{2,1,0:T(8,128)(2,1)} collective-permute-done((bf16[4,64,1280]{2,1,0:T(8,128)(2,1)}, bf16[4,64,1280]{2,1,0:T(8,128)(2,1)}, u32[]{:S(2)}, u32[]{:S(2)}) %collective-permute-start.19) | collective-permute-done | bytes 655392 | tf_op jit(solution)/shard_map/ppermute | solution.py:539
  148.2 7.2 %rest_products.10 = (bf16[256,1280]{1,0:T(8,128)(2,1)}, bf16[256,1280]{1,0:T(8,128)(2,1)}, bf16[256,1280]{1,0:T(8,128)(2,1)}) custom-call(s32[2]{0:T(128)} %pad_add_fusion.where_ref, bf16[4,64,1280]{2,1,0:T(8,128)(2,1)} %get-tuple-element.68.refs_0_.refs_10_.refs_2_, bf16[4,1280,1280]{2,1,0:T(8,128)(2,1)} %bitcast.36, ...), custom_call_target="tpu_custom_call" | custom-call | flops 199999995904 | bytes 1000 | tf_op jit(solution)/shard_map/rest_products/pallas_call | solution.py:101
  155.4 1.3 collective-permute-start.22
  156.8 3.1 %add_received.12.refs_4_ = bf16[256,1280]{1,0:T(8,128)(2,1)} custom-call(s32[2]{0:T(128)} %pad_add_fusion.where_ref, bf16[256,1280]{1,0:T(8,128)(2,1)} %get-tuple-element.73.kept_ref, bf16[256,1280]{1,0:T(8,128)(2,1)} %collective-permute-done.24.received_ref, bf16[256,1280]{1,0:T(8,128)(2,1)} %get-tuple-element.72.refs_0_), custom_call_target="tpu_custom_call" | custom-call | flops 1000 | bytes 1000 | tf_op jit(solution)/shard_map/add_received/pallas_call | solution.py:148
  159.9 1.3 collective-permute-start.25
  161.2 1.3 collective-permute-start.23
  162.6 5.1 %lead_products.11 = (bf16[4,64,1280]{2,1,0:T(8,128)(2,1)}, bf16[256,1280]{1,0:T(8,128)(2,1)}) custom-call(s32[2]{0:T(128)} %pad_add_fusion.where_ref, bf16[4,64,1280]{2,1,0:T(8,128)(2,1)} %collective-permute-done.19.refs_2_.refs_0_, bf16[4,64,1280]{2,1,0:T(8,128)(2,1)} %collective-permute-done.20.refs_3_.refs_1_, ...), custom_call_target="tpu_custom_call" | custom-call | flops 1000 | bytes 1000 | tf_op jit(solution)/shard_map/lead_products/pallas_call | solution.py:101
  168.3 1.3 collective-permute-start.27
  169.6 6.1 %collective-permute-start.28 = (bf16[256,1280]{1,0:T(8,128)(2,1)}, bf16[256,1280]{1,0:T(8,128)(2,1)}, u32[]{:S(2)}, u32[]{:S(2)}) collective-permute-start(bf16[256,1280]{1,0:T(8,128)(2,1)} %get-tuple-element.77), channel_id=1, source_target_pairs={{8,9},{9,8},{10,11},{11,10},{12,13},{13,12},{14,15},{15,14}} | collective-permute-start | bytes 1966088 | tf_op jit(solution)/shard_map/ppermute | solution.py:539
  177.0 1.7 collective-permute-start.30
  180.6 7.1 %rest_products.11 = (bf16[256,1280]{1,0:T(8,128)(2,1)}, bf16[256,1280]{1,0:T(8,128)(2,1)}, bf16[256,1280]{1,0:T(8,128)(2,1)}) custom-call(s32[2]{0:T(128)} %pad_add_fusion.where_ref, bf16[4,64,1280]{2,1,0:T(8,128)(2,1)} %get-tuple-element.75.refs_0_.refs_1_.refs_11_.refs_3_, bf16[4,1280,1280]{2,1,0:T(8,128)(2,1)} %bitcast.38, ...), custom_call_target="tpu_custom_call" | custom-call | flops 199999995904 | bytes 1000 | tf_op jit(solution)/shard_map/rest_products/pallas_call | solution.py:101
  188.7 3.1 %add_received.13.refs_4_ = bf16[256,1280]{1,0:T(8,128)(2,1)} custom-call(s32[2]{0:T(128)} %pad_add_fusion.where_ref, bf16[256,1280]{1,0:T(8,128)(2,1)} %get-tuple-element.76.kept_ref, bf16[256,1280]{1,0:T(8,128)(2,1)} %collective-permute-done.28.received_ref, bf16[256,1280]{1,0:T(8,128)(2,1)} %get-tuple-element.78.refs_0_), custom_call_target="tpu_custom_call" | custom-call | flops 1000 | bytes 1000 | tf_op jit(solution)/shard_map/add_received/pallas_call | solution.py:148
  194.2 1.3 collective-permute-start.34
  195.5 1.3 collective-permute-start.36
  196.9 1.3 collective-permute-start.35
  198.3 1.0 copy-done.1
  199.3 1.1 copy-done.2
  201.2 1.5 collective-permute-start.40
  202.7 3.0 pick.3
  205.7 1.5 collective-permute-start.32
  207.2 1.5 collective-permute-start.33
  208.7 3.1 %collective-permute-start.41 = (bf16[2,4,64,1280]{3,2,1,0:T(8,128)(2,1)}, bf16[2,4,64,1280]{3,2,1,0:T(8,128)(2,1)}, u32[]{:S(2)}, u32[]{:S(2)}) collective-permute-start(bf16[2,4,64,1280]{3,2,1,0:T(8,128)(2,1)} %pick.3), channel_id=1, source_target_pairs={{8,12},{9,13},{10,14},{11,15},{12,8},{13,9},{14,10},{15,11}} | collective-permute-start | bytes 3932168 | tf_op jit(solution)/shard_map/ppermute | solution.py:539
  211.8 1.0 collective-permute-done.35.refs_2_.refs_1_
  215.8 1.7 collective-permute-start.43
  218.3 1.5 collective-permute-start.38
  219.8 1.5 collective-permute-start.44
  221.3 1.5 collective-permute-start.37
  222.8 6.3 %collective-permute-done.41.refs_4_.refs_18_ = bf16[2,4,64,1280]{3,2,1,0:T(8,128)(2,1)} collective-permute-done((bf16[2,4,64,1280]{3,2,1,0:T(8,128)(2,1)}, bf16[2,4,64,1280]{3,2,1,0:T(8,128)(2,1)}, u32[]{:S(2)}, u32[]{:S(2)}) %collective-permute-start.41) | collective-permute-done | bytes 1310752 | tf_op jit(solution)/shard_map/ppermute | solution.py:539
  231.2 3.3 %cut_shards.1 = (bf16[128,1280]{1,0:T(8,128)(2,1)}, bf16[128,1280]{1,0:T(8,128)(2,1)}, bf16[128,1280]{1,0:T(8,128)(2,1)}, bf16[128,1280]{1,0:T(8,128)(2,1)}) custom-call(s32[2]{0:T(128)} %pad_add_fusion.where_ref, bf16[4,64,1280]{2,1,0:T(8,128)(2,1)} %get-tuple-element.88.refs_2_.refs_8_.refs_0_, bf16[4,64,1280]{2,1,0:T(8,128)(2,1)} %get-tuple-element.89.refs_9_.refs_1_, ...), custom_call_target="tpu_custom_call" | custom-call | flops 1000 | bytes 1000 | tf_op jit(solution)/shard_map/cut_shards/pallas_call | solution.py:328
  234.5 21.5 %collective-permute-start.45 = (bf16[128,1280]{1,0:T(8,128)(2,1)}, bf16[128,1280]{1,0:T(8,128)(2,1)S(1)}, u32[]{:S(2)}, u32[]{:S(2)}) collective-permute-start(bf16[128,1280]{1,0:T(8,128)(2,1)} %get-tuple-element.90), channel_id=1, source_target_pairs={{0,8},{1,9},{2,10},{3,11},{4,12},{5,13},{6,14},{7,15},{8,16},{9,17... | collective-permute-start | bytes 983048 | tf_op jit(solution)/shard_map/ppermute | solution.py:539
  256.0 3.4 %collective-permute-start.46 = (bf16[128,1280]{1,0:T(8,128)(2,1)}, bf16[128,1280]{1,0:T(8,128)(2,1)S(1)}, u32[]{:S(2)}, u32[]{:S(2)}) collective-permute-start(bf16[128,1280]{1,0:T(8,128)(2,1)} %get-tuple-element.91), channel_id=1, source_target_pairs={{0,9},{1,8},{2,11},{3,10},{4,13},{5,12},{6,15},{7,14},{8,17},{9,16... | collective-permute-start | bytes 983048 | tf_op jit(solution)/shard_map/ppermute | solution.py:539
  259.4 10.5 %collective-permute-start.47 = (bf16[128,1280]{1,0:T(8,128)(2,1)}, bf16[128,1280]{1,0:T(8,128)(2,1)S(1)}, u32[]{:S(2)}, u32[]{:S(2)}) collective-permute-start(bf16[128,1280]{1,0:T(8,128)(2,1)} %get-tuple-element.92), channel_id=1, source_target_pairs={{0,10},{1,11},{2,8},{3,9},{4,14},{5,15},{6,12},{7,13},{8,18},{9,19... | collective-permute-start | bytes 983048 | tf_op jit(solution)/shard_map/ppermute | solution.py:539
  269.9 3.1 %collective-permute-start.48 = (bf16[128,1280]{1,0:T(8,128)(2,1)}, bf16[128,1280]{1,0:T(8,128)(2,1)S(1)}, u32[]{:S(2)}, u32[]{:S(2)}) collective-permute-start(bf16[128,1280]{1,0:T(8,128)(2,1)} %get-tuple-element.93), channel_id=1, source_target_pairs={{0,11},{1,10},{2,9},{3,8},{4,15},{5,14},{6,13},{7,12},{8,19},{9,18... | collective-permute-start | bytes 983048 | tf_op jit(solution)/shard_map/ppermute | solution.py:539
  273.0 14.7 %weight_products.1.refs_6_ = f32[2560,1280]{1,0:T(8,128)} custom-call(s32[2]{0:T(128)} %pad_add_fusion.where_ref, bf16[256,2560]{1,0:T(8,128)(2,1)} %join.2.refs_0_, bf16[256,2560]{1,0:T(8,128)(2,1)} %collective-permute-done.8.refs_4_.refs_1_, bf16[256,2560]{1,0:T(8,128)(2,1)} %collective-permute-done.9.refs_5_.refs_2_, ...), custom_call_target="tpu_custom_call" | custom-call | flops 1000 | bytes 1000 | tf_op jit(solution)/shard_map/weight_products/pallas_call | solution.py:501
  288.6 4.0 %first_inputs.1.sums_ref = bf16[128,5120]{1,0:T(8,128)(2,1)} custom-call(s32[2]{0:T(128)} %pad_add_fusion.where_ref, f32[64,5120]{1,0:T(8,128)} %get-tuple-element.79.refs_0_, bf16[64,5120]{1,0:T(8,128)(2,1)} %collective-permute-done.32.refs_2_.refs_1_, bf16[64,5120]{1,0:T(8,128)(2,1)} %collective-permute-done.37.refs_2_, ...), custom_call_target="tpu_custom_call" | custom-call | flops 1000 | bytes 1000 | tf_op jit(solution)/shard_map/first_inputs/pallas_call | solution.py:266
  292.6 5.2 %collective-permute-done.47.refs_2_ = bf16[128,1280]{1,0:T(8,128)(2,1)S(1)} collective-permute-done((bf16[128,1280]{1,0:T(8,128)(2,1)}, bf16[128,1280]{1,0:T(8,128)(2,1)S(1)}, u32[]{:S(2)}, u32[]{:S(2)}) %collective-permute-start.47) | collective-permute-done | bytes 327712 | tf_op jit(solution)/shard_map/ppermute | solution.py:539
  299.3 2.9 place_inputs.1
  (131 shorter events, 33.4 us)
Async XLA Ops:
  0.6 2.3 copy-start.5
  3.0 15.6 %collective-permute-start.7 = (bf16[128,2560]{1,0:T(8,128)(2,1)S(1)}, bf16[128,2560]{1,0:T(8,128)(2,1)S(1)}, u32[]{:S(2)}, u32[]{:S(2)}) collective-permute-start(bf16[128,2560]{1,0:T(8,128)(2,1)S(1)} %get-tuple-element.94), channel_id=1, source_target_pairs={{0,4},{1,5},{2,6},{3,7},{4,0},{5,1},{6,2},{7,3},{8,12},{9,13},{10,... | collective-permute-start | bytes 1966088 | tf_op jit(solution)/shard_map/ppermute | solution.py:539
  3.9 2.6 collective-permute-start.2
  4.6 1.9 collective-permute-start
  5.3 1.3 collective-permute-start.1
  10.6 21.4 %collective-permute-start.5 = (bf16[256,1280]{1,0:T(8,128)(2,1)}, bf16[256,1280]{1,0:T(8,128)(2,1)}, u32[]{:S(2)}, u32[]{:S(2)}) collective-permute-start(bf16[256,1280]{1,0:T(8,128)(2,1)} %get-tuple-element.53), channel_id=1, source_target_pairs={{24,25},{25,24},{26,27},{27,26},{28,29},{29,28},{30,31},{31,30}} | collective-permute-start | bytes 1966088 | tf_op jit(solution)/shard_map/ppermute | solution.py:539
  22.4 60.9 %collective-permute-start.9 = (bf16[256,2560]{1,0:T(8,128)(2,1)}, bf16[256,2560]{1,0:T(8,128)(2,1)}, u32[]{:S(2)}, u32[]{:S(2)}) collective-permute-start(bf16[256,2560]{1,0:T(8,128)(2,1)} %join.2.refs_0_), channel_id=1, source_target_pairs={{0,2},{1,3},{2,0},{3,1},{4,6},{5,7},{6,4},{7,5},{8,10},{9,11},{10,... | collective-permute-start | bytes 3932168 | tf_op jit(solution)/shard_map/ppermute | solution.py:539
  26.7 56.6 %collective-permute-start.8 = (bf16[256,2560]{1,0:T(8,128)(2,1)}, bf16[256,2560]{1,0:T(8,128)(2,1)}, u32[]{:S(2)}, u32[]{:S(2)}) collective-permute-start(bf16[256,2560]{1,0:T(8,128)(2,1)} %join.2.refs_0_), channel_id=1, source_target_pairs={{0,1},{1,0},{2,3},{3,2},{4,5},{5,4},{6,7},{7,6},{8,9},{9,8},{10,11... | collective-permute-start | bytes 3932168 | tf_op jit(solution)/shard_map/ppermute | solution.py:539
  30.6 4.4 %collective-permute-start.3 = (bf16[4,64,1280]{2,1,0:T(8,128)(2,1)}, bf16[4,64,1280]{2,1,0:T(8,128)(2,1)S(1)}, u32[]{:S(2)}, u32[]{:S(2)}) collective-permute-start(bf16[4,64,1280]{2,1,0:T(8,128)(2,1)} %bitcast.59), channel_id=1, source_target_pairs={{24,16},{25,17},{26,18},{27,19},{28,20},{29,21},{30,22},{31,23}} | collective-permute-start | bytes 1966088 | tf_op jit(solution)/shard_map/ppermute | solution.py:539
  31.3 5.2 %collective-permute-start.4 = (bf16[4,64,1280]{2,1,0:T(8,128)(2,1)}, bf16[4,64,1280]{2,1,0:T(8,128)(2,1)S(1)}, u32[]{:S(2)}, u32[]{:S(2)}) collective-permute-start(bf16[4,64,1280]{2,1,0:T(8,128)(2,1)} %bitcast.51), channel_id=1, source_target_pairs={{24,17},{25,16},{26,19},{27,18},{28,21},{29,20},{30,23},{31,22}} | collective-permute-start | bytes 1966088 | tf_op jit(solution)/shard_map/ppermute | solution.py:539
  33.5 54.2 %collective-permute-start.10 = (bf16[256,1280]{1,0:T(8,128)(2,1)}, bf16[256,1280]{1,0:T(8,128)(2,1)}, u32[]{:S(2)}, u32[]{:S(2)}) collective-permute-start(bf16[256,1280]{1,0:T(8,128)(2,1)} %get-tuple-element.57), channel_id=1, source_target_pairs={{24,25},{25,24},{26,27},{27,26},{28,29},{29,28},{30,31},{31,30}} | collective-permute-start | bytes 1966088 | tf_op jit(solution)/shard_map/ppermute | solution.py:539
  35.0 48.3 %copy-start.10 = (bf16[4,64,1280]{2,1,0:T(8,128)(2,1)}, bf16[4,64,1280]{2,1,0:T(8,128)(2,1)S(1)}, u32[]{:S(2)}) copy-start(bf16[4,64,1280]{2,1,0:T(8,128)(2,1)S(1)} %collective-permute-done.3.refs_2_.refs_0_) | copy-start | bytes 1966084
  35.0 52.1 %collective-permute-start.6 = (bf16[4,64,1280]{2,1,0:T(8,128)(2,1)}, bf16[4,64,1280]{2,1,0:T(8,128)(2,1)}, u32[]{:S(2)}, u32[]{:S(2)}) collective-permute-start(bf16[4,64,1280]{2,1,0:T(8,128)(2,1)} %bitcast.5), channel_id=1, source_target_pairs={{24,18},{25,19},{26,16},{27,17},{28,22},{29,23},{30,20},{31,21}} | collective-permute-start | bytes 1966088 | tf_op jit(solution)/shard_map/ppermute | solution.py:539
  36.5 46.8 %copy-start.12 = (bf16[4,64,1280]{2,1,0:T(8,128)(2,1)}, bf16[4,64,1280]{2,1,0:T(8,128)(2,1)S(1)}, u32[]{:S(2)}) copy-start(bf16[4,64,1280]{2,1,0:T(8,128)(2,1)S(1)} %collective-permute-done.4.refs_3_.refs_1_) | copy-start | bytes 1966084
  84.1 8.2 %collective-permute-start.12 = (bf16[4,64,1280]{2,1,0:T(8,128)(2,1)}, bf16[4,64,1280]{2,1,0:T(8,128)(2,1)}, u32[]{:S(2)}, u32[]{:S(2)}) collective-permute-start(bf16[4,64,1280]{2,1,0:T(8,128)(2,1)} %bitcast.58), channel_id=1, source_target_pairs={{24,17},{25,16},{26,19},{27,18},{28,21},{29,20},{30,23},{31,22}} | collective-permute-start | bytes 1966088 | tf_op jit(solution)/shard_map/ppermute | solution.py:539
  85.6 6.7 %collective-permute-start.11 = (bf16[4,64,1280]{2,1,0:T(8,128)(2,1)}, bf16[4,64,1280]{2,1,0:T(8,128)(2,1)}, u32[]{:S(2)}, u32[]{:S(2)}) collective-permute-start(bf16[4,64,1280]{2,1,0:T(8,128)(2,1)} %bitcast.55), channel_id=1, source_target_pairs={{24,16},{25,17},{26,18},{27,19},{28,20},{29,21},{30,22},{31,23}} | collective-permute-start | bytes 1966088 | tf_op jit(solution)/shard_map/ppermute | solution.py:539
  88.4 12.7 %collective-permute-start.17 = (bf16[4,64,1280]{2,1,0:T(8,128)(2,1)}, bf16[4,64,1280]{2,1,0:T(8,128)(2,1)}, u32[]{:S(2)}, u32[]{:S(2)}) collective-permute-start(bf16[4,64,1280]{2,1,0:T(8,128)(2,1)} %bitcast.43), channel_id=1, source_target_pairs={{24,18},{25,19},{26,16},{27,17},{28,22},{29,23},{30,20},{31,21}} | collective-permute-start | bytes 1966088 | tf_op jit(solution)/shard_map/ppermute | solution.py:539
  90.7 8.3 %collective-permute-start.15 = (bf16[256,1280]{1,0:T(8,128)(2,1)}, bf16[256,1280]{1,0:T(8,128)(2,1)}, u32[]{:S(2)}, u32[]{:S(2)}) collective-permute-start(bf16[256,1280]{1,0:T(8,128)(2,1)} %get-tuple-element.64), channel_id=1, source_target_pairs={{16,17},{17,16},{18,19},{19,18},{20,21},{21,20},{22,23},{23,22}} | collective-permute-start | bytes 1966088 | tf_op jit(solution)/shard_map/ppermute | solution.py:539
  93.1 22.7 %collective-permute-start.13 = (bf16[4,64,1280]{2,1,0:T(8,128)(2,1)}, bf16[4,64,1280]{2,1,0:T(8,128)(2,1)S(1)}, u32[]{:S(2)}, u32[]{:S(2)}) collective-permute-start(bf16[4,64,1280]{2,1,0:T(8,128)(2,1)} %bitcast.57), channel_id=1, source_target_pairs={{16,8},{17,9},{18,10},{19,11},{20,12},{21,13},{22,14},{23,15}} | collective-permute-start | bytes 1966088 | tf_op jit(solution)/shard_map/ppermute | solution.py:539
  94.4 21.4 %collective-permute-start.14 = (bf16[4,64,1280]{2,1,0:T(8,128)(2,1)}, bf16[4,64,1280]{2,1,0:T(8,128)(2,1)S(1)}, u32[]{:S(2)}, u32[]{:S(2)}) collective-permute-start(bf16[4,64,1280]{2,1,0:T(8,128)(2,1)} %bitcast.50), channel_id=1, source_target_pairs={{16,9},{17,8},{18,11},{19,10},{20,13},{21,12},{22,15},{23,14}} | collective-permute-start | bytes 1966088 | tf_op jit(solution)/shard_map/ppermute | solution.py:539
  95.7 40.6 %collective-permute-start.21 = (bf16[256,2560]{1,0:T(8,128)(2,1)}, bf16[256,2560]{1,0:T(8,128)(2,1)}, u32[]{:S(2)}, u32[]{:S(2)}) collective-permute-start(bf16[256,2560]{1,0:T(8,128)(2,1)} %collective-permute-done.9.refs_5_.refs_2_), channel_id=1, source_target_pairs={{0,1},{1,0},{2,3},{3,2},{4,5},{5,4},{6,7},{7,6},{8,9},{9,8},{10,11... | collective-permute-start | bytes 3932168 | tf_op jit(solution)/shard_map/ppermute | solution.py:539
  99.8 26.1 %collective-permute-start.16 = (bf16[4,64,1280]{2,1,0:T(8,128)(2,1)}, bf16[4,64,1280]{2,1,0:T(8,128)(2,1)}, u32[]{:S(2)}, u32[]{:S(2)}) collective-permute-start(bf16[4,64,1280]{2,1,0:T(8,128)(2,1)} %bitcast.46), channel_id=1, source_target_pairs={{16,10},{17,11},{18,8},{19,9},{20,14},{21,15},{22,12},{23,13}} | collective-permute-start | bytes 1966088 | tf_op jit(solution)/shard_map/ppermute | solution.py:539
  101.8 24.6 %collective-permute-start.18 = (bf16[256,1280]{1,0:T(8,128)(2,1)}, bf16[256,1280]{1,0:T(8,128)(2,1)}, u32[]{:S(2)}, u32[]{:S(2)}) collective-permute-start(bf16[256,1280]{1,0:T(8,128)(2,1)} %get-tuple-element.67), channel_id=1, source_target_pairs={{16,17},{17,16},{18,19},{19,18},{20,21},{21,20},{22,23},{23,22}} | collective-permute-start | bytes 1966088 | tf_op jit(solution)/shard_map/ppermute | solution.py:539
  117.6 24.2 %collective-permute-start.20 = (bf16[4,64,1280]{2,1,0:T(8,128)(2,1)}, bf16[4,64,1280]{2,1,0:T(8,128)(2,1)}, u32[]{:S(2)}, u32[]{:S(2)}) collective-permute-start(bf16[4,64,1280]{2,1,0:T(8,128)(2,1)} %bitcast.56), channel_id=1, source_target_pairs={{16,9},{17,8},{18,11},{19,10},{20,13},{21,12},{22,15},{23,14}} | collective-permute-start | bytes 1966088 | tf_op jit(solution)/shard_map/ppermute | solution.py:539
  118.9 29.4 %collective-permute-start.19 = (bf16[4,64,1280]{2,1,0:T(8,128)(2,1)}, bf16[4,64,1280]{2,1,0:T(8,128)(2,1)}, u32[]{:S(2)}, u32[]{:S(2)}) collective-permute-start(bf16[4,64,1280]{2,1,0:T(8,128)(2,1)} %bitcast.54), channel_id=1, source_target_pairs={{16,8},{17,9},{18,10},{19,11},{20,12},{21,13},{22,14},{23,15}} | collective-permute-start | bytes 1966088 | tf_op jit(solution)/shard_map/ppermute | solution.py:539
  127.2 35.4 %collective-permute-start.26 = (bf16[4,64,1280]{2,1,0:T(8,128)(2,1)}, bf16[4,64,1280]{2,1,0:T(8,128)(2,1)}, u32[]{:S(2)}, u32[]{:S(2)}) collective-permute-start(bf16[4,64,1280]{2,1,0:T(8,128)(2,1)} %bitcast.44), channel_id=1, source_target_pairs={{16,10},{17,11},{18,8},{19,9},{20,14},{21,15},{22,12},{23,13}} | collective-permute-start | bytes 1966088 | tf_op jit(solution)/shard_map/ppermute | solution.py:539
  133.6 23.1 %collective-permute-start.24 = (bf16[256,1280]{1,0:T(8,128)(2,1)}, bf16[256,1280]{1,0:T(8,128)(2,1)}, u32[]{:S(2)}, u32[]{:S(2)}) collective-permute-start(bf16[256,1280]{1,0:T(8,128)(2,1)} %get-tuple-element.74), channel_id=1, source_target_pairs={{8,9},{9,8},{10,11},{11,10},{12,13},{13,12},{14,15},{15,14}} | collective-permute-start | bytes 1966088 | tf_op jit(solution)/shard_map/ppermute | solution.py:539
  155.4 23.3 %collective-permute-start.22 = (bf16[4,64,1280]{2,1,0:T(8,128)(2,1)}, bf16[4,64,1280]{2,1,0:T(8,128)(2,1)S(1)}, u32[]{:S(2)}, u32[]{:S(2)}) collective-permute-start(bf16[4,64,1280]{2,1,0:T(8,128)(2,1)} %bitcast.53), channel_id=1, source_target_pairs={{8,0},{9,1},{10,2},{11,3},{12,4},{13,5},{14,6},{15,7}} | collective-permute-start | bytes 1966088 | tf_op jit(solution)/shard_map/ppermute | solution.py:539
  156.8 4.4 %copy-start.19 = (bf16[256,1280]{1,0:T(8,128)(2,1)S(1)}, bf16[256,1280]{1,0:T(8,128)(2,1)}, u32[]{:S(2)}) copy-start(bf16[256,1280]{1,0:T(8,128)(2,1)} %get-tuple-element.72.refs_0_) | copy-start | bytes 1966084
  159.9 18.9 %collective-permute-start.25 = (bf16[4,64,1280]{2,1,0:T(8,128)(2,1)}, bf16[4,64,1280]{2,1,0:T(8,128)(2,1)S(1)}, u32[]{:S(2)}, u32[]{:S(2)}) collective-permute-start(bf16[4,64,1280]{2,1,0:T(8,128)(2,1)} %bitcast.45), channel_id=1, source_target_pairs={{8,2},{9,3},{10,0},{11,1},{12,6},{13,7},{14,4},{15,5}} | collective-permute-start | bytes 1966088 | tf_op jit(solution)/shard_map/ppermute | solution.py:539
  161.2 17.5 %collective-permute-start.23 = (bf16[4,64,1280]{2,1,0:T(8,128)(2,1)S(1)}, bf16[4,64,1280]{2,1,0:T(8,128)(2,1)S(1)}, u32[]{:S(2)}, u32[]{:S(2)}) collective-permute-start(bf16[4,64,1280]{2,1,0:T(8,128)(2,1)S(1)} %bitcast.49), channel_id=1, source_target_pairs={{8,1},{9,0},{10,3},{11,2},{12,5},{13,4},{14,7},{15,6}} | collective-permute-start | bytes 1966088 | tf_op jit(solution)/shard_map/ppermute | solution.py:539
  168.3 7.4 %collective-permute-start.27 = (f32[8,128]{1,0:T(8,128)}, f32[8,128]{1,0:T(8,128)S(1)}, u32[]{:S(2)}, u32[]{:S(2)}) collective-permute-start(f32[8,128]{1,0:T(8,128)} %mark.7), channel_id=1, source_target_pairs={{8,16},{9,17},{10,18},{11,19},{12,20},{13,21},{14,22},{15,23},{16,... | collective-permute-start | bytes 12296 | tf_op jit(solution)/shard_map/ppermute | solution.py:539
  169.6 19.1 %collective-permute-start.28 = (bf16[256,1280]{1,0:T(8,128)(2,1)}, bf16[256,1280]{1,0:T(8,128)(2,1)}, u32[]{:S(2)}, u32[]{:S(2)}) collective-permute-start(bf16[256,1280]{1,0:T(8,128)(2,1)} %get-tuple-element.77), channel_id=1, source_target_pairs={{8,9},{9,8},{10,11},{11,10},{12,13},{13,12},{14,15},{15,14}} | collective-permute-start | bytes 1966088 | tf_op jit(solution)/shard_map/ppermute | solution.py:539
  177.0 19.9 %collective-permute-start.30 = (bf16[256,2560]{1,0:T(8,128)(2,1)}, bf16[256,2560]{1,0:T(8,128)(2,1)}, u32[]{:S(2)}, u32[]{:S(2)}) collective-permute-start(bf16[256,2560]{1,0:T(8,128)(2,1)} %join.3.refs_4_), channel_id=1, source_target_pairs={{16,18},{17,19},{18,16},{19,17},{20,22},{21,23},{22,20},{23,21},{2... | collective-permute-start | bytes 3932168 | tf_op jit(solution)/shard_map/ppermute | solution.py:539
  178.7 1.1 copy-start.7
  188.7 3.1 %copy-start.3 = (bf16[256,2560]{1,0:T(8,128)(2,1)S(1)}, bf16[256,2560]{1,0:T(8,128)(2,1)}, u32[]{:S(2)}) copy-start(bf16[256,2560]{1,0:T(8,128)(2,1)} %join.3.refs_4_) | copy-start | bytes 3932164
  191.8 2.4 copy-start.28
  191.8 3.7 %copy-start = (bf16[256,1280]{1,0:T(8,128)(2,1)S(1)}, bf16[256,1280]{1,0:T(8,128)(2,1)}, u32[]{:S(2)}) copy-start(bf16[256,1280]{1,0:T(8,128)(2,1)} %add_received.13.refs_4_) | copy-start | bytes 1966084
  191.8 5.1 %copy-start.18 = (bf16[256,1280]{1,0:T(8,128)(2,1)S(1)}, bf16[256,1280]{1,0:T(8,128)(2,1)}, u32[]{:S(2)}) copy-start(bf16[256,1280]{1,0:T(8,128)(2,1)} %get-tuple-element.78.refs_0_) | copy-start | bytes 1966084
  191.8 6.4 %collective-permute-start.29 = (bf16[256,2560]{1,0:T(8,128)(2,1)S(1)}, bf16[256,2560]{1,0:T(8,128)(2,1)S(1)}, u32[]{:S(2)}, u32[]{:S(2)}) collective-permute-start(bf16[256,2560]{1,0:T(8,128)(2,1)S(1)} %copy-done.3), channel_id=1, source_target_pairs={{16,17},{17,16},{18,19},{19,18},{20,21},{21,20},{22,23},{23,22},{2... | collective-permute-start | bytes 3932168 | tf_op jit(solution)/shard_map/ppermute | solution.py:539
  193.4 4.8 %collective-permute-start.31 = (bf16[2,4,64,1280]{3,2,1,0:T(8,128)(2,1)}, bf16[2,4,64,1280]{3,2,1,0:T(8,128)(2,1)S(1)}, u32[]{:S(2)}, u32[]{:S(2)}) collective-permute-start(bf16[2,4,64,1280]{3,2,1,0:T(8,128)(2,1)} %pick.2), channel_id=1, source_target_pairs={{16,20},{17,21},{18,22},{19,23},{20,16},{21,17},{22,18},{23,19},{2... | collective-permute-start | bytes 3932168 | tf_op jit(solution)/shard_map/ppermute | solution.py:539
  194.2 13.0 %collective-permute-start.34 = (bf16[4,64,1280]{2,1,0:T(8,128)(2,1)S(1)}, bf16[4,64,1280]{2,1,0:T(8,128)(2,1)S(1)}, u32[]{:S(2)}, u32[]{:S(2)}) collective-permute-start(bf16[4,64,1280]{2,1,0:T(8,128)(2,1)S(1)} %bitcast.52), channel_id=1, source_target_pairs={{8,0},{9,1},{10,2},{11,3},{12,4},{13,5},{14,6},{15,7}} | collective-permute-start | bytes 1966088 | tf_op jit(solution)/shard_map/ppermute | solution.py:539
  195.5 13.1 %collective-permute-start.36 = (bf16[4,64,1280]{2,1,0:T(8,128)(2,1)S(1)}, bf16[4,64,1280]{2,1,0:T(8,128)(2,1)S(1)}, u32[]{:S(2)}, u32[]{:S(2)}) collective-permute-start(bf16[4,64,1280]{2,1,0:T(8,128)(2,1)S(1)} %bitcast.42), channel_id=1, source_target_pairs={{8,2},{9,3},{10,0},{11,1},{12,6},{13,7},{14,4},{15,5}} | collective-permute-start | bytes 1966088 | tf_op jit(solution)/shard_map/ppermute | solution.py:539
  196.9 15.9 %collective-permute-start.35 = (bf16[4,64,1280]{2,1,0:T(8,128)(2,1)S(1)}, bf16[4,64,1280]{2,1,0:T(8,128)(2,1)S(1)}, u32[]{:S(2)}, u32[]{:S(2)}) collective-permute-start(bf16[4,64,1280]{2,1,0:T(8,128)(2,1)S(1)} %bitcast.48), channel_id=1, source_target_pairs={{8,1},{9,0},{10,3},{11,2},{12,5},{13,4},{14,7},{15,6}} | collective-permute-start | bytes 1966088 | tf_op jit(solution)/shard_map/ppermute | solution.py:539
  198.3 1.1 copy-start.1
  201.2 18.6 %collective-permute-start.40 = (bf16[4,64,1280]{2,1,0:T(8,128)(2,1)}, bf16[4,64,1280]{2,1,0:T(8,128)(2,1)}, u32[]{:S(2)}, u32[]{:S(2)}) collective-permute-start(bf16[4,64,1280]{2,1,0:T(8,128)(2,1)} %get-tuple-element.88.refs_2_.refs_8_.refs_0_), channel_id=1, source_target_pairs={{0,4},{1,5},{2,6},{3,7},{4,0},{5,1},{6,2},{7,3}} | collective-permute-start | bytes 1966088 | tf_op jit(solution)/shard_map/ppermute | solution.py:539
  205.7 12.6 %collective-permute-start.32 = (bf16[64,5120]{1,0:T(8,128)(2,1)}, bf16[64,5120]{1,0:T(8,128)(2,1)}, u32[]{:S(2)}, u32[]{:S(2)}) collective-permute-start(bf16[64,5120]{1,0:T(8,128)(2,1)} %get-tuple-element.80), channel_id=1, source_target_pairs={{0,1},{1,0},{2,3},{3,2},{4,5},{5,4},{6,7},{7,6}} | collective-permute-start | bytes 1966088 | tf_op jit(solution)/shard_map/ppermute | solution.py:539
  207.2 5.7 %copy-start.14 = (bf16[4,64,1280]{2,1,0:T(8,128)(2,1)}, bf16[4,64,1280]{2,1,0:T(8,128)(2,1)S(1)}, u32[]{:S(2)}) copy-start(bf16[4,64,1280]{2,1,0:T(8,128)(2,1)S(1)} %collective-permute-done.34.refs_1_.refs_0_) | copy-start | bytes 1966084
  207.2 8.6 %collective-permute-start.33 = (bf16[64,5120]{1,0:T(8,128)(2,1)}, bf16[64,5120]{1,0:T(8,128)(2,1)}, u32[]{:S(2)}, u32[]{:S(2)}) collective-permute-start(bf16[64,5120]{1,0:T(8,128)(2,1)} %get-tuple-element.82), channel_id=1, source_target_pairs={{0,1},{1,0},{2,3},{3,2},{4,5},{5,4},{6,7},{7,6}} | collective-permute-start | bytes 1966088 | tf_op jit(solution)/shard_map/ppermute | solution.py:539
  208.7 4.2 %copy-start.15 = (bf16[4,64,1280]{2,1,0:T(8,128)(2,1)}, bf16[4,64,1280]{2,1,0:T(8,128)(2,1)S(1)}, u32[]{:S(2)}) copy-start(bf16[4,64,1280]{2,1,0:T(8,128)(2,1)S(1)} %collective-permute-done.36.refs_3_.refs_2_) | copy-start | bytes 1966084
  208.7 20.4 %collective-permute-start.41 = (bf16[2,4,64,1280]{3,2,1,0:T(8,128)(2,1)}, bf16[2,4,64,1280]{3,2,1,0:T(8,128)(2,1)}, u32[]{:S(2)}, u32[]{:S(2)}) collective-permute-start(bf16[2,4,64,1280]{3,2,1,0:T(8,128)(2,1)} %pick.3), channel_id=1, source_target_pairs={{8,12},{9,13},{10,14},{11,15},{12,8},{13,9},{14,10},{15,11}} | collective-permute-start | bytes 3932168 | tf_op jit(solution)/shard_map/ppermute | solution.py:539
  215.1 6.2 %collective-permute-start.39 = (bf16[64,5120]{1,0:T(8,128)(2,1)}, bf16[64,5120]{1,0:T(8,128)(2,1)S(1)}, u32[]{:S(2)}, u32[]{:S(2)}) collective-permute-start(bf16[64,5120]{1,0:T(8,128)(2,1)} %get-tuple-element.87), channel_id=1, source_target_pairs={{0,1},{1,0},{2,3},{3,2},{4,5},{5,4},{6,7},{7,6}} | collective-permute-start | bytes 1966088 | tf_op jit(solution)/shard_map/ppermute | solution.py:539
  215.8 43.5 %collective-permute-start.43 = (bf16[256,2560]{1,0:T(8,128)(2,1)}, bf16[256,2560]{1,0:T(8,128)(2,1)}, u32[]{:S(2)}, u32[]{:S(2)}) collective-permute-start(bf16[256,2560]{1,0:T(8,128)(2,1)} %collective-permute-done.30.refs_6_), channel_id=1, source_target_pairs={{16,17},{17,16},{18,19},{19,18},{20,21},{21,20},{22,23},{23,22},{2... | collective-permute-start | bytes 3932168 | tf_op jit(solution)/shard_map/ppermute | solution.py:539
  218.3 12.9 %collective-permute-start.38 = (bf16[64,5120]{1,0:T(8,128)(2,1)}, bf16[64,5120]{1,0:T(8,128)(2,1)}, u32[]{:S(2)}, u32[]{:S(2)}) collective-permute-start(bf16[64,5120]{1,0:T(8,128)(2,1)} %get-tuple-element.86), channel_id=1, source_target_pairs={{0,1},{1,0},{2,3},{3,2},{4,5},{5,4},{6,7},{7,6}} | collective-permute-start | bytes 1966088 | tf_op jit(solution)/shard_map/ppermute | solution.py:539
  219.8 11.4 %collective-permute-start.44 = (bf16[4,64,1280]{2,1,0:T(8,128)(2,1)}, bf16[4,64,1280]{2,1,0:T(8,128)(2,1)}, u32[]{:S(2)}, u32[]{:S(2)}) collective-permute-start(bf16[4,64,1280]{2,1,0:T(8,128)(2,1)} %get-tuple-element.89.refs_9_.refs_1_), channel_id=1, source_target_pairs={{0,4},{1,5},{2,6},{3,7},{4,0},{5,1},{6,2},{7,3}} | collective-permute-start | bytes 1966088 | tf_op jit(solution)/shard_map/ppermute | solution.py:539
  221.3 7.8 %copy-start.17 = (bf16[64,5120]{1,0:T(8,128)(2,1)}, bf16[64,5120]{1,0:T(8,128)(2,1)S(1)}, u32[]{:S(2)}) copy-start(bf16[64,5120]{1,0:T(8,128)(2,1)S(1)} %collective-permute-done.39.refs_1_.received_ref) | copy-start | bytes 1966084
  221.3 48.6 %collective-permute-start.37 = (bf16[64,5120]{1,0:T(8,128)(2,1)}, bf16[64,5120]{1,0:T(8,128)(2,1)}, u32[]{:S(2)}, u32[]{:S(2)}) collective-permute-start(bf16[64,5120]{1,0:T(8,128)(2,1)} %add_received.14.refs_0_), channel_id=1, source_target_pairs={{0,2},{1,3},{2,0},{3,1},{4,6},{5,7},{6,4},{7,5}} | collective-permute-start | bytes 1966088 | tf_op jit(solution)/shard_map/ppermute | solution.py:539
  230.4 57.3 %collective-permute-start.42 = (bf16[64,5120]{1,0:T(8,128)(2,1)}, bf16[64,5120]{1,0:T(8,128)(2,1)S(1)}, u32[]{:S(2)}, u32[]{:S(2)}) collective-permute-start(bf16[64,5120]{1,0:T(8,128)(2,1)} %add_received.15.refs_6_), channel_id=1, source_target_pairs={{0,2},{1,3},{2,0},{3,1},{4,6},{5,7},{6,4},{7,5}} | collective-permute-start | bytes 1966088 | tf_op jit(solution)/shard_map/ppermute | solution.py:539
  234.5 58.1 %collective-permute-start.45 = (bf16[128,1280]{1,0:T(8,128)(2,1)}, bf16[128,1280]{1,0:T(8,128)(2,1)S(1)}, u32[]{:S(2)}, u32[]{:S(2)}) collective-permute-start(bf16[128,1280]{1,0:T(8,128)(2,1)} %get-tuple-element.90), channel_id=1, source_target_pairs={{0,8},{1,9},{2,10},{3,11},{4,12},{5,13},{6,14},{7,15},{8,16},{9,17... | collective-permute-start | bytes 983048 | tf_op jit(solution)/shard_map/ppermute | solution.py:539
  256.0 36.6 %collective-permute-start.46 = (bf16[128,1280]{1,0:T(8,128)(2,1)}, bf16[128,1280]{1,0:T(8,128)(2,1)S(1)}, u32[]{:S(2)}, u32[]{:S(2)}) collective-permute-start(bf16[128,1280]{1,0:T(8,128)(2,1)} %get-tuple-element.91), channel_id=1, source_target_pairs={{0,9},{1,8},{2,11},{3,10},{4,13},{5,12},{6,15},{7,14},{8,17},{9,16... | collective-permute-start | bytes 983048 | tf_op jit(solution)/shard_map/ppermute | solution.py:539
  259.4 38.5 %collective-permute-start.47 = (bf16[128,1280]{1,0:T(8,128)(2,1)}, bf16[128,1280]{1,0:T(8,128)(2,1)S(1)}, u32[]{:S(2)}, u32[]{:S(2)}) collective-permute-start(bf16[128,1280]{1,0:T(8,128)(2,1)} %get-tuple-element.92), channel_id=1, source_target_pairs={{0,10},{1,11},{2,8},{3,9},{4,14},{5,15},{6,12},{7,13},{8,18},{9,19... | collective-permute-start | bytes 983048 | tf_op jit(solution)/shard_map/ppermute | solution.py:539
  269.9 27.9 %collective-permute-start.48 = (bf16[128,1280]{1,0:T(8,128)(2,1)}, bf16[128,1280]{1,0:T(8,128)(2,1)S(1)}, u32[]{:S(2)}, u32[]{:S(2)}) collective-permute-start(bf16[128,1280]{1,0:T(8,128)(2,1)} %get-tuple-element.93), channel_id=1, source_target_pairs={{0,11},{1,10},{2,9},{3,8},{4,15},{5,14},{6,13},{7,12},{8,19},{9,18... | collective-permute-start | bytes 983048 | tf_op jit(solution)/shard_map/ppermute | solution.py:539
  292.6 5.3 %copy-start.20 = (bf16[128,1280]{1,0:T(8,128)(2,1)}, bf16[128,1280]{1,0:T(8,128)(2,1)S(1)}, u32[]{:S(2)}) copy-start(bf16[128,1280]{1,0:T(8,128)(2,1)S(1)} %collective-permute-done.45.refs_0_) | copy-start | bytes 983044
  292.6 5.3 %copy-start.21 = (bf16[128,1280]{1,0:T(8,128)(2,1)}, bf16[128,1280]{1,0:T(8,128)(2,1)S(1)}, u32[]{:S(2)}) copy-start(bf16[128,1280]{1,0:T(8,128)(2,1)S(1)} %collective-permute-done.46.refs_1_) | copy-start | bytes 983044
  (14 other events, 11.7 us)

commit v5 on v4

--- a/solution.py
+++ b/solution.py
@@ -12,6 +12,7 @@
 VMEM = 56 * 1024 * 1024
 ADD = 56 * 1024 * 1024
 SMALL = 56 * 1024 * 1024
+TAIL = 48 * 1024 * 1024
 F32 = jnp.float32
 BF16 = jnp.bfloat16
 LONG = pl.CostEstimate(flops=200000000000, bytes_accessed=1000, transcendentals=0)
@@ -268,7 +269,7 @@
         in_specs=[pl.BlockSpec(memory_space=pltpu.SMEM)] + [memory] * len(terms) + [ANY],
         out_specs=memory,
         out_shape=jax.ShapeDtypeStruct((tokens, model), BF16),
-        compiler_params=params(SMALL),
+        compiler_params=params(TAIL),
         cost_estimate=BRIEF,
         name="first_inputs",
     )(where, *terms, after)
@@ -289,7 +290,7 @@
         in_specs=[pl.BlockSpec(memory_space=pltpu.SMEM)] + [memory] * (1 + len(pieces)),
         out_specs=memory,
         out_shape=jax.ShapeDtypeStruct(sums.shape, BF16),
-        compiler_params=params(SMALL),
+        compiler_params=params(TAIL),
         name="place_inputs",
     )(where, sums, *pieces)
 

time: 306 us -> 304 us (level)
    unnamed x58 -> x52, local copies, waits for them, and re-layouts: 10.5 us -> 8.27 us
  transfers between devices with their start and end apart: 49 -> 49, of which waited for: 10 -> 10; matrix products, arithmetic and copies ran while one was open for 1% -> 1% of each run, Pallas kernels for 26% -> 25%
where the time goes in v5:
time: 304 us; the launch traced here: 299 us
  starting transfers between devices  110 us (36%)
  waiting for transfers between devices  98.9 us (33%)
  Pallas kernels  77.2 us (25%)
  local copies, waits for them, and re-layouts  11.6 us (4%)
    ppermute x49, starting transfers between devices, permute(): return lax.ppermute(value, AXES, pairs)  110 us
    ppermute x49, waiting for transfers between devices, permute(): return lax.ppermute(value, AXES, pairs)  98.9 us
    pallas_call x12, Pallas kernels, products(): pl.pallas_call(functools.partial(products_kernel, active, order, len(part...  30.3 us
    pallas_call x1, Pallas kernels, weight_products(): pl.pallas_call(functools.partial(weight_kernel, owners, half, sections, s...  14.7 us
    pallas_call x8, Pallas kernels, add_received(): pl.pallas_call(functools.partial(add_kernel, active), in_specs=[pl.BlockS...  10.4 us
    unnamed x52, local copies, waits for them, and re-layouts  8.27 us
  transfers between devices with their start and end apart: 49, of which 10 were waited for; matrix products, arithmetic and copies ran while one was open for 1% of the time, Pallas kernels for 25%

profile of v5, /device:TPU:5, one launch (start us, length us, event | category | flops | bytes accessed | tf_op | source)
XLA Modules:
  0.0 299.3 jit_solution(12129632083202137223)
XLA Ops:
  0.7 2.3 dynamic-slice_bitcast_fusion
  3.0 1.0 constant_dynamic-slice_fusion
  7.5 2.4 place_shards.1
  10.7 1.5 collective-permute-start.5
  12.2 6.4 %collective-permute-done.7.refs_1_ = bf16[128,2560]{1,0:T(8,128)(2,1)S(1)} collective-permute-done((bf16[128,2560]{1,0:T(8,128)(2,1)S(1)}, bf16[128,2560]{1,0:T(8,128)(2,1)S(1)}, u32[]{:S(2)}, u32[]{:S(2)}) %collective-permute-start.7) | collective-permute-done | bytes 655392 | tf_op jit(solution)/shard_map/ppermute | solution.py:540
  19.4 3.0 %join.2.refs_0_ = bf16[256,2560]{1,0:T(8,128)(2,1)} custom-call(s32[2]{0:T(128)} %pad_add_fusion.where_ref, bf16[128,2560]{1,0:T(8,128)(2,1)} %get-tuple-element.95.refs_0_, bf16[128,2560]{1,0:T(8,128)(2,1)} %copy-done.6, bf16[4,64,1280]{2,1,0:T(8,128)(2,1)} %get-tuple-element.48.refs_0_.refs_2_), custom_call_target="tpu_custom_call" | custom-call | flops 1000 | bytes 1000 | tf_op jit(solution)/shard_map/join/pallas_call | solution.py:412
  22.4 4.2 %collective-permute-start.9 = (bf16[256,2560]{1,0:T(8,128)(2,1)}, bf16[256,2560]{1,0:T(8,128)(2,1)}, u32[]{:S(2)}, u32[]{:S(2)}) collective-permute-start(bf16[256,2560]{1,0:T(8,128)(2,1)} %join.2.refs_0_), channel_id=1, source_target_pairs={{0,2},{1,3},{2,0},{3,1},{4,6},{5,7},{6,4},{7,5},{8,10},{9,11},{10,... | collective-permute-start | bytes 3932168 | tf_op jit(solution)/shard_map/ppermute | solution.py:540
  26.7 3.2 %collective-permute-start.8 = (bf16[256,2560]{1,0:T(8,128)(2,1)}, bf16[256,2560]{1,0:T(8,128)(2,1)}, u32[]{:S(2)}, u32[]{:S(2)}) collective-permute-start(bf16[256,2560]{1,0:T(8,128)(2,1)} %join.2.refs_0_), channel_id=1, source_target_pairs={{0,1},{1,0},{2,3},{3,2},{4,5},{5,4},{6,7},{7,6},{8,9},{9,8},{10,11... | collective-permute-start | bytes 3932168 | tf_op jit(solution)/shard_map/ppermute | solution.py:540
  33.5 1.5 collective-permute-start.10
  35.0 1.6 collective-permute-start.6
  36.6 46.8 %collective-permute-done.9.refs_5_.refs_2_ = bf16[256,2560]{1,0:T(8,128)(2,1)} collective-permute-done((bf16[256,2560]{1,0:T(8,128)(2,1)}, bf16[256,2560]{1,0:T(8,128)(2,1)}, u32[]{:S(2)}, u32[]{:S(2)}) %collective-permute-start.9) | collective-permute-done | bytes 1310752 | tf_op jit(solution)/shard_map/ppermute | solution.py:540
  84.1 1.5 collective-permute-start.12
  85.6 1.5 collective-permute-start.11
  88.4 1.6 collective-permute-start.17
  90.7 1.6 collective-permute-start.15
  93.0 1.3 collective-permute-start.13
  94.3 1.3 collective-permute-start.14
  95.6 3.4 %collective-permute-start.21 = (bf16[256,2560]{1,0:T(8,128)(2,1)}, bf16[256,2560]{1,0:T(8,128)(2,1)}, u32[]{:S(2)}, u32[]{:S(2)}) collective-permute-start(bf16[256,2560]{1,0:T(8,128)(2,1)} %collective-permute-done.9.refs_5_.refs_2_), channel_id=1, source_target_pairs={{0,1},{1,0},{2,3},{3,2},{4,5},{5,4},{6,7},{7,6},{8,9},{9,8},{10,11... | collective-permute-start | bytes 3932168 | tf_op jit(solution)/shard_map/ppermute | solution.py:540
  99.8 1.3 collective-permute-start.16
  101.8 1.5 collective-permute-start.18
  103.3 12.4 %collective-permute-done.13.refs_2_.refs_0_ = bf16[4,64,1280]{2,1,0:T(8,128)(2,1)S(1)} collective-permute-done((bf16[4,64,1280]{2,1,0:T(8,128)(2,1)}, bf16[4,64,1280]{2,1,0:T(8,128)(2,1)S(1)}, u32[]{:S(2)}, u32[]{:S(2)}) %collective-permute-start.13) | collective-permute-done | bytes 655392 | tf_op jit(solution)/shard_map/ppermute | solution.py:540
  117.5 1.3 collective-permute-start.20
  118.8 1.3 collective-permute-start.19
  120.1 5.7 %collective-permute-done.16.refs_1_.refs_2_ = bf16[4,64,1280]{2,1,0:T(8,128)(2,1)} collective-permute-done((bf16[4,64,1280]{2,1,0:T(8,128)(2,1)}, bf16[4,64,1280]{2,1,0:T(8,128)(2,1)}, u32[]{:S(2)}, u32[]{:S(2)}) %collective-permute-start.16) | collective-permute-done | bytes 655392 | tf_op jit(solution)/shard_map/ppermute | solution.py:540
  127.0 1.3 collective-permute-start.26
  128.3 5.1 %lead_products.10 = (bf16[4,64,1280]{2,1,0:T(8,128)(2,1)}, bf16[256,1280]{1,0:T(8,128)(2,1)}) custom-call(s32[2]{0:T(128)} %pad_add_fusion.where_ref, bf16[4,64,1280]{2,1,0:T(8,128)(2,1)} %copy-done.11, bf16[4,64,1280]{2,1,0:T(8,128)(2,1)} %copy-done.13, bf16[4,64,1280]{2,1,0:T(8,128)(2,1)} %collective-permute-done.16.refs_1_.refs_2_, ...), custom_call_target="tpu_custom_call" | custom-call | flops 1000 | bytes 1000 | tf_op jit(solution)/shard_map/lead_products/pallas_call | solution.py:102
  133.5 2.7 collective-permute-start.24
  136.2 5.5 %collective-permute-done.20.refs_3_.refs_1_ = bf16[4,64,1280]{2,1,0:T(8,128)(2,1)} collective-permute-done((bf16[4,64,1280]{2,1,0:T(8,128)(2,1)}, bf16[4,64,1280]{2,1,0:T(8,128)(2,1)}, u32[]{:S(2)}, u32[]{:S(2)}) %collective-permute-start.20) | collective-permute-done | bytes 655392 | tf_op jit(solution)/shard_map/ppermute | solution.py:540
  141.7 6.5 %collective-permute-done.19.refs_2_.refs_0_ = bf16[4,64,1280]{2,1,0:T(8,128)(2,1)} collective-permute-done((bf16[4,64,1280]{2,1,0:T(8,128)(2,1)}, bf16[4,64,1280]{2,1,0:T(8,128)(2,1)}, u32[]{:S(2)}, u32[]{:S(2)}) %collective-permute-start.19) | collective-permute-done | bytes 655392 | tf_op jit(solution)/shard_map/ppermute | solution.py:540
  148.1 7.1 %rest_products.10 = (bf16[256,1280]{1,0:T(8,128)(2,1)}, bf16[256,1280]{1,0:T(8,128)(2,1)}, bf16[256,1280]{1,0:T(8,128)(2,1)}) custom-call(s32[2]{0:T(128)} %pad_add_fusion.where_ref, bf16[4,64,1280]{2,1,0:T(8,128)(2,1)} %get-tuple-element.68.refs_0_.refs_10_.refs_2_, bf16[4,1280,1280]{2,1,0:T(8,128)(2,1)} %bitcast.36, ...), custom_call_target="tpu_custom_call" | custom-call | flops 199999995904 | bytes 1000 | tf_op jit(solution)/shard_map/rest_products/pallas_call | solution.py:102
  155.3 1.3 collective-permute-start.22
  156.7 3.1 %add_received.12.refs_4_ = bf16[256,1280]{1,0:T(8,128)(2,1)} custom-call(s32[2]{0:T(128)} %pad_add_fusion.where_ref, bf16[256,1280]{1,0:T(8,128)(2,1)} %get-tuple-element.73.kept_ref, bf16[256,1280]{1,0:T(8,128)(2,1)} %collective-permute-done.24.received_ref, bf16[256,1280]{1,0:T(8,128)(2,1)} %get-tuple-element.72.refs_0_), custom_call_target="tpu_custom_call" | custom-call | flops 1000 | bytes 1000 | tf_op jit(solution)/shard_map/add_received/pallas_call | solution.py:149
  159.8 1.3 collective-permute-start.25
  161.1 1.3 collective-permute-start.23
  162.5 5.1 %lead_products.11 = (bf16[4,64,1280]{2,1,0:T(8,128)(2,1)}, bf16[256,1280]{1,0:T(8,128)(2,1)}) custom-call(s32[2]{0:T(128)} %pad_add_fusion.where_ref, bf16[4,64,1280]{2,1,0:T(8,128)(2,1)} %collective-permute-done.19.refs_2_.refs_0_, bf16[4,64,1280]{2,1,0:T(8,128)(2,1)} %collective-permute-done.20.refs_3_.refs_1_, ...), custom_call_target="tpu_custom_call" | custom-call | flops 1000 | bytes 1000 | tf_op jit(solution)/shard_map/lead_products/pallas_call | solution.py:102
  168.2 1.3 collective-permute-start.27
  169.5 6.1 %collective-permute-start.28 = (bf16[256,1280]{1,0:T(8,128)(2,1)}, bf16[256,1280]{1,0:T(8,128)(2,1)}, u32[]{:S(2)}, u32[]{:S(2)}) collective-permute-start(bf16[256,1280]{1,0:T(8,128)(2,1)} %get-tuple-element.77), channel_id=1, source_target_pairs={{8,9},{9,8},{10,11},{11,10},{12,13},{13,12},{14,15},{15,14}} | collective-permute-start | bytes 1966088 | tf_op jit(solution)/shard_map/ppermute | solution.py:540
  176.9 1.7 collective-permute-start.30
  180.6 7.1 %rest_products.11 = (bf16[256,1280]{1,0:T(8,128)(2,1)}, bf16[256,1280]{1,0:T(8,128)(2,1)}, bf16[256,1280]{1,0:T(8,128)(2,1)}) custom-call(s32[2]{0:T(128)} %pad_add_fusion.where_ref, bf16[4,64,1280]{2,1,0:T(8,128)(2,1)} %get-tuple-element.75.refs_0_.refs_1_.refs_11_.refs_3_, bf16[4,1280,1280]{2,1,0:T(8,128)(2,1)} %bitcast.38, ...), custom_call_target="tpu_custom_call" | custom-call | flops 199999995904 | bytes 1000 | tf_op jit(solution)/shard_map/rest_products/pallas_call | solution.py:102
  188.6 3.1 %add_received.13.refs_4_ = bf16[256,1280]{1,0:T(8,128)(2,1)} custom-call(s32[2]{0:T(128)} %pad_add_fusion.where_ref, bf16[256,1280]{1,0:T(8,128)(2,1)} %get-tuple-element.76.kept_ref, bf16[256,1280]{1,0:T(8,128)(2,1)} %collective-permute-done.28.received_ref, bf16[256,1280]{1,0:T(8,128)(2,1)} %get-tuple-element.78.refs_0_), custom_call_target="tpu_custom_call" | custom-call | flops 1000 | bytes 1000 | tf_op jit(solution)/shard_map/add_received/pallas_call | solution.py:149
  194.1 1.3 collective-permute-start.34
  195.5 1.3 collective-permute-start.36
  196.8 1.3 collective-permute-start.35
  198.2 1.0 copy-done.3
  199.2 1.1 copy-done.4
  201.1 1.5 collective-permute-start.40
  202.6 3.0 %pick.3 = bf16[2,4,64,1280]{3,2,1,0:T(8,128)(2,1)} custom-call(s32[2]{0:T(128)} %pad_add_fusion.where_ref, bf16[4,64,1280]{2,1,0:T(8,128)(2,1)} %get-tuple-element.68.refs_0_.refs_10_.refs_2_, bf16[4,64,1280]{2,1,0:T(8,128)(2,1)} %get-tuple-element.75.refs_0_.refs_1_.refs_11_.refs_3_, bf16[4,64,1280]{2,1,0:T(8,128)(2,1)} %get-tuple-element.88.refs_2_.refs_8_.refs_0_), custom_call_target="tpu_custom_call" | custom-call | flops 1000 | bytes 1000 | tf_op jit(solution)/shard_map/pick/pallas_call | solution.py:364
  205.6 1.5 collective-permute-start.32
  207.2 1.5 collective-permute-start.33
  208.7 3.1 %collective-permute-start.41 = (bf16[2,4,64,1280]{3,2,1,0:T(8,128)(2,1)}, bf16[2,4,64,1280]{3,2,1,0:T(8,128)(2,1)}, u32[]{:S(2)}, u32[]{:S(2)}) collective-permute-start(bf16[2,4,64,1280]{3,2,1,0:T(8,128)(2,1)} %pick.3), channel_id=1, source_target_pairs={{8,12},{9,13},{10,14},{11,15},{12,8},{13,9},{14,10},{15,11}} | collective-permute-start | bytes 3932168 | tf_op jit(solution)/shard_map/ppermute | solution.py:540
  215.7 1.7 collective-permute-start.43
  218.2 1.5 collective-permute-start.38
  219.7 1.5 collective-permute-start.44
  221.2 1.5 collective-permute-start.37
  222.7 6.4 %collective-permute-done.41.refs_4_.refs_18_ = bf16[2,4,64,1280]{3,2,1,0:T(8,128)(2,1)} collective-permute-done((bf16[2,4,64,1280]{3,2,1,0:T(8,128)(2,1)}, bf16[2,4,64,1280]{3,2,1,0:T(8,128)(2,1)}, u32[]{:S(2)}, u32[]{:S(2)}) %collective-permute-start.41) | collective-permute-done | bytes 1310752 | tf_op jit(solution)/shard_map/ppermute | solution.py:540
  231.1 3.3 %cut_shards.1 = (bf16[128,1280]{1,0:T(8,128)(2,1)}, bf16[128,1280]{1,0:T(8,128)(2,1)}, bf16[128,1280]{1,0:T(8,128)(2,1)}, bf16[128,1280]{1,0:T(8,128)(2,1)}) custom-call(s32[2]{0:T(128)} %pad_add_fusion.where_ref, bf16[4,64,1280]{2,1,0:T(8,128)(2,1)} %get-tuple-element.88.refs_2_.refs_8_.refs_0_, bf16[4,64,1280]{2,1,0:T(8,128)(2,1)} %get-tuple-element.89.refs_9_.refs_1_, ...), custom_call_target="tpu_custom_call" | custom-call | flops 1000 | bytes 1000 | tf_op jit(solution)/shard_map/cut_shards/pallas_call | solution.py:329
  234.5 21.4 %collective-permute-start.45 = (bf16[128,1280]{1,0:T(8,128)(2,1)}, bf16[128,1280]{1,0:T(8,128)(2,1)S(1)}, u32[]{:S(2)}, u32[]{:S(2)}) collective-permute-start(bf16[128,1280]{1,0:T(8,128)(2,1)} %get-tuple-element.90), channel_id=1, source_target_pairs={{0,8},{1,9},{2,10},{3,11},{4,12},{5,13},{6,14},{7,15},{8,16},{9,17... | collective-permute-start | bytes 983048 | tf_op jit(solution)/shard_map/ppermute | solution.py:540
  255.9 3.4 %collective-permute-start.46 = (bf16[128,1280]{1,0:T(8,128)(2,1)}, bf16[128,1280]{1,0:T(8,128)(2,1)S(1)}, u32[]{:S(2)}, u32[]{:S(2)}) collective-permute-start(bf16[128,1280]{1,0:T(8,128)(2,1)} %get-tuple-element.91), channel_id=1, source_target_pairs={{0,9},{1,8},{2,11},{3,10},{4,13},{5,12},{6,15},{7,14},{8,17},{9,16... | collective-permute-start | bytes 983048 | tf_op jit(solution)/shard_map/ppermute | solution.py:540
  259.2 10.5 %collective-permute-start.47 = (bf16[128,1280]{1,0:T(8,128)(2,1)}, bf16[128,1280]{1,0:T(8,128)(2,1)S(1)}, u32[]{:S(2)}, u32[]{:S(2)}) collective-permute-start(bf16[128,1280]{1,0:T(8,128)(2,1)} %get-tuple-element.92), channel_id=1, source_target_pairs={{0,10},{1,11},{2,8},{3,9},{4,14},{5,15},{6,12},{7,13},{8,18},{9,19... | collective-permute-start | bytes 983048 | tf_op jit(solution)/shard_map/ppermute | solution.py:540
  269.8 3.2 %collective-permute-start.48 = (bf16[128,1280]{1,0:T(8,128)(2,1)}, bf16[128,1280]{1,0:T(8,128)(2,1)S(1)}, u32[]{:S(2)}, u32[]{:S(2)}) collective-permute-start(bf16[128,1280]{1,0:T(8,128)(2,1)} %get-tuple-element.93), channel_id=1, source_target_pairs={{0,11},{1,10},{2,9},{3,8},{4,15},{5,14},{6,13},{7,12},{8,19},{9,18... | collective-permute-start | bytes 983048 | tf_op jit(solution)/shard_map/ppermute | solution.py:540
  273.0 14.7 %weight_products.1.refs_6_ = f32[2560,1280]{1,0:T(8,128)} custom-call(s32[2]{0:T(128)} %pad_add_fusion.where_ref, bf16[256,2560]{1,0:T(8,128)(2,1)} %join.2.refs_0_, bf16[256,2560]{1,0:T(8,128)(2,1)} %collective-permute-done.8.refs_4_.refs_1_, bf16[256,2560]{1,0:T(8,128)(2,1)} %collective-permute-done.9.refs_5_.refs_2_, ...), custom_call_target="tpu_custom_call" | custom-call | flops 1000 | bytes 1000 | tf_op jit(solution)/shard_map/weight_products/pallas_call | solution.py:502
  287.8 2.4 first_inputs.1.sums_ref
  290.2 7.4 %collective-permute-done.47.refs_2_ = bf16[128,1280]{1,0:T(8,128)(2,1)S(1)} collective-permute-done((bf16[128,1280]{1,0:T(8,128)(2,1)}, bf16[128,1280]{1,0:T(8,128)(2,1)S(1)}, u32[]{:S(2)}, u32[]{:S(2)}) %collective-permute-start.47) | collective-permute-done | bytes 327712 | tf_op jit(solution)/shard_map/ppermute | solution.py:540
  297.6 1.8 place_inputs.1
  (125 shorter events, 31.1 us)
Async XLA Ops:
  0.6 2.3 copy-start.7
  3.0 15.6 %collective-permute-start.7 = (bf16[128,2560]{1,0:T(8,128)(2,1)S(1)}, bf16[128,2560]{1,0:T(8,128)(2,1)S(1)}, u32[]{:S(2)}, u32[]{:S(2)}) collective-permute-start(bf16[128,2560]{1,0:T(8,128)(2,1)S(1)} %get-tuple-element.94), channel_id=1, source_target_pairs={{0,4},{1,5},{2,6},{3,7},{4,0},{5,1},{6,2},{7,3},{8,12},{9,13},{10,... | collective-permute-start | bytes 1966088 | tf_op jit(solution)/shard_map/ppermute | solution.py:540
  4.0 2.6 collective-permute-start.2
  4.6 2.0 collective-permute-start
  5.3 1.3 collective-permute-start.1
  10.7 21.4 %collective-permute-start.5 = (bf16[256,1280]{1,0:T(8,128)(2,1)}, bf16[256,1280]{1,0:T(8,128)(2,1)}, u32[]{:S(2)}, u32[]{:S(2)}) collective-permute-start(bf16[256,1280]{1,0:T(8,128)(2,1)} %get-tuple-element.53), channel_id=1, source_target_pairs={{24,25},{25,24},{26,27},{27,26},{28,29},{29,28},{30,31},{31,30}} | collective-permute-start | bytes 1966088 | tf_op jit(solution)/shard_map/ppermute | solution.py:540
  22.4 60.9 %collective-permute-start.9 = (bf16[256,2560]{1,0:T(8,128)(2,1)}, bf16[256,2560]{1,0:T(8,128)(2,1)}, u32[]{:S(2)}, u32[]{:S(2)}) collective-permute-start(bf16[256,2560]{1,0:T(8,128)(2,1)} %join.2.refs_0_), channel_id=1, source_target_pairs={{0,2},{1,3},{2,0},{3,1},{4,6},{5,7},{6,4},{7,5},{8,10},{9,11},{10,... | collective-permute-start | bytes 3932168 | tf_op jit(solution)/shard_map/ppermute | solution.py:540
  26.7 56.6 %collective-permute-start.8 = (bf16[256,2560]{1,0:T(8,128)(2,1)}, bf16[256,2560]{1,0:T(8,128)(2,1)}, u32[]{:S(2)}, u32[]{:S(2)}) collective-permute-start(bf16[256,2560]{1,0:T(8,128)(2,1)} %join.2.refs_0_), channel_id=1, source_target_pairs={{0,1},{1,0},{2,3},{3,2},{4,5},{5,4},{6,7},{7,6},{8,9},{9,8},{10,11... | collective-permute-start | bytes 3932168 | tf_op jit(solution)/shard_map/ppermute | solution.py:540
  30.6 4.4 %collective-permute-start.3 = (bf16[4,64,1280]{2,1,0:T(8,128)(2,1)}, bf16[4,64,1280]{2,1,0:T(8,128)(2,1)S(1)}, u32[]{:S(2)}, u32[]{:S(2)}) collective-permute-start(bf16[4,64,1280]{2,1,0:T(8,128)(2,1)} %bitcast.59), channel_id=1, source_target_pairs={{24,16},{25,17},{26,18},{27,19},{28,20},{29,21},{30,22},{31,23}} | collective-permute-start | bytes 1966088 | tf_op jit(solution)/shard_map/ppermute | solution.py:540
  31.3 5.2 %collective-permute-start.4 = (bf16[4,64,1280]{2,1,0:T(8,128)(2,1)}, bf16[4,64,1280]{2,1,0:T(8,128)(2,1)S(1)}, u32[]{:S(2)}, u32[]{:S(2)}) collective-permute-start(bf16[4,64,1280]{2,1,0:T(8,128)(2,1)} %bitcast.51), channel_id=1, source_target_pairs={{24,17},{25,16},{26,19},{27,18},{28,21},{29,20},{30,23},{31,22}} | collective-permute-start | bytes 1966088 | tf_op jit(solution)/shard_map/ppermute | solution.py:540
  33.5 54.2 %collective-permute-start.10 = (bf16[256,1280]{1,0:T(8,128)(2,1)}, bf16[256,1280]{1,0:T(8,128)(2,1)}, u32[]{:S(2)}, u32[]{:S(2)}) collective-permute-start(bf16[256,1280]{1,0:T(8,128)(2,1)} %get-tuple-element.57), channel_id=1, source_target_pairs={{24,25},{25,24},{26,27},{27,26},{28,29},{29,28},{30,31},{31,30}} | collective-permute-start | bytes 1966088 | tf_op jit(solution)/shard_map/ppermute | solution.py:540
  35.0 48.3 %copy-start.12 = (bf16[4,64,1280]{2,1,0:T(8,128)(2,1)}, bf16[4,64,1280]{2,1,0:T(8,128)(2,1)S(1)}, u32[]{:S(2)}) copy-start(bf16[4,64,1280]{2,1,0:T(8,128)(2,1)S(1)} %collective-permute-done.3.refs_2_.refs_0_) | copy-start | bytes 1966084
  35.0 52.1 %collective-permute-start.6 = (bf16[4,64,1280]{2,1,0:T(8,128)(2,1)}, bf16[4,64,1280]{2,1,0:T(8,128)(2,1)}, u32[]{:S(2)}, u32[]{:S(2)}) collective-permute-start(bf16[4,64,1280]{2,1,0:T(8,128)(2,1)} %bitcast.5), channel_id=1, source_target_pairs={{24,18},{25,19},{26,16},{27,17},{28,22},{29,23},{30,20},{31,21}} | collective-permute-start | bytes 1966088 | tf_op jit(solution)/shard_map/ppermute | solution.py:540
  36.6 46.8 %copy-start.14 = (bf16[4,64,1280]{2,1,0:T(8,128)(2,1)}, bf16[4,64,1280]{2,1,0:T(8,128)(2,1)S(1)}, u32[]{:S(2)}) copy-start(bf16[4,64,1280]{2,1,0:T(8,128)(2,1)S(1)} %collective-permute-done.4.refs_3_.refs_1_) | copy-start | bytes 1966084
  84.1 8.2 %collective-permute-start.12 = (bf16[4,64,1280]{2,1,0:T(8,128)(2,1)}, bf16[4,64,1280]{2,1,0:T(8,128)(2,1)}, u32[]{:S(2)}, u32[]{:S(2)}) collective-permute-start(bf16[4,64,1280]{2,1,0:T(8,128)(2,1)} %bitcast.58), channel_id=1, source_target_pairs={{24,17},{25,16},{26,19},{27,18},{28,21},{29,20},{30,23},{31,22}} | collective-permute-start | bytes 1966088 | tf_op jit(solution)/shard_map/ppermute | solution.py:540
  85.6 6.7 %collective-permute-start.11 = (bf16[4,64,1280]{2,1,0:T(8,128)(2,1)}, bf16[4,64,1280]{2,1,0:T(8,128)(2,1)}, u32[]{:S(2)}, u32[]{:S(2)}) collective-permute-start(bf16[4,64,1280]{2,1,0:T(8,128)(2,1)} %bitcast.55), channel_id=1, source_target_pairs={{24,16},{25,17},{26,18},{27,19},{28,20},{29,21},{30,22},{31,23}} | collective-permute-start | bytes 1966088 | tf_op jit(solution)/shard_map/ppermute | solution.py:540
  88.4 12.6 %collective-permute-start.17 = (bf16[4,64,1280]{2,1,0:T(8,128)(2,1)}, bf16[4,64,1280]{2,1,0:T(8,128)(2,1)}, u32[]{:S(2)}, u32[]{:S(2)}) collective-permute-start(bf16[4,64,1280]{2,1,0:T(8,128)(2,1)} %bitcast.43), channel_id=1, source_target_pairs={{24,18},{25,19},{26,16},{27,17},{28,22},{29,23},{30,20},{31,21}} | collective-permute-start | bytes 1966088 | tf_op jit(solution)/shard_map/ppermute | solution.py:540
  90.7 8.3 %collective-permute-start.15 = (bf16[256,1280]{1,0:T(8,128)(2,1)}, bf16[256,1280]{1,0:T(8,128)(2,1)}, u32[]{:S(2)}, u32[]{:S(2)}) collective-permute-start(bf16[256,1280]{1,0:T(8,128)(2,1)} %get-tuple-element.64), channel_id=1, source_target_pairs={{16,17},{17,16},{18,19},{19,18},{20,21},{21,20},{22,23},{23,22}} | collective-permute-start | bytes 1966088 | tf_op jit(solution)/shard_map/ppermute | solution.py:540
  93.0 22.6 %collective-permute-start.13 = (bf16[4,64,1280]{2,1,0:T(8,128)(2,1)}, bf16[4,64,1280]{2,1,0:T(8,128)(2,1)S(1)}, u32[]{:S(2)}, u32[]{:S(2)}) collective-permute-start(bf16[4,64,1280]{2,1,0:T(8,128)(2,1)} %bitcast.57), channel_id=1, source_target_pairs={{16,8},{17,9},{18,10},{19,11},{20,12},{21,13},{22,14},{23,15}} | collective-permute-start | bytes 1966088 | tf_op jit(solution)/shard_map/ppermute | solution.py:540
  94.3 21.4 %collective-permute-start.14 = (bf16[4,64,1280]{2,1,0:T(8,128)(2,1)}, bf16[4,64,1280]{2,1,0:T(8,128)(2,1)S(1)}, u32[]{:S(2)}, u32[]{:S(2)}) collective-permute-start(bf16[4,64,1280]{2,1,0:T(8,128)(2,1)} %bitcast.50), channel_id=1, source_target_pairs={{16,9},{17,8},{18,11},{19,10},{20,13},{21,12},{22,15},{23,14}} | collective-permute-start | bytes 1966088 | tf_op jit(solution)/shard_map/ppermute | solution.py:540
  95.6 40.6 %collective-permute-start.21 = (bf16[256,2560]{1,0:T(8,128)(2,1)}, bf16[256,2560]{1,0:T(8,128)(2,1)}, u32[]{:S(2)}, u32[]{:S(2)}) collective-permute-start(bf16[256,2560]{1,0:T(8,128)(2,1)} %collective-permute-done.9.refs_5_.refs_2_), channel_id=1, source_target_pairs={{0,1},{1,0},{2,3},{3,2},{4,5},{5,4},{6,7},{7,6},{8,9},{9,8},{10,11... | collective-permute-start | bytes 3932168 | tf_op jit(solution)/shard_map/ppermute | solution.py:540
  99.8 26.0 %collective-permute-start.16 = (bf16[4,64,1280]{2,1,0:T(8,128)(2,1)}, bf16[4,64,1280]{2,1,0:T(8,128)(2,1)}, u32[]{:S(2)}, u32[]{:S(2)}) collective-permute-start(bf16[4,64,1280]{2,1,0:T(8,128)(2,1)} %bitcast.46), channel_id=1, source_target_pairs={{16,10},{17,11},{18,8},{19,9},{20,14},{21,15},{22,12},{23,13}} | collective-permute-start | bytes 1966088 | tf_op jit(solution)/shard_map/ppermute | solution.py:540
  101.8 24.5 %collective-permute-start.18 = (bf16[256,1280]{1,0:T(8,128)(2,1)}, bf16[256,1280]{1,0:T(8,128)(2,1)}, u32[]{:S(2)}, u32[]{:S(2)}) collective-permute-start(bf16[256,1280]{1,0:T(8,128)(2,1)} %get-tuple-element.67), channel_id=1, source_target_pairs={{16,17},{17,16},{18,19},{19,18},{20,21},{21,20},{22,23},{23,22}} | collective-permute-start | bytes 1966088 | tf_op jit(solution)/shard_map/ppermute | solution.py:540
  117.5 24.2 %collective-permute-start.20 = (bf16[4,64,1280]{2,1,0:T(8,128)(2,1)}, bf16[4,64,1280]{2,1,0:T(8,128)(2,1)}, u32[]{:S(2)}, u32[]{:S(2)}) collective-permute-start(bf16[4,64,1280]{2,1,0:T(8,128)(2,1)} %bitcast.56), channel_id=1, source_target_pairs={{16,9},{17,8},{18,11},{19,10},{20,13},{21,12},{22,15},{23,14}} | collective-permute-start | bytes 1966088 | tf_op jit(solution)/shard_map/ppermute | solution.py:540
  118.8 29.4 %collective-permute-start.19 = (bf16[4,64,1280]{2,1,0:T(8,128)(2,1)}, bf16[4,64,1280]{2,1,0:T(8,128)(2,1)}, u32[]{:S(2)}, u32[]{:S(2)}) collective-permute-start(bf16[4,64,1280]{2,1,0:T(8,128)(2,1)} %bitcast.54), channel_id=1, source_target_pairs={{16,8},{17,9},{18,10},{19,11},{20,12},{21,13},{22,14},{23,15}} | collective-permute-start | bytes 1966088 | tf_op jit(solution)/shard_map/ppermute | solution.py:540
  127.0 35.4 %collective-permute-start.26 = (bf16[4,64,1280]{2,1,0:T(8,128)(2,1)}, bf16[4,64,1280]{2,1,0:T(8,128)(2,1)}, u32[]{:S(2)}, u32[]{:S(2)}) collective-permute-start(bf16[4,64,1280]{2,1,0:T(8,128)(2,1)} %bitcast.44), channel_id=1, source_target_pairs={{16,10},{17,11},{18,8},{19,9},{20,14},{21,15},{22,12},{23,13}} | collective-permute-start | bytes 1966088 | tf_op jit(solution)/shard_map/ppermute | solution.py:540
  133.5 23.2 %collective-permute-start.24 = (bf16[256,1280]{1,0:T(8,128)(2,1)}, bf16[256,1280]{1,0:T(8,128)(2,1)}, u32[]{:S(2)}, u32[]{:S(2)}) collective-permute-start(bf16[256,1280]{1,0:T(8,128)(2,1)} %get-tuple-element.74), channel_id=1, source_target_pairs={{8,9},{9,8},{10,11},{11,10},{12,13},{13,12},{14,15},{15,14}} | collective-permute-start | bytes 1966088 | tf_op jit(solution)/shard_map/ppermute | solution.py:540
  155.3 23.4 %collective-permute-start.22 = (bf16[4,64,1280]{2,1,0:T(8,128)(2,1)}, bf16[4,64,1280]{2,1,0:T(8,128)(2,1)S(1)}, u32[]{:S(2)}, u32[]{:S(2)}) collective-permute-start(bf16[4,64,1280]{2,1,0:T(8,128)(2,1)} %bitcast.53), channel_id=1, source_target_pairs={{8,0},{9,1},{10,2},{11,3},{12,4},{13,5},{14,6},{15,7}} | collective-permute-start | bytes 1966088 | tf_op jit(solution)/shard_map/ppermute | solution.py:540
  156.6 4.4 %copy-start.20 = (bf16[256,1280]{1,0:T(8,128)(2,1)S(1)}, bf16[256,1280]{1,0:T(8,128)(2,1)}, u32[]{:S(2)}) copy-start(bf16[256,1280]{1,0:T(8,128)(2,1)} %get-tuple-element.72.refs_0_) | copy-start | bytes 1966084
  159.8 18.9 %collective-permute-start.25 = (bf16[4,64,1280]{2,1,0:T(8,128)(2,1)}, bf16[4,64,1280]{2,1,0:T(8,128)(2,1)S(1)}, u32[]{:S(2)}, u32[]{:S(2)}) collective-permute-start(bf16[4,64,1280]{2,1,0:T(8,128)(2,1)} %bitcast.45), channel_id=1, source_target_pairs={{8,2},{9,3},{10,0},{11,1},{12,6},{13,7},{14,4},{15,5}} | collective-permute-start | bytes 1966088 | tf_op jit(solution)/shard_map/ppermute | solution.py:540
  161.1 17.6 %collective-permute-start.23 = (bf16[4,64,1280]{2,1,0:T(8,128)(2,1)S(1)}, bf16[4,64,1280]{2,1,0:T(8,128)(2,1)S(1)}, u32[]{:S(2)}, u32[]{:S(2)}) collective-permute-start(bf16[4,64,1280]{2,1,0:T(8,128)(2,1)S(1)} %bitcast.49), channel_id=1, source_target_pairs={{8,1},{9,0},{10,3},{11,2},{12,5},{13,4},{14,7},{15,6}} | collective-permute-start | bytes 1966088 | tf_op jit(solution)/shard_map/ppermute | solution.py:540
  168.2 7.4 %collective-permute-start.27 = (f32[8,128]{1,0:T(8,128)}, f32[8,128]{1,0:T(8,128)S(1)}, u32[]{:S(2)}, u32[]{:S(2)}) collective-permute-start(f32[8,128]{1,0:T(8,128)} %mark.7), channel_id=1, source_target_pairs={{8,16},{9,17},{10,18},{11,19},{12,20},{13,21},{14,22},{15,23},{16,... | collective-permute-start | bytes 12296 | tf_op jit(solution)/shard_map/ppermute | solution.py:540
  169.5 19.1 %collective-permute-start.28 = (bf16[256,1280]{1,0:T(8,128)(2,1)}, bf16[256,1280]{1,0:T(8,128)(2,1)}, u32[]{:S(2)}, u32[]{:S(2)}) collective-permute-start(bf16[256,1280]{1,0:T(8,128)(2,1)} %get-tuple-element.77), channel_id=1, source_target_pairs={{8,9},{9,8},{10,11},{11,10},{12,13},{13,12},{14,15},{15,14}} | collective-permute-start | bytes 1966088 | tf_op jit(solution)/shard_map/ppermute | solution.py:540
  176.9 19.9 %collective-permute-start.30 = (bf16[256,2560]{1,0:T(8,128)(2,1)}, bf16[256,2560]{1,0:T(8,128)(2,1)}, u32[]{:S(2)}, u32[]{:S(2)}) collective-permute-start(bf16[256,2560]{1,0:T(8,128)(2,1)} %join.3.refs_4_), channel_id=1, source_target_pairs={{16,18},{17,19},{18,16},{19,17},{20,22},{21,23},{22,20},{23,21},{2... | collective-permute-start | bytes 3932168 | tf_op jit(solution)/shard_map/ppermute | solution.py:540
  178.7 1.1 copy-start.9
  188.6 3.1 %copy-start.5 = (bf16[256,2560]{1,0:T(8,128)(2,1)S(1)}, bf16[256,2560]{1,0:T(8,128)(2,1)}, u32[]{:S(2)}) copy-start(bf16[256,2560]{1,0:T(8,128)(2,1)} %join.3.refs_4_) | copy-start | bytes 3932164
  191.7 2.4 copy-start.25
  191.8 3.7 %copy-start.2 = (bf16[256,1280]{1,0:T(8,128)(2,1)S(1)}, bf16[256,1280]{1,0:T(8,128)(2,1)}, u32[]{:S(2)}) copy-start(bf16[256,1280]{1,0:T(8,128)(2,1)} %add_received.13.refs_4_) | copy-start | bytes 1966084
  191.8 5.1 %copy-start.19 = (bf16[256,1280]{1,0:T(8,128)(2,1)S(1)}, bf16[256,1280]{1,0:T(8,128)(2,1)}, u32[]{:S(2)}) copy-start(bf16[256,1280]{1,0:T(8,128)(2,1)} %get-tuple-element.78.refs_0_) | copy-start | bytes 1966084
  191.8 6.4 %collective-permute-start.29 = (bf16[256,2560]{1,0:T(8,128)(2,1)S(1)}, bf16[256,2560]{1,0:T(8,128)(2,1)S(1)}, u32[]{:S(2)}, u32[]{:S(2)}) collective-permute-start(bf16[256,2560]{1,0:T(8,128)(2,1)S(1)} %copy-done.5), channel_id=1, source_target_pairs={{16,17},{17,16},{18,19},{19,18},{20,21},{21,20},{22,23},{23,22},{2... | collective-permute-start | bytes 3932168 | tf_op jit(solution)/shard_map/ppermute | solution.py:540
  193.4 4.8 %collective-permute-start.31 = (bf16[2,4,64,1280]{3,2,1,0:T(8,128)(2,1)}, bf16[2,4,64,1280]{3,2,1,0:T(8,128)(2,1)S(1)}, u32[]{:S(2)}, u32[]{:S(2)}) collective-permute-start(bf16[2,4,64,1280]{3,2,1,0:T(8,128)(2,1)} %pick.2), channel_id=1, source_target_pairs={{16,20},{17,21},{18,22},{19,23},{20,16},{21,17},{22,18},{23,19},{2... | collective-permute-start | bytes 3932168 | tf_op jit(solution)/shard_map/ppermute | solution.py:540
  194.1 13.0 %collective-permute-start.34 = (bf16[4,64,1280]{2,1,0:T(8,128)(2,1)S(1)}, bf16[4,64,1280]{2,1,0:T(8,128)(2,1)S(1)}, u32[]{:S(2)}, u32[]{:S(2)}) collective-permute-start(bf16[4,64,1280]{2,1,0:T(8,128)(2,1)S(1)} %bitcast.52), channel_id=1, source_target_pairs={{8,0},{9,1},{10,2},{11,3},{12,4},{13,5},{14,6},{15,7}} | collective-permute-start | bytes 1966088 | tf_op jit(solution)/shard_map/ppermute | solution.py:540
  195.5 13.2 %collective-permute-start.36 = (bf16[4,64,1280]{2,1,0:T(8,128)(2,1)S(1)}, bf16[4,64,1280]{2,1,0:T(8,128)(2,1)S(1)}, u32[]{:S(2)}, u32[]{:S(2)}) collective-permute-start(bf16[4,64,1280]{2,1,0:T(8,128)(2,1)S(1)} %bitcast.42), channel_id=1, source_target_pairs={{8,2},{9,3},{10,0},{11,1},{12,6},{13,7},{14,4},{15,5}} | collective-permute-start | bytes 1966088 | tf_op jit(solution)/shard_map/ppermute | solution.py:540
  196.8 15.9 %collective-permute-start.35 = (bf16[4,64,1280]{2,1,0:T(8,128)(2,1)S(1)}, bf16[4,64,1280]{2,1,0:T(8,128)(2,1)S(1)}, u32[]{:S(2)}, u32[]{:S(2)}) collective-permute-start(bf16[4,64,1280]{2,1,0:T(8,128)(2,1)S(1)} %bitcast.48), channel_id=1, source_target_pairs={{8,1},{9,0},{10,3},{11,2},{12,5},{13,4},{14,7},{15,6}} | collective-permute-start | bytes 1966088 | tf_op jit(solution)/shard_map/ppermute | solution.py:540
  199.2 1.1 copy-start.4
  201.1 18.6 %collective-permute-start.40 = (bf16[4,64,1280]{2,1,0:T(8,128)(2,1)}, bf16[4,64,1280]{2,1,0:T(8,128)(2,1)}, u32[]{:S(2)}, u32[]{:S(2)}) collective-permute-start(bf16[4,64,1280]{2,1,0:T(8,128)(2,1)} %get-tuple-element.88.refs_2_.refs_8_.refs_0_), channel_id=1, source_target_pairs={{0,4},{1,5},{2,6},{3,7},{4,0},{5,1},{6,2},{7,3}} | collective-permute-start | bytes 1966088 | tf_op jit(solution)/shard_map/ppermute | solution.py:540
  205.6 12.5 %collective-permute-start.32 = (bf16[64,5120]{1,0:T(8,128)(2,1)}, bf16[64,5120]{1,0:T(8,128)(2,1)}, u32[]{:S(2)}, u32[]{:S(2)}) collective-permute-start(bf16[64,5120]{1,0:T(8,128)(2,1)} %get-tuple-element.80), channel_id=1, source_target_pairs={{0,1},{1,0},{2,3},{3,2},{4,5},{5,4},{6,7},{7,6}} | collective-permute-start | bytes 1966088 | tf_op jit(solution)/shard_map/ppermute | solution.py:540
  207.2 5.6 %copy-start.15 = (bf16[4,64,1280]{2,1,0:T(8,128)(2,1)}, bf16[4,64,1280]{2,1,0:T(8,128)(2,1)S(1)}, u32[]{:S(2)}) copy-start(bf16[4,64,1280]{2,1,0:T(8,128)(2,1)S(1)} %collective-permute-done.34.refs_1_.refs_0_) | copy-start | bytes 1966084
  207.2 8.5 %collective-permute-start.33 = (bf16[64,5120]{1,0:T(8,128)(2,1)}, bf16[64,5120]{1,0:T(8,128)(2,1)}, u32[]{:S(2)}, u32[]{:S(2)}) collective-permute-start(bf16[64,5120]{1,0:T(8,128)(2,1)} %get-tuple-element.82), channel_id=1, source_target_pairs={{0,1},{1,0},{2,3},{3,2},{4,5},{5,4},{6,7},{7,6}} | collective-permute-start | bytes 1966088 | tf_op jit(solution)/shard_map/ppermute | solution.py:540
  208.7 4.1 %copy-start.16 = (bf16[4,64,1280]{2,1,0:T(8,128)(2,1)}, bf16[4,64,1280]{2,1,0:T(8,128)(2,1)S(1)}, u32[]{:S(2)}) copy-start(bf16[4,64,1280]{2,1,0:T(8,128)(2,1)S(1)} %collective-permute-done.36.refs_3_.refs_2_) | copy-start | bytes 1966084
  208.7 20.4 %collective-permute-start.41 = (bf16[2,4,64,1280]{3,2,1,0:T(8,128)(2,1)}, bf16[2,4,64,1280]{3,2,1,0:T(8,128)(2,1)}, u32[]{:S(2)}, u32[]{:S(2)}) collective-permute-start(bf16[2,4,64,1280]{3,2,1,0:T(8,128)(2,1)} %pick.3), channel_id=1, source_target_pairs={{8,12},{9,13},{10,14},{11,15},{12,8},{13,9},{14,10},{15,11}} | collective-permute-start | bytes 3932168 | tf_op jit(solution)/shard_map/ppermute | solution.py:540
  215.0 6.2 %collective-permute-start.39 = (bf16[64,5120]{1,0:T(8,128)(2,1)}, bf16[64,5120]{1,0:T(8,128)(2,1)S(1)}, u32[]{:S(2)}, u32[]{:S(2)}) collective-permute-start(bf16[64,5120]{1,0:T(8,128)(2,1)} %get-tuple-element.87), channel_id=1, source_target_pairs={{0,1},{1,0},{2,3},{3,2},{4,5},{5,4},{6,7},{7,6}} | collective-permute-start | bytes 1966088 | tf_op jit(solution)/shard_map/ppermute | solution.py:540
  215.7 43.5 %collective-permute-start.43 = (bf16[256,2560]{1,0:T(8,128)(2,1)}, bf16[256,2560]{1,0:T(8,128)(2,1)}, u32[]{:S(2)}, u32[]{:S(2)}) collective-permute-start(bf16[256,2560]{1,0:T(8,128)(2,1)} %collective-permute-done.30.refs_6_), channel_id=1, source_target_pairs={{16,17},{17,16},{18,19},{19,18},{20,21},{21,20},{22,23},{23,22},{2... | collective-permute-start | bytes 3932168 | tf_op jit(solution)/shard_map/ppermute | solution.py:540
  218.2 13.0 %collective-permute-start.38 = (bf16[64,5120]{1,0:T(8,128)(2,1)}, bf16[64,5120]{1,0:T(8,128)(2,1)}, u32[]{:S(2)}, u32[]{:S(2)}) collective-permute-start(bf16[64,5120]{1,0:T(8,128)(2,1)} %get-tuple-element.86), channel_id=1, source_target_pairs={{0,1},{1,0},{2,3},{3,2},{4,5},{5,4},{6,7},{7,6}} | collective-permute-start | bytes 1966088 | tf_op jit(solution)/shard_map/ppermute | solution.py:540
  219.7 11.5 %collective-permute-start.44 = (bf16[4,64,1280]{2,1,0:T(8,128)(2,1)}, bf16[4,64,1280]{2,1,0:T(8,128)(2,1)}, u32[]{:S(2)}, u32[]{:S(2)}) collective-permute-start(bf16[4,64,1280]{2,1,0:T(8,128)(2,1)} %get-tuple-element.89.refs_9_.refs_1_), channel_id=1, source_target_pairs={{0,4},{1,5},{2,6},{3,7},{4,0},{5,1},{6,2},{7,3}} | collective-permute-start | bytes 1966088 | tf_op jit(solution)/shard_map/ppermute | solution.py:540
  221.2 7.9 %copy-start.18 = (bf16[64,5120]{1,0:T(8,128)(2,1)}, bf16[64,5120]{1,0:T(8,128)(2,1)S(1)}, u32[]{:S(2)}) copy-start(bf16[64,5120]{1,0:T(8,128)(2,1)S(1)} %collective-permute-done.39.refs_1_.received_ref) | copy-start | bytes 1966084
  221.2 48.6 %collective-permute-start.37 = (bf16[64,5120]{1,0:T(8,128)(2,1)}, bf16[64,5120]{1,0:T(8,128)(2,1)}, u32[]{:S(2)}, u32[]{:S(2)}) collective-permute-start(bf16[64,5120]{1,0:T(8,128)(2,1)} %add_received.14.refs_0_), channel_id=1, source_target_pairs={{0,2},{1,3},{2,0},{3,1},{4,6},{5,7},{6,4},{7,5}} | collective-permute-start | bytes 1966088 | tf_op jit(solution)/shard_map/ppermute | solution.py:540
  230.4 57.3 %collective-permute-start.42 = (bf16[64,5120]{1,0:T(8,128)(2,1)}, bf16[64,5120]{1,0:T(8,128)(2,1)S(1)}, u32[]{:S(2)}, u32[]{:S(2)}) collective-permute-start(bf16[64,5120]{1,0:T(8,128)(2,1)} %add_received.15.refs_6_), channel_id=1, source_target_pairs={{0,2},{1,3},{2,0},{3,1},{4,6},{5,7},{6,4},{7,5}} | collective-permute-start | bytes 1966088 | tf_op jit(solution)/shard_map/ppermute | solution.py:540
  234.5 55.7 %collective-permute-start.45 = (bf16[128,1280]{1,0:T(8,128)(2,1)}, bf16[128,1280]{1,0:T(8,128)(2,1)S(1)}, u32[]{:S(2)}, u32[]{:S(2)}) collective-permute-start(bf16[128,1280]{1,0:T(8,128)(2,1)} %get-tuple-element.90), channel_id=1, source_target_pairs={{0,8},{1,9},{2,10},{3,11},{4,12},{5,13},{6,14},{7,15},{8,16},{9,17... | collective-permute-start | bytes 983048 | tf_op jit(solution)/shard_map/ppermute | solution.py:540
  255.9 34.3 %collective-permute-start.46 = (bf16[128,1280]{1,0:T(8,128)(2,1)}, bf16[128,1280]{1,0:T(8,128)(2,1)S(1)}, u32[]{:S(2)}, u32[]{:S(2)}) collective-permute-start(bf16[128,1280]{1,0:T(8,128)(2,1)} %get-tuple-element.91), channel_id=1, source_target_pairs={{0,9},{1,8},{2,11},{3,10},{4,13},{5,12},{6,15},{7,14},{8,17},{9,16... | collective-permute-start | bytes 983048 | tf_op jit(solution)/shard_map/ppermute | solution.py:540
  259.2 38.3 %collective-permute-start.47 = (bf16[128,1280]{1,0:T(8,128)(2,1)}, bf16[128,1280]{1,0:T(8,128)(2,1)S(1)}, u32[]{:S(2)}, u32[]{:S(2)}) collective-permute-start(bf16[128,1280]{1,0:T(8,128)(2,1)} %get-tuple-element.92), channel_id=1, source_target_pairs={{0,10},{1,11},{2,8},{3,9},{4,14},{5,15},{6,12},{7,13},{8,18},{9,19... | collective-permute-start | bytes 983048 | tf_op jit(solution)/shard_map/ppermute | solution.py:540
  269.8 18.0 %copy-start = (f32[64,5120]{1,0:T(8,128)S(1)}, f32[64,5120]{1,0:T(8,128)}, u32[]{:S(2)}) copy-start(f32[64,5120]{1,0:T(8,128)} %get-tuple-element.79.refs_0_) | copy-start | bytes 3932164
  269.8 18.0 %copy-start.1 = (s32[2]{0:T(128)S(1)}, s32[2]{0:T(128)}, u32[]{:S(2)}) copy-start(s32[2]{0:T(128)} %pad_add_fusion.where_ref) | copy-start | bytes 28
  269.8 27.8 %collective-permute-start.48 = (bf16[128,1280]{1,0:T(8,128)(2,1)}, bf16[128,1280]{1,0:T(8,128)(2,1)S(1)}, u32[]{:S(2)}, u32[]{:S(2)}) collective-permute-start(bf16[128,1280]{1,0:T(8,128)(2,1)} %get-tuple-element.93), channel_id=1, source_target_pairs={{0,11},{1,10},{2,9},{3,8},{4,15},{5,14},{6,13},{7,12},{8,19},{9,18... | collective-permute-start | bytes 983048 | tf_op jit(solution)/shard_map/ppermute | solution.py:540
  (11 other events, 9.4 us)
